TPU v7x, 128 devices: a whole 4x4x4 slice. The times are simulated.
128 devices in a mesh: span: 8 (over z, core), seq: 16 (over x, y).
Axes of the slice: x: 4, y: 4, z: 4, core: 2. Of those that a mesh axis runs over, the one named last changes fastest.
Arguments:
- queries: bfloat16 [8, 2048, 6144], P('span', 'seq'), as said below
- key_states: bfloat16 [8, 2048, 1024], P('span', 'seq'), as said below
- value_states: bfloat16 [8, 2048, 1024], P('span', 'seq'), may hold values from -6 to 6
- block_lists: int32 [8, 8, 8, 8], P('span'), may hold values from -1 to 111, as said below
Outputs:
- attended: bfloat16 [8, 2048, 6144], P('span', 'seq')
Inputs may be any that keep to these rules, and one draw needn't show every extreme that they name: `queries`: real numbers. `key_states`: real numbers. `block_lists`: entry [c, g, t, j] is -1 for an unused slot or the number of a block among the first c * 16 blocks, that is, of an earlier span. The used slots of a tile come first, and every tile of a span after the first uses at least one; the first span uses none. In every span after the first some tile uses all 8 slots. Blocks may repeat.
All inputs are finite; a program needn't handle non-finite values.
Results may differ from a plain program's by a relative error of at most 0.0049.
Values may be sent and summed in bfloat16 or wider, within the bound.
No kernel may reach another device: no remote copies, remote signals or barrier semaphores. Data moves between devices by JAX's collectives and lax.ppermute only.
A program may use at most 128 MiB of HBM per device.

v0:
```python
import jax
import jax.numpy as jnp
from jax import lax
from jax.sharding import PartitionSpec as P

DH = 128
QT = 256
BK = 128


def joint_attention(query_rows, own_keys, own_values, far_keys, far_values, usable):
    seq_len = query_rows.shape[0]
    tile_count = seq_len // QT
    scaling = DH ** (-0.5)
    own_scores = (
        jnp.einsum("qd,kd->qk", query_rows, own_keys, preferred_element_type=jnp.float32) * scaling
    )
    own_scores = own_scores.reshape(tile_count, QT, seq_len)
    query_tiles = query_rows.reshape(tile_count, QT, DH)
    far_scores = (
        jnp.einsum("tqd,tkd->tqk", query_tiles, far_keys, preferred_element_type=jnp.float32)
        * scaling
    )
    far_scores = jnp.where(usable[:, None, :], far_scores, -jnp.inf)
    row_max = jnp.maximum(jnp.max(own_scores, axis=-1), jnp.max(far_scores, axis=-1))
    own_exp = jnp.exp(own_scores - row_max[..., None])
    far_exp = jnp.exp(far_scores - row_max[..., None])
    denominator = jnp.sum(own_exp, axis=-1) + jnp.sum(far_exp, axis=-1)
    own_prob = (own_exp / denominator[..., None]).astype(jnp.bfloat16)
    far_prob = (far_exp / denominator[..., None]).astype(jnp.bfloat16)
    result = jnp.einsum("tqk,kd->tqd", own_prob, own_values, preferred_element_type=jnp.float32)
    result = result + jnp.einsum(
        "tqk,tkd->tqd", far_prob, far_values, preferred_element_type=jnp.float32
    )
    return result.reshape(seq_len, DH).astype(jnp.bfloat16)


def on_device(queries, key_states, value_states, block_lists):
    tok_rows = queries.shape[1]
    model_width = queries.shape[2]
    head_count = model_width // DH
    kv_heads = key_states.shape[2] // DH
    copies = lax.axis_size("seq") // kv_heads
    query_split = queries[0].reshape(tok_rows, head_count, DH)
    key_spread = jnp.repeat(key_states[0].reshape(tok_rows, kv_heads, DH), copies, axis=1)
    value_spread = jnp.repeat(value_states[0].reshape(tok_rows, kv_heads, DH), copies, axis=1)
    local_q, local_k, local_v = (
        lax.all_to_all(query_split, "seq", split_axis=1, concat_axis=0, tiled=True),
        lax.all_to_all(key_spread, "seq", split_axis=1, concat_axis=0, tiled=True),
        lax.all_to_all(value_spread, "seq", split_axis=1, concat_axis=0, tiled=True),
    )
    local_heads = local_q.shape[1]
    own_k = local_k[:, 0, :]
    own_v = local_v[:, 0, :]
    group = lax.axis_index("seq") // copies
    block_ids = lax.dynamic_index_in_dim(block_lists[0], group, 0, keepdims=False)
    tile_count = block_ids.shape[0]
    slot_count = block_ids.shape[1]
    every_key, every_value = (
        lax.all_gather(own_k, "span", axis=0, tiled=True),
        lax.all_gather(own_v, "span", axis=0, tiled=True),
    )
    block_total = every_key.shape[0] // BK
    clipped = jnp.maximum(block_ids, 0)
    picked_k = every_key.reshape(block_total, BK, DH)[clipped]
    picked_v = every_value.reshape(block_total, BK, DH)[clipped]
    far_keys = picked_k.reshape(tile_count, slot_count * BK, DH)
    far_values = picked_v.reshape(tile_count, slot_count * BK, DH)
    usable = jnp.repeat(block_ids >= 0, BK, axis=1)

    def one_head(head):
        query_rows = lax.dynamic_index_in_dim(local_q, head, 1, keepdims=False)
        return joint_attention(query_rows, own_k, own_v, far_keys, far_values, usable)

    per_head = lax.map(one_head, jnp.arange(local_heads, dtype=jnp.int32))
    token_major = jnp.transpose(per_head, (1, 0, 2))
    returned = lax.all_to_all(token_major, "seq", split_axis=0, concat_axis=1, tiled=True)
    return returned.reshape(1, tok_rows, model_width)


def solution(mesh):
    in_specs = (
        P("span", "seq", None),
        P("span", "seq", None),
        P("span", "seq", None),
        P("span", None, None, None),
    )
    out_specs = P("span", "seq", None)
    return jax.shard_map(
        on_device, mesh=mesh, in_specs=in_specs, out_specs=out_specs, check_vma=False
    )
```

profile of v0, /device:TPU:0, one launch (start us, length us, event | category | flops | bytes accessed | tf_op | source)
XLA Modules:
  0.0 271.9 jit_solution(4756764774829381718)
XLA Ops:
  6.5 0.0 all-gather.3.cloned.1.call-start
  6.5 1.0 copy.33
  7.6 0.1 broadcast_in_dim.35
  7.7 18.5 %all_to_all.63 = bf16[128,16,128]{2,0,1:T(8,128)(2,1)} all-to-all(bf16[128,16,128]{2,0,1:T(8,128)(2,1)S(1)} %bitcast.101), channel_id=1, replica_groups=mesh['span'=8,'seq'=16] {'seq'}, dimensions={1} | all-to-all | bytes 1048576 | tf_op jit(solution)/shard_map/all_to_all | solution.py:49
  26.2 0.0 all-gather.3.cloned.1.call-update
  26.2 0.0 all-gather.5.cloned.1.call-start
  26.3 1.0 copy.34
  27.3 0.1 broadcast_in_dim.37
  27.4 13.7 %all_to_all.64 = bf16[128,16,128]{2,0,1:T(8,128)(2,1)} all-to-all(bf16[128,16,128]{2,0,1:T(8,128)(2,1)S(1)} %bitcast.102), channel_id=1, replica_groups=mesh['span'=8,'seq'=16] {'seq'}, dimensions={1} | all-to-all | bytes 1048576 | tf_op jit(solution)/shard_map/all_to_all | solution.py:50
  41.1 0.0 all-gather.5.cloned.1.call-update
  41.2 0.0 copy-start
  41.2 0.0 copy-start.2
  41.2 2.7 %copy.21 = bf16[1,128,6144]{1,2,0:T(8,128)(2,1)} copy(bf16[1,128,6144]{2,1,0:T(8,128)(2,1)} %param.6) | data formatting | bytes 3145728 | tf_op args[0]
  43.9 3.7 %all-to-all-start = ((bf16[128,48,128]{0,2,1:T(8,128)(2,1)}), bf16[128,48,128]{0,2,1:T(8,128)(2,1)S(1)}, u32[]{:S(2)}, u32[]{:S(2)}) async-start(bf16[128,48,128]{0,2,1:T(8,128)(2,1)} %bitcast.95), calls=%async_computation | async-start | bytes 3145728 | tf_op jit(solution)/shard_map/all_to_all | solution.py:48
  47.7 0.7 dynamic-slice_maximum_fusion
  48.4 0.1 reshape.90
  48.5 0.7 compare_bitcast_fusion
  49.2 0.1 copy.26
  49.2 19.2 %all-to-all-done = bf16[128,48,128]{0,2,1:T(8,128)(2,1)S(1)} async-done(((bf16[128,48,128]{0,2,1:T(8,128)(2,1)}), bf16[128,48,128]{0,2,1:T(8,128)(2,1)S(1)}, u32[]{:S(2)}, u32[]{:S(2)}) %all-to-all-start) | async-done | bytes 1572896 | tf_op jit(solution)/shard_map/all_to_all | solution.py:48
  68.4 1.6 copy.23
  70.0 3.1 %gather_fusion = bf16[64,128,128]{2,1,0:T(8,128)(2,1)S(1)} fusion(bf16[128,128,128]{2,1,0:T(8,128)(2,1)} %bitcast.104, s32[1024]{0:T(1024)S(1)} %pad_clamp_fusion), kind=kCustom, calls=%fused_computation | custom fusion | bytes 4194560 | tf_op jit(solution)/shard_map/gather | solution.py:65
  73.1 18.3 %all-gather.5.cloned.1.call-done = bf16[16384,128]{1,0:T(8,128)(2,1)} async-done(((bf16[2048,128]{1,0:T(8,128)(2,1)}), bf16[16384,128]{1,0:T(8,128)(2,1)}) %all-gather.5.cloned.1.call-update) | async-done | bytes 4194320 | tf_op jit(solution)/shard_map/all_gather | solution.py:61
  91.4 4.4 %gather_fusion.1 = bf16[64,128,128]{2,1,0:T(8,128)(2,1)} fusion(bf16[128,128,128]{2,1,0:T(8,128)(2,1)} %bitcast.105, s32[1024]{0:T(1024)S(1)} %pad_clamp_fusion), kind=kCustom, calls=%fused_computation.1 | custom fusion | bytes 4194560 | tf_op jit(solution)/shard_map/gather | solution.py:66
  95.8 0.0 copy-done
  95.8 0.0 copy-done.2
  95.8 126.3 %while.11 = (s32[]{:T(128)}, bf16[3,2048,128]{2,1,0:T(8,128)(2,1)}, s32[3]{0:T(128)S(1)}, bf16[2048,3,128]{2,0,1:T(8,128)(2,1)}, bf16[2048,128]{1,0:T(8,128)(2,1...) while((s32[]{:T(128)}, bf16[3,2048,128]{2,1,0:T(8,128)(2,1)}, ...), condition=%wide.region_5.6_spmd.clone, body=%wide.region_0.5_spmd.clone.sunk | while | flops 3276273664 | bytes 95134464 | solution.py:75
  95.8 0.7 dynamic_slice.21
  98.4 1.1 constant_dynamic-slice_fusion.2
  99.5 0.1 broadcast_bitcast_fusion.2
  99.5 4.5 %fusion.33 = (f32[8,256]{1,0:T(8,128)S(1)}, f32[8,256,1024]{2,1,0:T(8,128)}) fusion(pred[8,1024]{1,0:T(8,128)(4,1)S(1)} %broadcast_bitcast_fusion.2, bf16[8,256,128]{2,1,0:T(8,128)(2,1)S(1)} %bitcast.87, bf16[8,1024,128]{2,1,0:T(8,128)(2,1)S(1)} %get-tuple-element.224), kind=kOutput, calls=%fused_computation.10.clone.1 | convolution fusion | flops 543160320 | bytes 11026432 | tf_op jit(solution)/shard_map/while/body/eval_jaxpr/tqd,tkd->tqk/dot_general | solution.py:21
  104.0 8.1 %fusion.32 = (f32[2048]{0:T(1024)S(1)}, f32[2048,2048]{1,0:T(8,128)}) fusion(bf16[2048,128]{1,0:T(8,128)(2,1)S(1)} %get-tuple-element.223, bf16[2048,1,128]{2,0,1:T(8,128)(2,1)S(1)} %constant_dynamic-slice_fusion.2), kind=kOutput, calls=%fused_computation.26.clone.1 | convolution fusion | flops 1082128384 | bytes 17833984 | tf_op jit(solution)/shard_map/while/body/eval_jaxpr/qd,kd->qk/dot_general | solution.py:16
  112.1 4.5 %fusion.34 = f32[8,256]{1,0:T(8,128)S(1)} fusion(f32[8,256,1024]{2,1,0:T(8,128)} %get-tuple-element.194, f32[8,256]{1,0:T(8,128)S(1)} %max.31, pred[8,1024]{1,0:T(8,128)(4,1)S(1)} %broadcast_bitcast_fusion.2), kind=kLoop, calls=%fused_computation.11.clone.1 | loop fusion | flops 8386560 | bytes 8413184 | tf_op jit(solution)/shard_map/while/body/eval_jaxpr/reduce_sum | solution.py:28
  116.6 8.1 %exponential_reduce_fusion.2 = f32[2048]{0:T(1024)S(1)} fusion(f32[2048,2048]{1,0:T(8,128)} %get-tuple-element.191, f32[2048]{0:T(1024)S(1)} %max.30), kind=kLoop, calls=%fused_computation.4.clone.1 | loop fusion | flops 8386560 | bytes 16793600 | tf_op jit(solution)/shard_map/while/body/eval_jaxpr/reduce_sum | solution.py:28
  124.8 0.0 copy-start.1
  124.8 7.4 %fusion.35 = f32[8,256,128]{2,1,0:T(8,128)S(1)} fusion(f32[8,256,2048]{2,1,0:T(8,128)} %bitcast.86, f32[8,256]{1,0:T(8,128)S(1)} %add.39, f32[8,256]{1,0:T(8,128)S(1)} %max.31, bf16[2048,128]{1,0:T(8,128)(2,1)S(1)} %get-tuple-element.225), kind=kOutput, calls=%fused_computation.9.clone.1 | convolution fusion | flops 1086324736 | bytes 18366464 | tf_op jit(solution)/shard_map/while/body/eval_jaxpr/tqk,kd->tqd/dot_general | solution.py:31
  132.2 0.0 copy-done.1
  132.2 4.9 %fusion.36 = bf16[8,256,128]{2,1,0:T(8,128)(2,1)S(1)} fusion(f32[8,256,128]{2,1,0:T(8,128)S(1)} %fusion.35, bf16[8,1024,128]{2,1,0:T(8,128)(2,1)S(1)} %copy-done.1, f32[8,256,1024]{2,1,0:T(8,128)} %get-tuple-element.194, f32[8,256]{1,0:T(8,128)S(1)} %add.39, f32[8,256]{1,0:T(8,128)S(1)} %max.31, pred[8,1024]{1,0:T(8,128)(4,1)S(1)} %broadcast_bitcast_fusion.2), kind=kOutput, calls=%fused_computation.14.clone.1 | convolution fusion | flops 547880960 | bytes 12083200 | tf_op jit(solution)/shard_map/while/body/eval_jaxpr/tqk,tkd->tqd/dot_general | solution.py:32
  137.1 0.8 bitcast_dynamic-update-slice_fusion.2
  137.9 0.6 dynamic_slice.21
  140.5 1.1 constant_dynamic-slice_fusion.2
  141.6 0.1 broadcast_bitcast_fusion.2
  141.6 4.5 %fusion.33 = (f32[8,256]{1,0:T(8,128)S(1)}, f32[8,256,1024]{2,1,0:T(8,128)}) fusion(pred[8,1024]{1,0:T(8,128)(4,1)S(1)} %broadcast_bitcast_fusion.2, bf16[8,256,128]{2,1,0:T(8,128)(2,1)S(1)} %bitcast.87, bf16[8,1024,128]{2,1,0:T(8,128)(2,1)S(1)} %get-tuple-element.224), kind=kOutput, calls=%fused_computation.10.clone.1 | convolution fusion | flops 543160320 | bytes 11026432 | tf_op jit(solution)/shard_map/while/body/eval_jaxpr/tqd,tkd->tqk/dot_general | solution.py:21
  146.1 8.1 %fusion.32 = (f32[2048]{0:T(1024)S(1)}, f32[2048,2048]{1,0:T(8,128)}) fusion(bf16[2048,128]{1,0:T(8,128)(2,1)S(1)} %get-tuple-element.223, bf16[2048,1,128]{2,0,1:T(8,128)(2,1)S(1)} %constant_dynamic-slice_fusion.2), kind=kOutput, calls=%fused_computation.26.clone.1 | convolution fusion | flops 1082128384 | bytes 17833984 | tf_op jit(solution)/shard_map/while/body/eval_jaxpr/qd,kd->qk/dot_general | solution.py:16
  154.2 4.5 %fusion.34 = f32[8,256]{1,0:T(8,128)S(1)} fusion(f32[8,256,1024]{2,1,0:T(8,128)} %get-tuple-element.194, f32[8,256]{1,0:T(8,128)S(1)} %max.31, pred[8,1024]{1,0:T(8,128)(4,1)S(1)} %broadcast_bitcast_fusion.2), kind=kLoop, calls=%fused_computation.11.clone.1 | loop fusion | flops 8386560 | bytes 8413184 | tf_op jit(solution)/shard_map/while/body/eval_jaxpr/reduce_sum | solution.py:28
  158.7 8.1 %exponential_reduce_fusion.2 = f32[2048]{0:T(1024)S(1)} fusion(f32[2048,2048]{1,0:T(8,128)} %get-tuple-element.191, f32[2048]{0:T(1024)S(1)} %max.30), kind=kLoop, calls=%fused_computation.4.clone.1 | loop fusion | flops 8386560 | bytes 16793600 | tf_op jit(solution)/shard_map/while/body/eval_jaxpr/reduce_sum | solution.py:28
  166.9 7.4 %fusion.35 = f32[8,256,128]{2,1,0:T(8,128)S(1)} fusion(f32[8,256,2048]{2,1,0:T(8,128)} %bitcast.86, f32[8,256]{1,0:T(8,128)S(1)} %add.39, f32[8,256]{1,0:T(8,128)S(1)} %max.31, bf16[2048,128]{1,0:T(8,128)(2,1)S(1)} %get-tuple-element.225), kind=kOutput, calls=%fused_computation.9.clone.1 | convolution fusion | flops 1086324736 | bytes 18366464 | tf_op jit(solution)/shard_map/while/body/eval_jaxpr/tqk,kd->tqd/dot_general | solution.py:31
  174.3 4.9 %fusion.36 = bf16[8,256,128]{2,1,0:T(8,128)(2,1)S(1)} fusion(f32[8,256,128]{2,1,0:T(8,128)S(1)} %fusion.35, bf16[8,1024,128]{2,1,0:T(8,128)(2,1)S(1)} %copy-done.1, f32[8,256,1024]{2,1,0:T(8,128)} %get-tuple-element.194, f32[8,256]{1,0:T(8,128)S(1)} %add.39, f32[8,256]{1,0:T(8,128)S(1)} %max.31, pred[8,1024]{1,0:T(8,128)(4,1)S(1)} %broadcast_bitcast_fusion.2), kind=kOutput, calls=%fused_computation.14.clone.1 | convolution fusion | flops 547880960 | bytes 12083200 | tf_op jit(solution)/shard_map/while/body/eval_jaxpr/tqk,tkd->tqd/dot_general | solution.py:32
  179.2 0.8 bitcast_dynamic-update-slice_fusion.2
  180.0 0.6 dynamic_slice.21
  182.6 1.1 constant_dynamic-slice_fusion.2
  183.7 0.1 broadcast_bitcast_fusion.2
  183.7 4.5 %fusion.33 = (f32[8,256]{1,0:T(8,128)S(1)}, f32[8,256,1024]{2,1,0:T(8,128)}) fusion(pred[8,1024]{1,0:T(8,128)(4,1)S(1)} %broadcast_bitcast_fusion.2, bf16[8,256,128]{2,1,0:T(8,128)(2,1)S(1)} %bitcast.87, bf16[8,1024,128]{2,1,0:T(8,128)(2,1)S(1)} %get-tuple-element.224), kind=kOutput, calls=%fused_computation.10.clone.1 | convolution fusion | flops 543160320 | bytes 11026432 | tf_op jit(solution)/shard_map/while/body/eval_jaxpr/tqd,tkd->tqk/dot_general | solution.py:21
  188.2 8.1 %fusion.32 = (f32[2048]{0:T(1024)S(1)}, f32[2048,2048]{1,0:T(8,128)}) fusion(bf16[2048,128]{1,0:T(8,128)(2,1)S(1)} %get-tuple-element.223, bf16[2048,1,128]{2,0,1:T(8,128)(2,1)S(1)} %constant_dynamic-slice_fusion.2), kind=kOutput, calls=%fused_computation.26.clone.1 | convolution fusion | flops 1082128384 | bytes 17833984 | tf_op jit(solution)/shard_map/while/body/eval_jaxpr/qd,kd->qk/dot_general | solution.py:16
  196.3 4.5 %fusion.34 = f32[8,256]{1,0:T(8,128)S(1)} fusion(f32[8,256,1024]{2,1,0:T(8,128)} %get-tuple-element.194, f32[8,256]{1,0:T(8,128)S(1)} %max.31, pred[8,1024]{1,0:T(8,128)(4,1)S(1)} %broadcast_bitcast_fusion.2), kind=kLoop, calls=%fused_computation.11.clone.1 | loop fusion | flops 8386560 | bytes 8413184 | tf_op jit(solution)/shard_map/while/body/eval_jaxpr/reduce_sum | solution.py:28
  200.8 8.1 %exponential_reduce_fusion.2 = f32[2048]{0:T(1024)S(1)} fusion(f32[2048,2048]{1,0:T(8,128)} %get-tuple-element.191, f32[2048]{0:T(1024)S(1)} %max.30), kind=kLoop, calls=%fused_computation.4.clone.1 | loop fusion | flops 8386560 | bytes 16793600 | tf_op jit(solution)/shard_map/while/body/eval_jaxpr/reduce_sum | solution.py:28
  209.0 0.0 copy-start.1
  209.0 7.4 %fusion.35 = f32[8,256,128]{2,1,0:T(8,128)S(1)} fusion(f32[8,256,2048]{2,1,0:T(8,128)} %bitcast.86, f32[8,256]{1,0:T(8,128)S(1)} %add.39, f32[8,256]{1,0:T(8,128)S(1)} %max.31, bf16[2048,128]{1,0:T(8,128)(2,1)S(1)} %get-tuple-element.225), kind=kOutput, calls=%fused_computation.9.clone.1 | convolution fusion | flops 1086324736 | bytes 18366464 | tf_op jit(solution)/shard_map/while/body/eval_jaxpr/tqk,kd->tqd/dot_general | solution.py:31
  216.4 4.9 %fusion.36 = bf16[8,256,128]{2,1,0:T(8,128)(2,1)S(1)} fusion(f32[8,256,128]{2,1,0:T(8,128)S(1)} %fusion.35, bf16[8,1024,128]{2,1,0:T(8,128)(2,1)S(1)} %copy-done.1, f32[8,256,1024]{2,1,0:T(8,128)} %get-tuple-element.194, f32[8,256]{1,0:T(8,128)S(1)} %add.39, f32[8,256]{1,0:T(8,128)S(1)} %max.31, pred[8,1024]{1,0:T(8,128)(4,1)S(1)} %broadcast_bitcast_fusion.2), kind=kOutput, calls=%fused_computation.14.clone.1 | convolution fusion | flops 547880960 | bytes 12083200 | tf_op jit(solution)/shard_map/while/body/eval_jaxpr/tqk,tkd->tqd/dot_general | solution.py:32
  221.3 0.8 bitcast_dynamic-update-slice_fusion.2
  222.1 3.2 %copy.36 = bf16[3,2048,128]{2,0,1:T(4,128)(2,1)S(1)} copy(bf16[3,2048,128]{2,1,0:T(8,128)(2,1)} %get-tuple-element.52) | data formatting | bytes 3145728 | tf_op jit(solution)/shard_map/while | solution.py:75
  225.3 35.4 %all_to_all.65 = bf16[2048,3,128]{2,1,0:T(4,128)(2,1)S(1)} all-to-all(bf16[2048,3,128]{2,1,0:T(4,128)(2,1)S(1)} %bitcast.93), channel_id=1, replica_groups=mesh['span'=8,'seq'=16] {'seq'}, dimensions={0} | all-to-all | bytes 3145728 | tf_op jit(solution)/shard_map/all_to_all | solution.py:77
  260.7 0.2 copy.28
  260.9 1.6 copy.29
  262.5 2.6 copy.30
  (27 shorter events, 0.2 us)
Async XLA Ops:
  6.5 63.5 %all-gather.3.cloned.1.call-start = ((), (), s32[]{:S(2)}) async-start(), calls=%async_computation.4 | async-start | bytes 4718592 | tf_op jit(solution)/shard_map/all_gather | solution.py:60
  26.2 65.2 %all-gather.5.cloned.1.call-start = ((), (), s32[]{:S(2)}) async-start(), calls=%async_computation.5 | async-start | bytes 4718592 | tf_op jit(solution)/shard_map/all_gather | solution.py:61
  41.2 54.7 %copy-start = (bf16[128,16,128]{2,0,1:T(8,128)(2,1)S(1)}, bf16[128,16,128]{2,0,1:T(8,128)(2,1)}, u32[]{:S(2)}) copy-start(bf16[128,16,128]{2,0,1:T(8,128)(2,1)} %all_to_all.63) | copy-start | bytes 1572868
  41.2 54.6 %copy-start.2 = (bf16[128,16,128]{2,0,1:T(8,128)(2,1)S(1)}, bf16[128,16,128]{2,0,1:T(8,128)(2,1)}, u32[]{:S(2)}) copy-start(bf16[128,16,128]{2,0,1:T(8,128)(2,1)} %all_to_all.64) | copy-start | bytes 1572868
  43.9 24.5 %all-to-all-start = ((bf16[128,48,128]{0,2,1:T(8,128)(2,1)}), bf16[128,48,128]{0,2,1:T(8,128)(2,1)S(1)}, u32[]{:S(2)}, u32[]{:S(2)}) async-start(bf16[128,48,128]{0,2,1:T(8,128)(2,1)} %bitcast.95), calls=%async_computation | async-start | bytes 3145728 | tf_op jit(solution)/shard_map/all_to_all | solution.py:48
  124.8 7.4 %copy-start.1 = (bf16[8,1024,128]{2,1,0:T(8,128)(2,1)S(1)}, bf16[8,1024,128]{2,1,0:T(8,128)(2,1)}, u32[]{:S(2)}) copy-start(bf16[8,1024,128]{2,1,0:T(8,128)(2,1)} %get-tuple-element.226) | copy-start | bytes 6291460 | tf_op jit(solution)/shard_map/while
  166.9 7.4 %copy-start.1 = (bf16[8,1024,128]{2,1,0:T(8,128)(2,1)S(1)}, bf16[8,1024,128]{2,1,0:T(8,128)(2,1)}, u32[]{:S(2)}) copy-start(bf16[8,1024,128]{2,1,0:T(8,128)(2,1)} %get-tuple-element.226) | copy-start | bytes 6291460 | tf_op jit(solution)/shard_map/while
  209.0 7.4 %copy-start.1 = (bf16[8,1024,128]{2,1,0:T(8,128)(2,1)S(1)}, bf16[8,1024,128]{2,1,0:T(8,128)(2,1)}, u32[]{:S(2)}) copy-start(bf16[8,1024,128]{2,1,0:T(8,128)(2,1)} %get-tuple-element.226) | copy-start | bytes 6291460 | tf_op jit(solution)/shard_map/while
Sparse Core Ops, SparseCore 0:
  26.3 31.1 all-gather.2
  59.3 32.1 all-gather.4
where the time goes:
time: 273 us; the launch traced here: 272 us
  matrix products  74.5 us (27%)
  blocking collectives  67.6 us (25%)
  other arithmetic  39.3 us (14%)
  waiting for transfers between devices  37.5 us (14%)
  local copies, waits for them, and re-layouts  29.8 us (11%)
  between operations  13.5 us (5%)
  loops' own time  5.93 us (2%)
  starting transfers between devices  3.75 us (1%)
    reduce_sum x6, other arithmetic, joint_attention(): denominator = jnp.sum(own_exp, axis=-1) + jnp.sum(far_exp, axis=-1)  37.8 us
    all_to_all x1, blocking collectives, on_device(): lax.all_to_all(token_major, 'seq', split_axis=0, concat_axis=1, tiled=True)  35.4 us
    dot_general x3, matrix products, joint_attention(): jnp.einsum('qd,kd->qk', query_rows, own_keys, preferred_element_type=jnp....  24.2 us
    dot_general x3, matrix products, joint_attention(): jnp.einsum('tqk,kd->tqd', own_prob, own_values, preferred_element_type=jn...  22.3 us
    all_to_all x1, waiting for transfers between devices, on_device(): lax.all_to_all(query_split, 'seq', split_axis=1, concat_axis=0, tiled=True)  19.2 us
    all_to_all x1, blocking collectives, on_device(): lax.all_to_all(key_spread, 'seq', split_axis=1, concat_axis=0, tiled=True)  18.5 us
    all_gather x1, waiting for transfers between devices, on_device(): lax.all_gather(own_v, 'span', axis=0, tiled=True)  18.3 us
    dot_general x3, matrix products, joint_attention(): jnp.einsum('tqk,tkd->tqd', far_prob, far_values, preferred_element_type=j...  14.6 us
  transfers between devices with their start and end apart: 3, of which 2 were waited for; matrix products, arithmetic and copies ran while one was open for 4% of the time, Pallas kernels for 0%

commit v1 on v0

v1 whole, which is shorter than its diff:
```python
import functools

import jax
import jax.numpy as jnp
from jax import lax
from jax.experimental import pallas as pl
from jax.experimental.pallas import tpu as pltpu
from jax.sharding import PartitionSpec as P

DH = 128
QT = 256
BK = 128
LOG2E = 1.4426950408889634
VMEM_BYTES = 52 * 2**20


def scaled_query(query_rows):
    scaled = query_rows.astype(jnp.float32) * (LOG2E * DH**-0.5)
    high = scaled.astype(jnp.bfloat16)
    low = (scaled - high.astype(jnp.float32)).astype(jnp.bfloat16)
    return jnp.concatenate([high, low], axis=1)


def scores_of(query_pair, keys_twice):
    return lax.dot_general(
        query_pair, keys_twice, (((1,), (1,)), ((), ())), preferred_element_type=jnp.float32
    )


def own_kernel(heads, q_ref, kv_ref, acc_ref, stat_ref, keys, values):
    rows = kv_ref.shape[0]
    block = kv_ref[:, :DH]
    keys[:, :DH] = block
    keys[:, DH:] = block
    values[:, :DH] = kv_ref[:, DH:]
    values[:, DH:] = jnp.ones((rows, DH), jnp.bfloat16)

    def tile(t, carry):
        at = pl.ds(pl.multiple_of(t * QT, QT), QT)
        for head in range(heads):
            columns = slice(head * DH, (head + 1) * DH)
            scores = scores_of(scaled_query(q_ref[at, columns]), keys[...])
            top = jnp.max(scores, axis=1, keepdims=True)
            weights = jnp.exp2(scores - top).astype(jnp.bfloat16)
            sums = jnp.dot(weights, values[...], preferred_element_type=jnp.float32)
            acc_ref[at, columns] = sums[:, :DH]
            stat_ref[at, head : head + 1] = top
            stat_ref[at, heads + head : heads + head + 1] = sums[:, DH : DH + 1]
        return carry

    lax.fori_loop(0, q_ref.shape[0] // QT, tile, 0)


def far_kernel(heads, tiles, slots, ids_ref, place_ref, q_ref, acc_ref, stat_ref, kv_ref, *rest):
    pieces, (out_ref, keys, values, key_sem, value_sem) = rest[:-5], rest[-5:]
    piece_blocks = pieces[0].shape[0] // BK
    plane, core = place_ref[0], place_ref[1]

    def fetch(source, first, t, j):
        rows = pl.ds(pl.multiple_of(first * BK, BK), BK)
        to = pl.ds(j * BK, BK)
        from_keys = source.at[rows, pl.ds(0, DH)]
        pltpu.make_async_copy(from_keys, keys.at[t, to, pl.ds(0, DH)], key_sem.at[t]).start()
        pltpu.make_async_copy(from_keys, keys.at[t, to, pl.ds(DH, DH)], key_sem.at[t]).start()
        pltpu.make_async_copy(
            source.at[rows, pl.ds(DH, DH)], values.at[t, to, pl.ds(0, DH)], value_sem.at[t]
        ).start()

    for t in range(tiles):
        for j in range(slots):
            block = ids_ref[t * slots + j]
            used = block >= 0
            number = jnp.maximum(block, 0)
            span, within = number // (2 * piece_blocks), number % (2 * piece_blocks)
            back = plane - span // 2
            direct = (span % 2 == core).astype(jnp.int32)
            at = jnp.where(back == 0, 0, 2 + (back - 1) * 4 + direct * 2) + within // piece_blocks
            at = jnp.where(used, at, -1)
            first = within % piece_blocks

            @pl.when(at < 0)
            def _():
                fetch(kv_ref, 0, t, j)

            for n, piece in enumerate(pieces):

                @pl.when(at == n)
                def _():
                    fetch(piece, first, t, j)

    for t in range(tiles):
        pltpu.make_async_copy(keys.at[t], keys.at[t], key_sem.at[t]).wait()
        pltpu.make_async_copy(
            values.at[t, :, pl.ds(0, DH)], values.at[t, :, pl.ds(0, DH)], value_sem.at[t]
        ).wait()
        values[t, :, DH:] = jnp.ones((slots * BK, DH), jnp.bfloat16)
        for j in range(slots):

            @pl.when(ids_ref[t * slots + j] < 0)
            def _():
                values[t, j * BK : (j + 1) * BK, :] = jnp.zeros((BK, 2 * DH), jnp.bfloat16)

        at = slice(t * QT, (t + 1) * QT)
        for head in range(heads):
            columns = slice(head * DH, (head + 1) * DH)
            scores = scores_of(scaled_query(q_ref[at, columns]), keys[t])
            own_top = stat_ref[at, head : head + 1]
            own_total = stat_ref[at, heads + head : heads + head + 1]
            top = jnp.maximum(jnp.max(scores, axis=1, keepdims=True), own_top)
            weights = jnp.exp2(scores - top).astype(jnp.bfloat16)
            sums = jnp.dot(weights, values[t], preferred_element_type=jnp.float32)
            shrink = jnp.exp2(own_top - top)
            total = own_total * shrink + sums[:, DH : DH + 1]
            result = (acc_ref[at, columns] * shrink + sums[:, :DH]) / total
            out_ref[at, columns] = result.astype(jnp.bfloat16)


def own_attention(q, kv):
    tokens, width = q.shape
    heads = width // DH
    whole = pl.BlockSpec(memory_space=pltpu.VMEM)
    scores = tokens * heads * kv.shape[0]
    return pl.pallas_call(
        functools.partial(own_kernel, heads),
        out_shape=(
            jax.ShapeDtypeStruct((tokens, width), jnp.float32),
            jax.ShapeDtypeStruct((tokens, 2 * heads), jnp.float32),
        ),
        in_specs=[whole] * 2,
        out_specs=(whole, whole),
        scratch_shapes=[
            pltpu.VMEM((kv.shape[0], 2 * DH), jnp.bfloat16),
            pltpu.VMEM((kv.shape[0], 2 * DH), jnp.bfloat16),
        ],
        cost_estimate=pl.CostEstimate(
            flops=8 * scores * DH, bytes_accessed=8 * tokens * width, transcendentals=scores
        ),
        compiler_params=pltpu.CompilerParams(vmem_limit_bytes=VMEM_BYTES),
        name="own_attention",
    )(q, kv)


def far_attention(ids, place, q, acc, stats, kv, pieces, tiles, slots):
    tokens, width = q.shape
    heads = width // DH
    whole = pl.BlockSpec(memory_space=pltpu.VMEM)
    scalars = pl.BlockSpec(memory_space=pltpu.SMEM)
    anywhere = pl.BlockSpec(memory_space=pl.ANY)
    scores = tokens * heads * slots * BK
    return pl.pallas_call(
        functools.partial(far_kernel, heads, tiles, slots),
        out_shape=jax.ShapeDtypeStruct((tokens, width), jnp.bfloat16),
        in_specs=[scalars] * 2 + [whole] * 3 + [anywhere] * (1 + len(pieces)),
        out_specs=whole,
        scratch_shapes=[
            pltpu.VMEM((tiles, slots * BK, 2 * DH), jnp.bfloat16),
            pltpu.VMEM((tiles, slots * BK, 2 * DH), jnp.bfloat16),
            pltpu.SemaphoreType.DMA((tiles,)),
            pltpu.SemaphoreType.DMA((tiles,)),
        ],
        cost_estimate=pl.CostEstimate(
            flops=8 * scores * DH, bytes_accessed=8 * tokens * width, transcendentals=scores
        ),
        compiler_params=pltpu.CompilerParams(vmem_limit_bytes=VMEM_BYTES),
        name="far_attention",
    )(ids, place, q, acc, stats, kv, *pieces)


def on_device(queries, key_states, value_states, block_lists):
    tok_rows = queries.shape[1]
    model_width = queries.shape[2]
    kv_heads = key_states.shape[2] // DH
    seq_size, spans = lax.axis_size("seq"), lax.axis_size("span")
    copies = seq_size // kv_heads
    width = model_width // kv_heads
    place = lax.axis_index("seq")
    group, part = place % kv_heads, place // kv_heads
    span = lax.axis_index("span")
    tile_count, slots = block_lists.shape[2], block_lists.shape[3]
    tiles = tile_count // copies
    rings = [list(range(c * kv_heads, (c + 1) * kv_heads)) for c in range(copies)]

    keys = key_states[0].reshape(tok_rows, kv_heads, DH)
    values = value_states[0].reshape(tok_rows, kv_heads, DH)
    kv_send = jnp.transpose(jnp.concatenate([keys, values], axis=2), (1, 0, 2))
    kv_send = jnp.concatenate([kv_send] * copies, axis=0)
    kv = lax.all_to_all(kv_send, "seq", 0, 0, tiled=True).reshape(seq_size * tok_rows, 2 * DH)

    q_send = jnp.transpose(queries[0].reshape(tok_rows, kv_heads, width), (1, 0, 2))
    q = lax.all_to_all(q_send, "seq", 0, 0, tiled=True, axis_index_groups=rings)
    q = q.reshape(kv_heads * tok_rows, width)

    def shift(x, by):
        return lax.ppermute(x, "span", [(i, (i + by) % spans) for i in range(spans)])

    def swap(x):
        return lax.ppermute(x, "span", [(i, i ^ 1) for i in range(spans)])

    half = kv.shape[0] // 2
    first, second = kv[:half], kv[half:]
    up_first = shift(first, 2)
    down_second = shift(second, -2)
    up_second = shift(second, 2)
    down_first = shift(first, -2)
    two_first = shift(up_first, 2)
    two_second = shift(down_second, -2)
    received = [up_first, up_second, two_first, two_second, down_first, down_second]
    pieces = [swap(first), swap(second)]
    for n in range(0, 6, 2):
        pieces += [swap(received[n]), swap(received[n + 1]), received[n], received[n + 1]]

    acc, stats = own_attention(q, kv)
    ids = lax.dynamic_slice(block_lists, (0, group, part * tiles, 0), (1, 1, tiles, slots))
    where = jnp.stack([span // 2, span % 2]).astype(jnp.int32)
    out = far_attention(ids.reshape(tiles * slots), where, q, acc, stats, kv, pieces, tiles, slots)

    out = out.reshape(kv_heads, tok_rows, width)
    back = lax.all_to_all(out, "seq", 0, 0, tiled=True, axis_index_groups=rings)
    return jnp.transpose(back, (1, 0, 2)).reshape(1, tok_rows, model_width)


def solution(mesh):
    in_specs = (
        P("span", "seq", None),
        P("span", "seq", None),
        P("span", "seq", None),
        P("span", None, None, None),
    )
    out_specs = P("span", "seq", None)
    return jax.shard_map(
        on_device, mesh=mesh, in_specs=in_specs, out_specs=out_specs, check_vma=False
    )
```

time: 273 us -> 142 us (0.52)
  matrix products: 74.5 us -> 0 us
  blocking collectives: 67.6 us -> 27.1 us
  Pallas kernels: 0 us -> 39.4 us
  other arithmetic: 39.3 us -> 1.22 us
  local copies, waits for them, and re-layouts: 29.8 us -> 7.26 us
  starting transfers between devices: 3.75 us -> 23.7 us
  between operations: 13.5 us -> 0.16 us
  loops' own time: 5.93 us -> 0 us
  waiting for transfers between devices: 37.5 us -> 42.8 us
    dot_general x12 -> x0, matrix products: 74.5 us -> none  [the longest x3 24.2 us: joint_attention(): jnp.einsum('qd,kd->qk', query_rows, own_keys, preferred_element_type=jnp....]
    all_to_all x3 -> x1, blocking collectives: 67.6 us -> 27.1 us  [on_device(): back = lax.all_to_all(out, 'seq', 0, 0, tiled=True, axis_index_groups=rings)]
    pallas_call x0 -> x2, Pallas kernels: none -> 39.4 us  [the longest x1 20.6 us: own_attention(): pl.pallas_call(functools.partial(own_kernel, heads), out_shape=(jax.Shape...]
    reduce_sum x6 -> x0, other arithmetic: 37.8 us -> none  [joint_attention(): denominator = jnp.sum(own_exp, axis=-1) + jnp.sum(far_exp, axis=-1)]
    ppermute x0 -> x14, waiting for transfers between devices: none -> 26.9 us  [the longest x6 26.9 us: shift(): lax.ppermute(x, 'span', [(i, (i + by) % spans) for i in range(spans)])]
    all_gather x2 -> x0, waiting for transfers between devices: 18.3 us -> none  [the longest x1 18.3 us: on_device(): lax.all_gather(own_v, 'span', axis=0, tiled=True)]
    ppermute x0 -> x14, starting transfers between devices: none -> 12.3 us  [the longest x6 11.1 us: shift(): lax.ppermute(x, 'span', [(i, (i + by) % spans) for i in range(spans)])]
    all_to_all x1 -> x2, starting transfers between devices: 3.71 us -> 11.4 us  [the longest x1 7.12 us: on_device(): lax.all_to_all(kv_send, 'seq', 0, 0, tiled=True)]
  transfers between devices with their start and end apart: 3 -> 16, of which waited for: 2 -> 6; matrix products, arithmetic and copies ran while one was open for 4% -> 1% of each run, Pallas kernels for 0% -> 15%
where the time goes in v1:
time: 142 us
  waiting for transfers between devices  42.8 us (30%)
  Pallas kernels  39.4 us (28%)
  blocking collectives  27.1 us (19%)
  starting transfers between devices  23.7 us (17%)
  local copies, waits for them, and re-layouts  7.26 us (5%)
    all_to_all x1, blocking collectives, on_device(): back = lax.all_to_all(out, 'seq', 0, 0, tiled=True, axis_index_groups=rings)  27.1 us
    ppermute x6, waiting for transfers between devices, shift(): lax.ppermute(x, 'span', [(i, (i + by) % spans) for i in range(spans)])  26.9 us
    pallas_call x1, Pallas kernels, own_attention(): pl.pallas_call(functools.partial(own_kernel, heads), out_shape=(jax.Shape...  20.6 us
    pallas_call x1, Pallas kernels, far_attention(): pl.pallas_call(functools.partial(far_kernel, heads, tiles, slots), out_sh...  18.8 us
    all_to_all x1, waiting for transfers between devices, on_device(): lax.all_to_all(kv_send, 'seq', 0, 0, tiled=True)  15.9 us
    ppermute x6, starting transfers between devices, shift(): lax.ppermute(x, 'span', [(i, (i + by) % spans) for i in range(spans)])  11.1 us
    all_to_all x1, starting transfers between devices, on_device(): lax.all_to_all(kv_send, 'seq', 0, 0, tiled=True)  7.12 us
    all_to_all x1, starting transfers between devices, on_device(): q = lax.all_to_all(q_send, 'seq', 0, 0, tiled=True, axis_index_groups=rings)  4.3 us
  transfers between devices with their start and end apart: 16, of which 6 were waited for; matrix products, arithmetic and copies ran while one was open for 1% of the time, Pallas kernels for 15%

profile of v1, /device:TPU:0, one launch (start us, length us, event | category | flops | bytes accessed | tf_op | source)
XLA Modules:
  0.0 141.6 jit_solution(4382432157677824014)
XLA Ops:
  0.0 0.0 copy-start
  0.0 1.0 copy.10
  1.0 1.0 copy.11
  2.1 0.1 maximum_bitcast_fusion
  2.2 0.0 copy-start.2
  2.2 1.1 pad_maximum_fusion
  3.3 7.1 %all-to-all-start.1 = ((bf16[16,128,256]{2,1,0:T(8,128)(2,1)}), bf16[16,128,256]{2,1,0:T(8,128)(2,1)S(1)}, u32[]{:S(2)}, u32[]{:S(2)}) async-start(bf16[16,128,256]{2,1,0:T(8,128)(2,1)} %pad_maximum_fusion), calls=%async_computation.1 | async-start | bytes 2097152 | tf_op jit(solution)/shard_map/all_to_all | solution.py:187
  10.4 0.0 copy-done.2
  10.4 0.3 copy.9
  10.7 1.4 %copy.13 = bf16[128,8,768]{2,0,1:T(8,128)(2,1)} copy(bf16[128,8,768]{2,1,0:T(8,128)(2,1)S(1)} %bitcast.25) | data formatting | bytes 3145728 | tf_op jit(solution)/shard_map/reshape;squeeze | solution.py:189
  12.2 15.9 %all-to-all-done.1 = bf16[16,128,256]{2,1,0:T(8,128)(2,1)S(1)} async-done(((bf16[16,128,256]{2,1,0:T(8,128)(2,1)}), bf16[16,128,256]{2,1,0:T(8,128)(2,1)S(1)}, u32[]{:S(2)}, u32[]{:S(2)}) %all-to-all-start.1) | async-done | bytes 1048608 | tf_op jit(solution)/shard_map/all_to_all | solution.py:187
  28.1 0.0 copy-start.1
  28.1 4.3 %all-to-all-start = ((bf16[8,128,768]{2,1,0:T(8,128)(2,1)}), bf16[8,128,768]{2,1,0:T(8,128)(2,1)}, u32[]{:S(2)}, u32[]{:S(2)}) async-start(bf16[8,128,768]{2,1,0:T(8,128)(2,1)} %bitcast.21), calls=%async_computation | async-start | bytes 3145728 | tf_op jit(solution)/shard_map/all_to_all | solution.py:190
  32.4 0.1 fusion
  32.5 4.1 %collective-permute-start.11 = (bf16[1024,256]{1,0:T(8,128)(2,1)S(1)}, bf16[1024,256]{1,0:T(8,128)(2,1)S(1)}, u32[]{:S(2)}, u32[]{:S(2)}) collective-permute-start(bf16[1024,256]{1,0:T(8,128)(2,1)S(1)} %bitcast.33), channel_id=1, source_target_pairs={{0,96},{16,112},{32,0},{48,16},{64,32},{80,48},{96,64},{112,80},{1... | collective-permute-start | bytes 1572872 | tf_op jit(solution)/shard_map/ppermute | solution.py:194
  36.6 0.0 collective-permute-start.2
  36.6 0.0 collective-permute-start
  36.6 3.2 %collective-permute-start.8 = (bf16[1024,256]{1,0:T(8,128)(2,1)S(1)}, bf16[1024,256]{1,0:T(8,128)(2,1)}, u32[]{:S(2)}, u32[]{:S(2)}) collective-permute-start(bf16[1024,256]{1,0:T(8,128)(2,1)S(1)} %bitcast.30), channel_id=1, source_target_pairs={{0,96},{16,112},{32,0},{48,16},{64,32},{80,48},{96,64},{112,80},{1... | collective-permute-start | bytes 1572872 | tf_op jit(solution)/shard_map/ppermute | solution.py:194
  39.8 0.0 collective-permute-start.4
  39.8 9.1 %collective-permute-done.11.rest_12_ = bf16[1024,256]{1,0:T(8,128)(2,1)S(1)} collective-permute-done((bf16[1024,256]{1,0:T(8,128)(2,1)S(1)}, bf16[1024,256]{1,0:T(8,128)(2,1)S(1)}, u32[]{:S(2)}, u32[]{:S(2)}) %collective-permute-start.11) | collective-permute-done | bytes 524320 | tf_op jit(solution)/shard_map/ppermute | solution.py:194
  49.0 0.0 copy-start.3
  49.0 0.0 collective-permute-start.1
  49.0 3.8 %collective-permute-done.2.rest_4_ = bf16[1024,256]{1,0:T(8,128)(2,1)} collective-permute-done((bf16[1024,256]{1,0:T(8,128)(2,1)S(1)}, bf16[1024,256]{1,0:T(8,128)(2,1)}, u32[]{:S(2)}, u32[]{:S(2)}) %collective-permute-start.2) | collective-permute-done | bytes 524320 | tf_op jit(solution)/shard_map/ppermute | solution.py:194
  52.8 0.0 collective-permute-start.12
  52.8 0.0 collective-permute-done.rest_0_
  52.8 0.0 collective-permute-start.6
  52.8 3.8 %collective-permute-done.8.rest_13_ = bf16[1024,256]{1,0:T(8,128)(2,1)} collective-permute-done((bf16[1024,256]{1,0:T(8,128)(2,1)S(1)}, bf16[1024,256]{1,0:T(8,128)(2,1)}, u32[]{:S(2)}, u32[]{:S(2)}) %collective-permute-start.8) | collective-permute-done | bytes 524320 | tf_op jit(solution)/shard_map/ppermute | solution.py:194
  56.5 3.8 %collective-permute-start.9 = (bf16[1024,256]{1,0:T(8,128)(2,1)}, bf16[1024,256]{1,0:T(8,128)(2,1)}, u32[]{:S(2)}, u32[]{:S(2)}) collective-permute-start(bf16[1024,256]{1,0:T(8,128)(2,1)} %collective-permute-done.8.rest_13_), channel_id=1, source_target_pairs={{0,96},{16,112},{32,0},{48,16},{64,32},{80,48},{96,64},{112,80},{1... | collective-permute-start | bytes 1572872 | tf_op jit(solution)/shard_map/ppermute | solution.py:194
  60.3 0.0 copy-done
  60.3 0.1 reshape.17.ids_ref
  60.4 0.1 pad_add_fusion.place_ref
  60.5 2.1 %collective-permute-done.4.rest_5_ = bf16[1024,256]{1,0:T(8,128)(2,1)} collective-permute-done((bf16[1024,256]{1,0:T(8,128)(2,1)S(1)}, bf16[1024,256]{1,0:T(8,128)(2,1)}, u32[]{:S(2)}, u32[]{:S(2)}) %collective-permute-start.4) | collective-permute-done | bytes 524320 | tf_op jit(solution)/shard_map/ppermute | solution.py:194
  62.6 0.0 collective-permute-start.3
  62.6 0.0 collective-permute-done.1.rest_1_
  62.6 0.5 collective-permute-start.13
  63.1 0.0 collective-permute-done.12.rest_10_
  63.1 0.1 collective-permute-start.5
  63.2 8.0 %collective-permute-done.6.rest_8_ = bf16[1024,256]{1,0:T(8,128)(2,1)} collective-permute-done((bf16[1024,256]{1,0:T(8,128)(2,1)}, bf16[1024,256]{1,0:T(8,128)(2,1)}, u32[]{:S(2)}, u32[]{:S(2)}) %collective-permute-start.6) | collective-permute-done | bytes 524320 | tf_op jit(solution)/shard_map/ppermute | solution.py:194
  71.3 0.0 collective-permute-start.7
  71.3 0.0 collective-permute-done.9.rest_9_
  71.3 0.5 collective-permute-start.10
  71.8 0.0 all-to-all-done
  71.8 0.0 copy-done.1
  71.8 20.6 %own_attention.1 = (f32[1024,768]{1,0:T(8,128)}, f32[1024,12]{1,0:T(8,128)S(1)}) custom-call(bf16[1024,768]{1,0:T(8,128)(2,1)} %bitcast.3.q_ref, bf16[2048,256]{1,0:T(8,128)(2,1)S(1)} %bitcast.22), custom_call_target="tpu_custom_call" | custom-call | flops 12884901888 | bytes 6291456 | tf_op jit(solution)/shard_map/own_attention/pallas_call | solution.py:123
  92.4 0.0 copy-done.3
  92.4 0.0 collective-permute-done.3.rest_2_
  92.4 0.0 collective-permute-done.13.rest_11_
  92.4 0.0 copy-start.4
  92.4 0.0 collective-permute-done.5.rest_3_
  92.4 0.0 collective-permute-done.7.rest_6_
  92.4 0.0 collective-permute-done.10.rest_7_
  92.5 0.8 copy-done.4
  93.2 18.8 %far_attention.1 = bf16[1024,768]{1,0:T(8,128)(2,1)} custom-call(s32[32]{0:T(128)S(1)} %reshape.17.ids_ref, s32[2]{0:T(128)S(1)} %pad_add_fusion.place_ref, bf16[1024,768]{1,0:T(8,128)(2,1)} %bitcast.3.q_ref, f32[1024,768]{1,0:T(8,128)} %get-tuple-element.7.acc_ref, f32[1024,12]{1,0:T(8,128)S(1)} %get-tuple-element.8.stat_ref, bf16[2048,256]{1,0:T(8,128)(2,1)} %bitcast.23, ...), custom_call_target="tpu_custom_call" | custom-call | flops 6442450944 | bytes 6291456 | tf_op jit(solution)/shard_map/far_attention/pallas_call | solution.py:150
  112.1 27.1 %all_to_all.15 = bf16[8,128,768]{2,1,0:T(8,128)(2,1)S(1)} all-to-all(bf16[8,128,768]{2,1,0:T(8,128)(2,1)} %bitcast.27), channel_id=1, replica_groups={{0,1,2,3,4,5,6,7},{8,9,10,11,12,13,14,15},{16,17,18,19,20,21,22,23},{24..., dimensions={0} | all-to-all | bytes 3145728 | tf_op jit(solution)/shard_map/all_to_all | solution.py:218
  139.1 0.9 copy.8
  140.0 1.6 %reshape.21 = bf16[1,128,6144]{2,1,0:T(8,128)(2,1)} reshape(bf16[128,8,768]{2,1,0:T(8,128)(2,1)S(1)} %copy.8) | data formatting | bytes 3145728 | tf_op jit(solution)/shard_map/reshape | solution.py:219
  (3 shorter events, 0.1 us)
Async XLA Ops:
  0.0 60.3 %copy-start = (s32[1,8,8,8]{3,2,1,0:T(8,128)S(1)}, s32[1,8,8,8]{3,2,1,0:T(8,128)}, u32[]{:S(2)}) copy-start(s32[1,8,8,8]{3,2,1,0:T(8,128)} %param.7) | copy-start | bytes 6148
  2.2 8.2 %copy-start.2 = (bf16[1,128,6144]{2,1,0:T(8,128)(2,1)S(1)}, bf16[1,128,6144]{2,1,0:T(8,128)(2,1)}, u32[]{:S(2)}) copy-start(bf16[1,128,6144]{2,1,0:T(8,128)(2,1)} %param.4) | copy-start | bytes 4718596
  3.3 24.8 %all-to-all-start.1 = ((bf16[16,128,256]{2,1,0:T(8,128)(2,1)}), bf16[16,128,256]{2,1,0:T(8,128)(2,1)S(1)}, u32[]{:S(2)}, u32[]{:S(2)}) async-start(bf16[16,128,256]{2,1,0:T(8,128)(2,1)} %pad_maximum_fusion), calls=%async_computation.1 | async-start | bytes 2097152 | tf_op jit(solution)/shard_map/all_to_all | solution.py:187
  28.1 43.7 %copy-start.1 = (bf16[16,128,256]{2,1,0:T(8,128)(2,1)}, bf16[16,128,256]{2,1,0:T(8,128)(2,1)S(1)}, u32[]{:S(2)}) copy-start(bf16[16,128,256]{2,1,0:T(8,128)(2,1)S(1)} %all-to-all-done.1) | copy-start | bytes 3145732
  28.1 43.7 %all-to-all-start = ((bf16[8,128,768]{2,1,0:T(8,128)(2,1)}), bf16[8,128,768]{2,1,0:T(8,128)(2,1)}, u32[]{:S(2)}, u32[]{:S(2)}) async-start(bf16[8,128,768]{2,1,0:T(8,128)(2,1)} %bitcast.21), calls=%async_computation | async-start | bytes 3145728 | tf_op jit(solution)/shard_map/all_to_all | solution.py:190
  32.5 16.5 %collective-permute-start.11 = (bf16[1024,256]{1,0:T(8,128)(2,1)S(1)}, bf16[1024,256]{1,0:T(8,128)(2,1)S(1)}, u32[]{:S(2)}, u32[]{:S(2)}) collective-permute-start(bf16[1024,256]{1,0:T(8,128)(2,1)S(1)} %bitcast.33), channel_id=1, source_target_pairs={{0,96},{16,112},{32,0},{48,16},{64,32},{80,48},{96,64},{112,80},{1... | collective-permute-start | bytes 1572872 | tf_op jit(solution)/shard_map/ppermute | solution.py:194
  36.6 16.2 %collective-permute-start.2 = (bf16[1024,256]{1,0:T(8,128)(2,1)S(1)}, bf16[1024,256]{1,0:T(8,128)(2,1)}, u32[]{:S(2)}, u32[]{:S(2)}) collective-permute-start(bf16[1024,256]{1,0:T(8,128)(2,1)S(1)} %bitcast.34), channel_id=1, source_target_pairs={{0,32},{16,48},{32,64},{48,80},{64,96},{80,112},{96,0},{112,16},{1... | collective-permute-start | bytes 1572872 | tf_op jit(solution)/shard_map/ppermute | solution.py:194
  36.6 16.2 %collective-permute-start = (bf16[1024,256]{1,0:T(8,128)(2,1)S(1)}, bf16[1024,256]{1,0:T(8,128)(2,1)S(1)}, u32[]{:S(2)}, u32[]{:S(2)}) collective-permute-start(bf16[1024,256]{1,0:T(8,128)(2,1)S(1)} %bitcast.35), channel_id=1, source_target_pairs={{0,16},{16,0},{32,48},{48,32},{64,80},{80,64},{96,112},{112,96},{1... | collective-permute-start | bytes 1572872 | tf_op jit(solution)/shard_map/ppermute | solution.py:197
  36.6 19.9 %collective-permute-start.8 = (bf16[1024,256]{1,0:T(8,128)(2,1)S(1)}, bf16[1024,256]{1,0:T(8,128)(2,1)}, u32[]{:S(2)}, u32[]{:S(2)}) collective-permute-start(bf16[1024,256]{1,0:T(8,128)(2,1)S(1)} %bitcast.30), channel_id=1, source_target_pairs={{0,96},{16,112},{32,0},{48,16},{64,32},{80,48},{96,64},{112,80},{1... | collective-permute-start | bytes 1572872 | tf_op jit(solution)/shard_map/ppermute | solution.py:194
  39.8 22.8 %collective-permute-start.4 = (bf16[1024,256]{1,0:T(8,128)(2,1)S(1)}, bf16[1024,256]{1,0:T(8,128)(2,1)}, u32[]{:S(2)}, u32[]{:S(2)}) collective-permute-start(bf16[1024,256]{1,0:T(8,128)(2,1)S(1)} %bitcast.31), channel_id=1, source_target_pairs={{0,32},{16,48},{32,64},{48,80},{64,96},{80,112},{96,0},{112,16},{1... | collective-permute-start | bytes 1572872 | tf_op jit(solution)/shard_map/ppermute | solution.py:194
  49.0 43.4 %copy-start.3 = (bf16[1024,256]{1,0:T(8,128)(2,1)}, bf16[1024,256]{1,0:T(8,128)(2,1)S(1)}, u32[]{:S(2)}) copy-start(bf16[1024,256]{1,0:T(8,128)(2,1)S(1)} %collective-permute-done.11.rest_12_) | copy-start | bytes 1572868
  49.0 13.7 %collective-permute-start.1 = (bf16[1024,256]{1,0:T(8,128)(2,1)S(1)}, bf16[1024,256]{1,0:T(8,128)(2,1)S(1)}, u32[]{:S(2)}, u32[]{:S(2)}) collective-permute-start(bf16[1024,256]{1,0:T(8,128)(2,1)S(1)} %bitcast.32), channel_id=1, source_target_pairs={{0,16},{16,0},{32,48},{48,32},{64,80},{80,64},{96,112},{112,96},{1... | collective-permute-start | bytes 1572872 | tf_op jit(solution)/shard_map/ppermute | solution.py:197
  52.8 10.4 %collective-permute-start.12 = (bf16[1024,256]{1,0:T(8,128)(2,1)S(1)}, bf16[1024,256]{1,0:T(8,128)(2,1)}, u32[]{:S(2)}, u32[]{:S(2)}) collective-permute-start(bf16[1024,256]{1,0:T(8,128)(2,1)S(1)} %collective-permute-done.11.rest_12_), channel_id=1, source_target_pairs={{0,16},{16,0},{32,48},{48,32},{64,80},{80,64},{96,112},{112,96},{1... | collective-permute-start | bytes 1572872 | tf_op jit(solution)/shard_map/ppermute | solution.py:197
  52.8 18.5 %collective-permute-start.6 = (bf16[1024,256]{1,0:T(8,128)(2,1)}, bf16[1024,256]{1,0:T(8,128)(2,1)}, u32[]{:S(2)}, u32[]{:S(2)}) collective-permute-start(bf16[1024,256]{1,0:T(8,128)(2,1)} %collective-permute-done.2.rest_4_), channel_id=1, source_target_pairs={{0,32},{16,48},{32,64},{48,80},{64,96},{80,112},{96,0},{112,16},{1... | collective-permute-start | bytes 1572872 | tf_op jit(solution)/shard_map/ppermute | solution.py:194
  56.5 14.8 %collective-permute-start.9 = (bf16[1024,256]{1,0:T(8,128)(2,1)}, bf16[1024,256]{1,0:T(8,128)(2,1)}, u32[]{:S(2)}, u32[]{:S(2)}) collective-permute-start(bf16[1024,256]{1,0:T(8,128)(2,1)} %collective-permute-done.8.rest_13_), channel_id=1, source_target_pairs={{0,96},{16,112},{32,0},{48,16},{64,32},{80,48},{96,64},{112,80},{1... | collective-permute-start | bytes 1572872 | tf_op jit(solution)/shard_map/ppermute | solution.py:194
  62.6 29.8 %collective-permute-start.3 = (bf16[1024,256]{1,0:T(8,128)(2,1)}, bf16[1024,256]{1,0:T(8,128)(2,1)}, u32[]{:S(2)}, u32[]{:S(2)}) collective-permute-start(bf16[1024,256]{1,0:T(8,128)(2,1)} %collective-permute-done.2.rest_4_), channel_id=1, source_target_pairs={{0,16},{16,0},{32,48},{48,32},{64,80},{80,64},{96,112},{112,96},{1... | collective-permute-start | bytes 1572872 | tf_op jit(solution)/shard_map/ppermute | solution.py:197
  62.6 29.8 %collective-permute-start.13 = (bf16[1024,256]{1,0:T(8,128)(2,1)}, bf16[1024,256]{1,0:T(8,128)(2,1)S(1)}, u32[]{:S(2)}, u32[]{:S(2)}) collective-permute-start(bf16[1024,256]{1,0:T(8,128)(2,1)} %collective-permute-done.8.rest_13_), channel_id=1, source_target_pairs={{0,16},{16,0},{32,48},{48,32},{64,80},{80,64},{96,112},{112,96},{1... | collective-permute-start | bytes 1572872 | tf_op jit(solution)/shard_map/ppermute | solution.py:197
  63.1 29.3 %collective-permute-start.5 = (bf16[1024,256]{1,0:T(8,128)(2,1)}, bf16[1024,256]{1,0:T(8,128)(2,1)}, u32[]{:S(2)}, u32[]{:S(2)}) collective-permute-start(bf16[1024,256]{1,0:T(8,128)(2,1)} %collective-permute-done.4.rest_5_), channel_id=1, source_target_pairs={{0,16},{16,0},{32,48},{48,32},{64,80},{80,64},{96,112},{112,96},{1... | collective-permute-start | bytes 1572872 | tf_op jit(solution)/shard_map/ppermute | solution.py:197
  71.3 21.2 %collective-permute-start.7 = (bf16[1024,256]{1,0:T(8,128)(2,1)}, bf16[1024,256]{1,0:T(8,128)(2,1)}, u32[]{:S(2)}, u32[]{:S(2)}) collective-permute-start(bf16[1024,256]{1,0:T(8,128)(2,1)} %collective-permute-done.6.rest_8_), channel_id=1, source_target_pairs={{0,16},{16,0},{32,48},{48,32},{64,80},{80,64},{96,112},{112,96},{1... | collective-permute-start | bytes 1572872 | tf_op jit(solution)/shard_map/ppermute | solution.py:197
  71.3 21.2 %collective-permute-start.10 = (bf16[1024,256]{1,0:T(8,128)(2,1)}, bf16[1024,256]{1,0:T(8,128)(2,1)}, u32[]{:S(2)}, u32[]{:S(2)}) collective-permute-start(bf16[1024,256]{1,0:T(8,128)(2,1)} %collective-permute-done.9.rest_9_), channel_id=1, source_target_pairs={{0,16},{16,0},{32,48},{48,32},{64,80},{80,64},{96,112},{112,96},{1... | collective-permute-start | bytes 1572872 | tf_op jit(solution)/shard_map/ppermute | solution.py:197
  92.4 0.8 copy-start.4

commit v2 on v1

v2 whole, which is shorter than its diff:
```python
import functools

import jax
import jax.numpy as jnp
from jax import lax
from jax.experimental import pallas as pl
from jax.experimental.pallas import tpu as pltpu
from jax.sharding import PartitionSpec as P

DH = 128
QT = 256
BK = 128
LOG2E = 1.4426950408889634
VMEM_BYTES = 52 * 2**20


def scaled_query(query_rows):
    scaled = query_rows.astype(jnp.float32) * (LOG2E * DH**-0.5)
    high = scaled.astype(jnp.bfloat16)
    low = (scaled - high.astype(jnp.float32)).astype(jnp.bfloat16)
    return jnp.concatenate([high, low], axis=1)


def scores_of(query_pair, keys_twice):
    return lax.dot_general(
        query_pair, keys_twice, (((1,), (1,)), ((), ())), preferred_element_type=jnp.float32
    )


def own_kernel(heads, q_ref, near_ref, other_ref, acc_ref, stat_ref, keys, values):
    blocks = near_ref.shape[0]
    for n in range(2 * blocks):
        source = near_ref if n < blocks else other_ref
        rows = slice(n * BK, (n + 1) * BK)
        block = source[n % blocks, 0]
        keys[rows, :DH] = block
        keys[rows, DH:] = block
        values[rows, :DH] = source[n % blocks, 1]
    values[:, DH:] = jnp.ones((2 * blocks * BK, DH), jnp.bfloat16)

    def tile(t, carry):
        at = pl.ds(pl.multiple_of(t * QT, QT), QT)
        for head in range(heads):
            columns = slice(head * DH, (head + 1) * DH)
            scores = scores_of(scaled_query(q_ref[at, columns]), keys[...])
            top = jnp.max(scores, axis=1, keepdims=True)
            weights = jnp.exp2(scores - top).astype(jnp.bfloat16)
            sums = jnp.dot(weights, values[...], preferred_element_type=jnp.float32)
            acc_ref[at, columns] = sums[:, :DH]
            stat_ref[at, head : head + 1] = top
            stat_ref[at, heads + head : heads + head + 1] = sums[:, DH : DH + 1]
        return carry

    lax.fori_loop(0, q_ref.shape[0] // QT, tile, 0)


def far_kernel(heads, tiles, slots, chunks, ids_ref, place_ref, q_ref, *rest):
    own = [(rest[2 * n], rest[2 * n + 1]) for n in range(chunks)]
    pieces, (out_ref, keys, values, key_sem, value_sem) = rest[2 * chunks : -5], rest[-5:]
    piece_blocks = pieces[0].shape[0]
    plane, core, part = place_ref[0], place_ref[1], place_ref[2]

    def fetch(source, block, t, j):
        to = pl.ds(pl.multiple_of(j * BK, BK), BK)
        for column in (0, DH):
            pltpu.make_async_copy(
                source.at[block, 0], keys.at[t, to, pl.ds(column, DH)], key_sem.at[t]
            ).start()
        pltpu.make_async_copy(
            source.at[block, 1], values.at[t, to, pl.ds(0, DH)], value_sem.at[t]
        ).start()

    def fetch_from(low, high, at, block, t, j):
        if high - low == 1:
            fetch(pieces[low], block, t, j)
            return
        middle = (low + high) // 2
        lax.cond(
            at < middle,
            lambda: fetch_from(low, middle, at, block, t, j),
            lambda: fetch_from(middle, high, at, block, t, j),
        )

    def slot(n, carry):
        t, j = n // slots, n % slots
        used = ids_ref[n] >= 0
        number = jnp.maximum(ids_ref[n], 0)
        span, within = number // (2 * piece_blocks), number % (2 * piece_blocks)
        half, block = within // piece_blocks, within % piece_blocks
        back = plane - span // 2
        sibling = (span % 2 != core).astype(jnp.int32)
        other = (half != part).astype(jnp.int32)
        at = jnp.where(used, back * 4 + sibling * 2 + other, 0)
        block = jnp.where(used, (block + half * (piece_blocks // 2)) % piece_blocks, 0)
        fetch_from(0, len(pieces), at, block, t, j)
        return carry

    lax.fori_loop(0, tiles * slots, slot, 0)

    for t in range(tiles):
        acc_ref, stat_ref = own[t * chunks // tiles]
        pltpu.make_async_copy(keys.at[t], keys.at[t], key_sem.at[t]).wait()
        pltpu.make_async_copy(
            values.at[t, :, pl.ds(0, DH)], values.at[t, :, pl.ds(0, DH)], value_sem.at[t]
        ).wait()
        values[t, :, DH:] = jnp.ones((slots * BK, DH), jnp.bfloat16)
        for j in range(slots):

            @pl.when(ids_ref[t * slots + j] < 0)
            def _():
                values[t, j * BK : (j + 1) * BK, :] = jnp.zeros((BK, 2 * DH), jnp.bfloat16)

        at = slice(t * QT, (t + 1) * QT)
        first = (t % (tiles // chunks)) * QT
        own_at = slice(first, first + QT)
        for head in range(heads):
            columns = slice(head * DH, (head + 1) * DH)
            scores = scores_of(scaled_query(q_ref[at, columns]), keys[t])
            own_top = stat_ref[own_at, head : head + 1]
            own_total = stat_ref[own_at, heads + head : heads + head + 1]
            top = jnp.maximum(jnp.max(scores, axis=1, keepdims=True), own_top)
            weights = jnp.exp2(scores - top).astype(jnp.bfloat16)
            sums = jnp.dot(weights, values[t], preferred_element_type=jnp.float32)
            shrink = jnp.exp2(own_top - top)
            total = own_total * shrink + sums[:, DH : DH + 1]
            result = (acc_ref[own_at, columns] * shrink + sums[:, :DH]) / total
            out_ref[at, columns] = result.astype(jnp.bfloat16)


def own_attention(q, near, other, chunk, chunks):
    tokens, width = q.shape[0] // chunks, q.shape[1]
    heads = width // DH
    keys = 2 * near.shape[0] * BK
    whole = pl.BlockSpec(memory_space=pltpu.VMEM)
    scores = tokens * heads * keys
    return pl.pallas_call(
        functools.partial(own_kernel, heads),
        grid=(1,),
        out_shape=(
            jax.ShapeDtypeStruct((tokens, width), jnp.float32),
            jax.ShapeDtypeStruct((tokens, 2 * heads), jnp.float32),
        ),
        in_specs=[pl.BlockSpec((tokens, width), lambda _: (chunk, 0)), whole, whole],
        out_specs=(whole, whole),
        scratch_shapes=[pltpu.VMEM((keys, 2 * DH), jnp.bfloat16)] * 2,
        cost_estimate=pl.CostEstimate(
            flops=8 * scores * DH, bytes_accessed=8 * tokens * width, transcendentals=scores
        ),
        compiler_params=pltpu.CompilerParams(vmem_limit_bytes=VMEM_BYTES),
        name="own_attention",
    )(q, near, other)


def far_attention(ids, place, q, own, pieces, tiles, slots):
    tokens, width = q.shape
    heads = width // DH
    whole = pl.BlockSpec(memory_space=pltpu.VMEM)
    scalars = pl.BlockSpec(memory_space=pltpu.SMEM)
    anywhere = pl.BlockSpec(memory_space=pl.ANY)
    scores = tokens * heads * slots * BK
    return pl.pallas_call(
        functools.partial(far_kernel, heads, tiles, slots, len(own)),
        out_shape=jax.ShapeDtypeStruct((tokens, width), jnp.bfloat16),
        in_specs=[scalars] * 2 + [whole] * (1 + 2 * len(own)) + [anywhere] * len(pieces),
        out_specs=whole,
        scratch_shapes=[
            pltpu.VMEM((tiles, slots * BK, 2 * DH), jnp.bfloat16),
            pltpu.VMEM((tiles, slots * BK, 2 * DH), jnp.bfloat16),
            pltpu.SemaphoreType.DMA((tiles,)),
            pltpu.SemaphoreType.DMA((tiles,)),
        ],
        cost_estimate=pl.CostEstimate(
            flops=8 * scores * DH, bytes_accessed=8 * tokens * width, transcendentals=scores
        ),
        compiler_params=pltpu.CompilerParams(vmem_limit_bytes=VMEM_BYTES),
        name="far_attention",
    )(ids, place, q, *[x for pair in own for x in pair], *pieces)


def on_device(queries, key_states, value_states, block_lists):
    tok_rows = queries.shape[1]
    model_width = queries.shape[2]
    kv_heads = key_states.shape[2] // DH
    seq_size, spans = lax.axis_size("seq"), lax.axis_size("span")
    width = model_width // kv_heads
    place = lax.axis_index("seq")
    part = place // kv_heads
    turned = kv_heads // 2
    group = (place + part * turned) % kv_heads
    span = lax.axis_index("span")
    tile_count, slots = block_lists.shape[2], block_lists.shape[3]
    tiles = tile_count // 2
    rings = [
        [c * kv_heads + (j + c * turned) % kv_heads for j in range(kv_heads)] for c in range(2)
    ]

    def turn(x):
        return lax.ppermute(x, "seq", [pair for a, b in zip(*rings) for pair in ((a, b), (b, a))])

    def shift(x, by):
        return lax.ppermute(x, "span", [(i, (i + by) % spans) for i in range(spans)])

    def swap(x):
        return lax.ppermute(x, "span", [(i, i ^ 1) for i in range(spans)])

    def by_head(x, columns):
        return jnp.transpose(x[0].reshape(tok_rows, kv_heads, columns), (1, 0, 2))

    kv_send = jnp.stack([by_head(key_states, DH), by_head(value_states, DH)], axis=1)
    near = lax.all_to_all(kv_send, "seq", 0, 0, tiled=True, axis_index_groups=rings)
    other = turn(near)
    q_send = by_head(queries, width)
    q = lax.all_to_all(q_send, "seq", 0, 0, tiled=True, axis_index_groups=rings)
    q = q.reshape(kv_heads * tok_rows, width)

    up_near = shift(near, 2)
    down_near = shift(near, -2)
    up_other = shift(other, 2)
    down_other = shift(other, -2)
    two_near = shift(up_near, 2)
    own_swaps = [swap(near), swap(other)]
    own = [own_attention(q, near, other, 0, 2)]
    (own[0], down_other, two_near) = lax.optimization_barrier((own[0], down_other, two_near))
    two_other = shift(down_other, -2)
    own.append(own_attention(q, near, other, 1, 2))
    late = (two_near, two_other, up_near, up_other, down_near, down_other)
    late, own[1] = lax.optimization_barrier((late, own[1]))
    two_near, two_other, up_near, up_other, down_near, down_other = late
    pieces = [near, other] + own_swaps
    for pair in ((up_near, up_other), (two_near, two_other), (down_near, down_other)):
        pieces += list(pair) + [swap(x) for x in pair]
    ids = lax.dynamic_slice(block_lists, (0, group, part * tiles, 0), (1, 1, tiles, slots))[0, 0]
    ids = jnp.where(part == 0, ids, jnp.roll(ids, tiles // 2, axis=0))
    where = jnp.stack([span // 2, span % 2, part]).astype(jnp.int32)
    out = far_attention(ids.reshape(tiles * slots), where, q, own, pieces, tiles, slots)

    out = out.reshape(kv_heads, tok_rows, width)
    back = lax.all_to_all(out, "seq", 0, 0, tiled=True, axis_index_groups=rings)
    return jnp.transpose(back, (1, 0, 2)).reshape(1, tok_rows, model_width)


def solution(mesh):
    in_specs = (
        P("span", "seq", None),
        P("span", "seq", None),
        P("span", "seq", None),
        P("span", None, None, None),
    )
    out_specs = P("span", "seq", None)
    return jax.shard_map(
        on_device, mesh=mesh, in_specs=in_specs, out_specs=out_specs, check_vma=False
    )
```

time: 142 us -> 124 us (0.87)
  waiting for transfers between devices: 42.8 us -> 23.7 us
  Pallas kernels: 39.4 us -> 41.6 us
  blocking collectives: 27.1 us -> 25.4 us
    ppermute x6, waiting for transfers between devices: 26.9 us -> 1.5 us  [shift(): lax.ppermute(x, 'span', [(i, (i + by) % spans) for i in range(spans)])]
    ppermute x0 -> x1, waiting for transfers between devices: none -> 8.2 us  [turn(): lax.ppermute(x, 'seq', [pair for a, b in zip(*rings) for pair in ((a, b),...]
    all_to_all x1, waiting for transfers between devices: 15.9 us -> 7.8 us  [on_device(): lax.all_to_all(kv_send, 'seq', 0, 0, tiled=True, axis_index_groups=rings)]
    ppermute x8, waiting for transfers between devices: 0.02 us -> 4.4 us  [swap(): return lax.ppermute(x, 'span', [(i, i ^ 1) for i in range(spans)])]
    ppermute x0 -> x1, starting transfers between devices: none -> 2.18 us  [turn(): lax.ppermute(x, 'seq', [pair for a, b in zip(*rings) for pair in ((a, b),...]
    pallas_call x2 -> x3, Pallas kernels: 39.4 us -> 41.6 us  [the longest x2 22.4 us: own_attention(): pl.pallas_call(functools.partial(own_kernel, heads), grid=(1,), out_shape...]
    all_to_all x1, waiting for transfers between devices: 0.01 us -> 1.77 us  [on_device(): q = lax.all_to_all(q_send, 'seq', 0, 0, tiled=True, axis_index_groups=rings)]
    all_to_all x1, starting transfers between devices: 7.12 us -> 5.48 us  [on_device(): lax.all_to_all(kv_send, 'seq', 0, 0, tiled=True, axis_index_groups=rings)]
  transfers between devices with their start and end apart: 16 -> 17, of which waited for: 6 -> 10; matrix products, arithmetic and copies ran while one was open for 1% -> 2% of each run, Pallas kernels for 15% -> 18%
where the time goes in v2:
time: 124 us
  Pallas kernels  41.6 us (34%)
  blocking collectives  25.4 us (20%)
  starting transfers between devices  23.9 us (19%)
  waiting for transfers between devices  23.7 us (19%)
  local copies, waits for them, and re-layouts  8.33 us (7%)
    all_to_all x1, blocking collectives, on_device(): back = lax.all_to_all(out, 'seq', 0, 0, tiled=True, axis_index_groups=rings)  25.4 us
    pallas_call x2, Pallas kernels, own_attention(): pl.pallas_call(functools.partial(own_kernel, heads), grid=(1,), out_shape...  22.4 us
    pallas_call x1, Pallas kernels, far_attention(): pl.pallas_call(functools.partial(far_kernel, heads, tiles, slots, len(own...  19.2 us
    ppermute x6, starting transfers between devices, shift(): lax.ppermute(x, 'span', [(i, (i + by) % spans) for i in range(spans)])  11.3 us
    ppermute x1, waiting for transfers between devices, turn(): lax.ppermute(x, 'seq', [pair for a, b in zip(*rings) for pair in ((a, b),...  8.2 us
    all_to_all x1, waiting for transfers between devices, on_device(): lax.all_to_all(kv_send, 'seq', 0, 0, tiled=True, axis_index_groups=rings)  7.8 us
    all_to_all x1, starting transfers between devices, on_device(): lax.all_to_all(kv_send, 'seq', 0, 0, tiled=True, axis_index_groups=rings)  5.48 us
    ppermute x8, waiting for transfers between devices, swap(): return lax.ppermute(x, 'span', [(i, i ^ 1) for i in range(spans)])  4.4 us
  transfers between devices with their start and end apart: 17, of which 10 were waited for; matrix products, arithmetic and copies ran while one was open for 2% of the time, Pallas kernels for 18%

profile of v2, /device:TPU:0, one launch (start us, length us, event | category | flops | bytes accessed | tf_op | source)
XLA Modules:
  0.0 124.1 jit_solution(2841373359890754590)
XLA Ops:
  0.0 0.0 copy-start
  0.0 1.1 copy.8
  1.1 0.2 copy.9
  1.3 0.0 copy-start.1
  1.3 1.2 copy.10
  2.6 0.2 copy.11
  2.8 0.9 pad_maximum_fusion
  3.6 5.5 %all-to-all-start.1 = ((bf16[8,2,128,128]{3,2,1,0:T(8,128)(2,1)}), bf16[8,2,128,128]{3,2,1,0:T(8,128)(2,1)S(1)}, u32[]{:S(2)}, u32[]{:S(2)}) async-start(bf16[8,2,128,128]{3,2,1,0:T(8,128)(2,1)} %pad_maximum_fusion), calls=%async_computation.1 | async-start | bytes 1048576 | tf_op jit(solution)/shard_map/all_to_all | solution.py:210
  9.1 0.0 copy-done.1
  9.1 0.3 copy.13
  9.5 1.4 %copy.15 = bf16[128,8,768]{2,0,1:T(8,128)(2,1)} copy(bf16[128,8,768]{2,1,0:T(8,128)(2,1)S(1)} %bitcast.25) | data formatting | bytes 3145728 | tf_op jit(solution)/shard_map/reshape;squeeze | solution.py:207
  10.9 7.8 %all-to-all-done.1.near_ref.rest_4_ = bf16[8,2,128,128]{3,2,1,0:T(8,128)(2,1)S(1)} async-done(((bf16[8,2,128,128]{3,2,1,0:T(8,128)(2,1)}), bf16[8,2,128,128]{3,2,1,0:T(8,128)(2,1)S(1)}, u32[]{:S(2)}, u32[]{:S(2)}) %all-to-all-start.1) | async-done | bytes 524320 | tf_op jit(solution)/shard_map/all_to_all | solution.py:210
  18.7 3.6 %all-to-all-start = ((bf16[8,128,768]{2,1,0:T(8,128)(2,1)}), bf16[8,128,768]{2,1,0:T(8,128)(2,1)S(1)}, u32[]{:S(2)}, u32[]{:S(2)}) async-start(bf16[8,128,768]{2,1,0:T(8,128)(2,1)} %bitcast.23), calls=%async_computation | async-start | bytes 3145728 | tf_op jit(solution)/shard_map/all_to_all | solution.py:213
  22.3 2.2 %collective-permute-start = (bf16[8,2,128,128]{3,2,1,0:T(8,128)(2,1)S(1)}, bf16[8,2,128,128]{3,2,1,0:T(8,128)(2,1)S(1)}, u32[]{:S(2)}, u32[]{:S(2)}) collective-permute-start(bf16[8,2,128,128]{3,2,1,0:T(8,128)(2,1)S(1)} %all-to-all-done.1.near_ref.rest_4_), channel_id=1, source_target_pairs={{0,12},{12,0},{1,13},{13,1},{2,14},{14,2},{3,15},{15,3},{4,8},{8,4... | collective-permute-start | bytes 1572872 | tf_op jit(solution)/shard_map/ppermute | solution.py:198
  24.5 1.9 %collective-permute-start.2 = (bf16[8,2,128,128]{3,2,1,0:T(8,128)(2,1)S(1)}, bf16[8,2,128,128]{3,2,1,0:T(8,128)(2,1)}, u32[]{:S(2)}, u32[]{:S(2)}) collective-permute-start(bf16[8,2,128,128]{3,2,1,0:T(8,128)(2,1)S(1)} %all-to-all-done.1.near_ref.rest_4_), channel_id=1, source_target_pairs={{0,32},{16,48},{32,64},{48,80},{64,96},{80,112},{96,0},{112,16},{1... | collective-permute-start | bytes 1572872 | tf_op jit(solution)/shard_map/ppermute | solution.py:201
  26.4 0.0 collective-permute-start.7
  26.4 2.1 %collective-permute-start.6 = (bf16[8,2,128,128]{3,2,1,0:T(8,128)(2,1)S(1)}, bf16[8,2,128,128]{3,2,1,0:T(8,128)(2,1)}, u32[]{:S(2)}, u32[]{:S(2)}) collective-permute-start(bf16[8,2,128,128]{3,2,1,0:T(8,128)(2,1)S(1)} %all-to-all-done.1.near_ref.rest_4_), channel_id=1, source_target_pairs={{0,96},{16,112},{32,0},{48,16},{64,32},{80,48},{96,64},{112,80},{1... | collective-permute-start | bytes 1572872 | tf_op jit(solution)/shard_map/ppermute | solution.py:201
  28.5 8.2 %collective-permute-done.other_ref.rest_5_ = bf16[8,2,128,128]{3,2,1,0:T(8,128)(2,1)S(1)} collective-permute-done((bf16[8,2,128,128]{3,2,1,0:T(8,128)(2,1)S(1)}, bf16[8,2,128,128]{3,2,1,0:T(8,128)(2,1)S(1)}, u32[]{:S(2)}, u32[]{:S(2)}) %collective-permute-start) | collective-permute-done | bytes 524320 | tf_op jit(solution)/shard_map/ppermute | solution.py:198
  36.7 0.0 collective-permute-start.8
  36.7 4.0 %collective-permute-start.1 = (bf16[8,2,128,128]{3,2,1,0:T(8,128)(2,1)S(1)}, bf16[8,2,128,128]{3,2,1,0:T(8,128)(2,1)}, u32[]{:S(2)}, u32[]{:S(2)}) collective-permute-start(bf16[8,2,128,128]{3,2,1,0:T(8,128)(2,1)S(1)} %collective-permute-done.other_ref.rest_5_), channel_id=1, source_target_pairs={{0,96},{16,112},{32,0},{48,16},{64,32},{80,48},{96,64},{112,80},{1... | collective-permute-start | bytes 1572872 | tf_op jit(solution)/shard_map/ppermute | solution.py:201
  40.7 0.0 collective-permute-done.2.rest_8_
  40.8 0.0 collective-permute-start.3
  40.8 1.8 %all-to-all-done = bf16[8,128,768]{2,1,0:T(8,128)(2,1)S(1)} async-done(((bf16[8,128,768]{2,1,0:T(8,128)(2,1)}), bf16[8,128,768]{2,1,0:T(8,128)(2,1)S(1)}, u32[]{:S(2)}, u32[]{:S(2)}) %all-to-all-start) | async-done | bytes 1572896 | tf_op jit(solution)/shard_map/all_to_all | solution.py:213
  42.5 0.0 copy-start.2
  42.5 1.1 copy-done.2
  43.7 11.2 %own_attention.2 = (f32[512,768]{1,0:T(8,128)}, f32[512,12]{1,0:T(8,128)S(1)}) custom-call(bf16[1024,768]{1,0:T(8,128)(2,1)} %bitcast.27, bf16[8,2,128,128]{3,2,1,0:T(8,128)(2,1)S(1)} %all-to-all-done.1.near_ref.rest_4_, bf16[8,2,128,128]{3,2,1,0:T(8,128)(2,1)S(1)} %collective-permute-done.other_ref.rest_5_), custom_call_target="tpu_custom_call" | custom-call | flops 6442450944 | bytes 3145728 | tf_op jit(solution)/shard_map/own_attention/pallas_call | solution.py:136
  54.9 1.5 %collective-permute-done.3.rest_12_ = bf16[8,2,128,128]{3,2,1,0:T(8,128)(2,1)} collective-permute-done((bf16[8,2,128,128]{3,2,1,0:T(8,128)(2,1)}, bf16[8,2,128,128]{3,2,1,0:T(8,128)(2,1)}, u32[]{:S(2)}, u32[]{:S(2)}) %collective-permute-start.3) | collective-permute-done | bytes 524320 | tf_op jit(solution)/shard_map/ppermute | solution.py:201
  56.3 0.5 collective-permute-start.5
  56.8 0.0 collective-permute-done.1.rest_17_
  56.8 2.8 %collective-permute-start.4 = (bf16[8,2,128,128]{3,2,1,0:T(8,128)(2,1)}, bf16[8,2,128,128]{3,2,1,0:T(8,128)(2,1)S(1)}, u32[]{:S(2)}, u32[]{:S(2)}) collective-permute-start(bf16[8,2,128,128]{3,2,1,0:T(8,128)(2,1)} %collective-permute-done.1.rest_17_), channel_id=1, source_target_pairs={{0,96},{16,112},{32,0},{48,16},{64,32},{80,48},{96,64},{112,80},{1... | collective-permute-start | bytes 1572872 | tf_op jit(solution)/shard_map/ppermute | solution.py:201
  59.6 11.2 %own_attention.3 = (f32[512,768]{1,0:T(8,128)}, f32[512,12]{1,0:T(8,128)S(1)}) custom-call(bf16[1024,768]{1,0:T(8,128)(2,1)} %bitcast.28, bf16[8,2,128,128]{3,2,1,0:T(8,128)(2,1)S(1)} %all-to-all-done.1.near_ref.rest_4_, bf16[8,2,128,128]{3,2,1,0:T(8,128)(2,1)S(1)} %collective-permute-done.other_ref.rest_5_), custom_call_target="tpu_custom_call" | custom-call | flops 6442450944 | bytes 3145728 | tf_op jit(solution)/shard_map/own_attention/pallas_call | solution.py:136
  70.7 0.0 collective-permute-done.6.rest_16_
  70.8 0.0 collective-permute-done.5.rest_9_
  70.8 0.0 copy-start.3
  70.8 0.0 collective-permute-done.4.rest_13_
  70.8 0.0 copy-start.4
  70.8 0.1 collective-permute-start.9
  70.9 0.0 copy-done
  70.9 0.5 collective-permute-start.10
  71.5 0.1 collective-permute-start.11
  71.6 0.0 collective-permute-done.7.rest_6_
  71.6 0.4 collective-permute-start.12
  72.0 0.0 collective-permute-done.8.rest_7_
  72.0 0.1 collective-permute-start.13
  72.1 0.9 collective-permute-done.9.rest_10_
  73.0 0.0 copy-start.5
  73.0 0.1 collective-permute-start.14
  73.1 0.1 squeeze.3
  73.2 0.1 concatenate.7
  73.3 0.1 pad_add_fusion.1.place_ref
  73.4 1.0 collective-permute-done.10.rest_11_
  74.4 0.2 collective-permute-done.11.rest_14_
  74.6 1.3 %collective-permute-done.12.rest_15_ = bf16[8,2,128,128]{3,2,1,0:T(8,128)(2,1)} collective-permute-done((bf16[8,2,128,128]{3,2,1,0:T(8,128)(2,1)S(1)}, bf16[8,2,128,128]{3,2,1,0:T(8,128)(2,1)}, u32[]{:S(2)}, u32[]{:S(2)}) %collective-permute-start.12) | collective-permute-done | bytes 524320 | tf_op jit(solution)/shard_map/ppermute | solution.py:204
  75.9 0.2 collective-permute-done.13.rest_18_
  76.1 0.7 collective-permute-done.14.rest_19_
  76.9 0.0 copy-done.3
  76.9 0.0 copy-done.4
  76.9 0.0 copy-done.5
  76.9 19.2 %far_attention.1 = bf16[1024,768]{1,0:T(8,128)(2,1)} custom-call(s32[32]{0:T(128)S(1)} %broadcast_select_fusion.ids_ref, s32[3]{0:T(128)S(1)} %pad_add_fusion.1.place_ref, bf16[1024,768]{1,0:T(8,128)(2,1)} %bitcast.29, f32[512,768]{1,0:T(8,128)} %get-tuple-element.23.rest_0_, f32[512,12]{1,0:T(8,128)S(1)} %get-tuple-element.24.rest_1_, ...), custom_call_target="tpu_custom_call" | custom-call | flops 6442450944 | bytes 6291456 | tf_op jit(solution)/shard_map/far_attention/pallas_call | solution.py:161
  96.1 25.4 %all_to_all.15 = bf16[8,128,768]{2,1,0:T(8,128)(2,1)S(1)} all-to-all(bf16[8,128,768]{2,1,0:T(8,128)(2,1)} %bitcast.30), channel_id=1, replica_groups={{0,1,2,3,4,5,6,7},{12,13,14,15,8,9,10,11},{16,17,18,19,20,21,22,23},{28..., dimensions={0} | all-to-all | bytes 3145728 | tf_op jit(solution)/shard_map/all_to_all | solution.py:238
  121.6 0.9 copy.12
  122.4 1.6 %reshape.16 = bf16[1,128,6144]{2,1,0:T(8,128)(2,1)} reshape(bf16[128,8,768]{2,1,0:T(8,128)(2,1)S(1)} %copy.12) | data formatting | bytes 3145728 | tf_op jit(solution)/shard_map/reshape | solution.py:239
  (4 shorter events, 0.0 us)
Async XLA Ops:
  0.0 70.9 %copy-start = (s32[1,8,8,8]{3,2,1,0:T(8,128)S(1)}, s32[1,8,8,8]{3,2,1,0:T(8,128)}, u32[]{:S(2)}) copy-start(s32[1,8,8,8]{3,2,1,0:T(8,128)} %param.7) | copy-start | bytes 6148
  1.3 7.8 %copy-start.1 = (bf16[1,128,6144]{2,1,0:T(8,128)(2,1)S(1)}, bf16[1,128,6144]{2,1,0:T(8,128)(2,1)}, u32[]{:S(2)}) copy-start(bf16[1,128,6144]{2,1,0:T(8,128)(2,1)} %param.4) | copy-start | bytes 4718596
  3.6 15.1 %all-to-all-start.1 = ((bf16[8,2,128,128]{3,2,1,0:T(8,128)(2,1)}), bf16[8,2,128,128]{3,2,1,0:T(8,128)(2,1)S(1)}, u32[]{:S(2)}, u32[]{:S(2)}) async-start(bf16[8,2,128,128]{3,2,1,0:T(8,128)(2,1)} %pad_maximum_fusion), calls=%async_computation.1 | async-start | bytes 1048576 | tf_op jit(solution)/shard_map/all_to_all | solution.py:210
  18.7 23.8 %all-to-all-start = ((bf16[8,128,768]{2,1,0:T(8,128)(2,1)}), bf16[8,128,768]{2,1,0:T(8,128)(2,1)S(1)}, u32[]{:S(2)}, u32[]{:S(2)}) async-start(bf16[8,128,768]{2,1,0:T(8,128)(2,1)} %bitcast.23), calls=%async_computation | async-start | bytes 3145728 | tf_op jit(solution)/shard_map/all_to_all | solution.py:213
  22.3 14.4 %collective-permute-start = (bf16[8,2,128,128]{3,2,1,0:T(8,128)(2,1)S(1)}, bf16[8,2,128,128]{3,2,1,0:T(8,128)(2,1)S(1)}, u32[]{:S(2)}, u32[]{:S(2)}) collective-permute-start(bf16[8,2,128,128]{3,2,1,0:T(8,128)(2,1)S(1)} %all-to-all-done.1.near_ref.rest_4_), channel_id=1, source_target_pairs={{0,12},{12,0},{1,13},{13,1},{2,14},{14,2},{3,15},{15,3},{4,8},{8,4... | collective-permute-start | bytes 1572872 | tf_op jit(solution)/shard_map/ppermute | solution.py:198
  24.5 16.3 %collective-permute-start.2 = (bf16[8,2,128,128]{3,2,1,0:T(8,128)(2,1)S(1)}, bf16[8,2,128,128]{3,2,1,0:T(8,128)(2,1)}, u32[]{:S(2)}, u32[]{:S(2)}) collective-permute-start(bf16[8,2,128,128]{3,2,1,0:T(8,128)(2,1)S(1)} %all-to-all-done.1.near_ref.rest_4_), channel_id=1, source_target_pairs={{0,32},{16,48},{32,64},{48,80},{64,96},{80,112},{96,0},{112,16},{1... | collective-permute-start | bytes 1572872 | tf_op jit(solution)/shard_map/ppermute | solution.py:201
  26.4 45.2 %collective-permute-start.7 = (bf16[8,2,128,128]{3,2,1,0:T(8,128)(2,1)S(1)}, bf16[8,2,128,128]{3,2,1,0:T(8,128)(2,1)}, u32[]{:S(2)}, u32[]{:S(2)}) collective-permute-start(bf16[8,2,128,128]{3,2,1,0:T(8,128)(2,1)S(1)} %all-to-all-done.1.near_ref.rest_4_), channel_id=1, source_target_pairs={{0,16},{16,0},{32,48},{48,32},{64,80},{80,64},{96,112},{112,96},{1... | collective-permute-start | bytes 1572872 | tf_op jit(solution)/shard_map/ppermute | solution.py:204
  26.4 44.4 %collective-permute-start.6 = (bf16[8,2,128,128]{3,2,1,0:T(8,128)(2,1)S(1)}, bf16[8,2,128,128]{3,2,1,0:T(8,128)(2,1)}, u32[]{:S(2)}, u32[]{:S(2)}) collective-permute-start(bf16[8,2,128,128]{3,2,1,0:T(8,128)(2,1)S(1)} %all-to-all-done.1.near_ref.rest_4_), channel_id=1, source_target_pairs={{0,96},{16,112},{32,0},{48,16},{64,32},{80,48},{96,64},{112,80},{1... | collective-permute-start | bytes 1572872 | tf_op jit(solution)/shard_map/ppermute | solution.py:201
  36.7 35.3 %collective-permute-start.8 = (bf16[8,2,128,128]{3,2,1,0:T(8,128)(2,1)S(1)}, bf16[8,2,128,128]{3,2,1,0:T(8,128)(2,1)}, u32[]{:S(2)}, u32[]{:S(2)}) collective-permute-start(bf16[8,2,128,128]{3,2,1,0:T(8,128)(2,1)S(1)} %collective-permute-done.other_ref.rest_5_), channel_id=1, source_target_pairs={{0,16},{16,0},{32,48},{48,32},{64,80},{80,64},{96,112},{112,96},{1... | collective-permute-start | bytes 1572872 | tf_op jit(solution)/shard_map/ppermute | solution.py:204
  36.7 20.1 %collective-permute-start.1 = (bf16[8,2,128,128]{3,2,1,0:T(8,128)(2,1)S(1)}, bf16[8,2,128,128]{3,2,1,0:T(8,128)(2,1)}, u32[]{:S(2)}, u32[]{:S(2)}) collective-permute-start(bf16[8,2,128,128]{3,2,1,0:T(8,128)(2,1)S(1)} %collective-permute-done.other_ref.rest_5_), channel_id=1, source_target_pairs={{0,96},{16,112},{32,0},{48,16},{64,32},{80,48},{96,64},{112,80},{1... | collective-permute-start | bytes 1572872 | tf_op jit(solution)/shard_map/ppermute | solution.py:201
  40.8 15.6 %collective-permute-start.3 = (bf16[8,2,128,128]{3,2,1,0:T(8,128)(2,1)}, bf16[8,2,128,128]{3,2,1,0:T(8,128)(2,1)}, u32[]{:S(2)}, u32[]{:S(2)}) collective-permute-start(bf16[8,2,128,128]{3,2,1,0:T(8,128)(2,1)} %collective-permute-done.2.rest_8_), channel_id=1, source_target_pairs={{0,32},{16,48},{32,64},{48,80},{64,96},{80,112},{96,0},{112,16},{1... | collective-permute-start | bytes 1572872 | tf_op jit(solution)/shard_map/ppermute | solution.py:201
  42.5 1.1 copy-start.2
  56.3 14.4 %collective-permute-start.5 = (bf16[8,2,128,128]{3,2,1,0:T(8,128)(2,1)S(1)}, bf16[8,2,128,128]{3,2,1,0:T(8,128)(2,1)S(1)}, u32[]{:S(2)}, u32[]{:S(2)}) collective-permute-start(bf16[8,2,128,128]{3,2,1,0:T(8,128)(2,1)S(1)} %collective-permute-done.other_ref.rest_5_), channel_id=1, source_target_pairs={{0,32},{16,48},{32,64},{48,80},{64,96},{80,112},{96,0},{112,16},{1... | collective-permute-start | bytes 1572872 | tf_op jit(solution)/shard_map/ppermute | solution.py:201
  56.8 14.0 %collective-permute-start.4 = (bf16[8,2,128,128]{3,2,1,0:T(8,128)(2,1)}, bf16[8,2,128,128]{3,2,1,0:T(8,128)(2,1)S(1)}, u32[]{:S(2)}, u32[]{:S(2)}) collective-permute-start(bf16[8,2,128,128]{3,2,1,0:T(8,128)(2,1)} %collective-permute-done.1.rest_17_), channel_id=1, source_target_pairs={{0,96},{16,112},{32,0},{48,16},{64,32},{80,48},{96,64},{112,80},{1... | collective-permute-start | bytes 1572872 | tf_op jit(solution)/shard_map/ppermute | solution.py:201
  70.8 6.1 %copy-start.3 = (bf16[8,2,128,128]{3,2,1,0:T(8,128)(2,1)}, bf16[8,2,128,128]{3,2,1,0:T(8,128)(2,1)S(1)}, u32[]{:S(2)}) copy-start(bf16[8,2,128,128]{3,2,1,0:T(8,128)(2,1)S(1)} %collective-permute-done.5.rest_9_) | copy-start | bytes 1572868
  70.8 6.1 %copy-start.4 = (bf16[8,2,128,128]{3,2,1,0:T(8,128)(2,1)}, bf16[8,2,128,128]{3,2,1,0:T(8,128)(2,1)S(1)}, u32[]{:S(2)}) copy-start(bf16[8,2,128,128]{3,2,1,0:T(8,128)(2,1)S(1)} %collective-permute-done.4.rest_13_) | copy-start | bytes 1572868
  70.8 2.2 %collective-permute-start.9 = (bf16[8,2,128,128]{3,2,1,0:T(8,128)(2,1)}, bf16[8,2,128,128]{3,2,1,0:T(8,128)(2,1)S(1)}, u32[]{:S(2)}, u32[]{:S(2)}) collective-permute-start(bf16[8,2,128,128]{3,2,1,0:T(8,128)(2,1)} %collective-permute-done.2.rest_8_), channel_id=1, source_target_pairs={{0,16},{16,0},{32,48},{48,32},{64,80},{80,64},{96,112},{112,96},{1... | collective-permute-start | bytes 1572872 | tf_op jit(solution)/shard_map/ppermute | solution.py:204
  70.9 3.5 %collective-permute-start.10 = (bf16[8,2,128,128]{3,2,1,0:T(8,128)(2,1)S(1)}, bf16[8,2,128,128]{3,2,1,0:T(8,128)(2,1)}, u32[]{:S(2)}, u32[]{:S(2)}) collective-permute-start(bf16[8,2,128,128]{3,2,1,0:T(8,128)(2,1)S(1)} %collective-permute-done.5.rest_9_), channel_id=1, source_target_pairs={{0,16},{16,0},{32,48},{48,32},{64,80},{80,64},{96,112},{112,96},{1... | collective-permute-start | bytes 1572872 | tf_op jit(solution)/shard_map/ppermute | solution.py:204
  71.5 3.2 %collective-permute-start.11 = (bf16[8,2,128,128]{3,2,1,0:T(8,128)(2,1)}, bf16[8,2,128,128]{3,2,1,0:T(8,128)(2,1)}, u32[]{:S(2)}, u32[]{:S(2)}) collective-permute-start(bf16[8,2,128,128]{3,2,1,0:T(8,128)(2,1)} %collective-permute-done.3.rest_12_), channel_id=1, source_target_pairs={{0,16},{16,0},{32,48},{48,32},{64,80},{80,64},{96,112},{112,96},{1... | collective-permute-start | bytes 1572872 | tf_op jit(solution)/shard_map/ppermute | solution.py:204
  71.6 4.3 %collective-permute-start.12 = (bf16[8,2,128,128]{3,2,1,0:T(8,128)(2,1)S(1)}, bf16[8,2,128,128]{3,2,1,0:T(8,128)(2,1)}, u32[]{:S(2)}, u32[]{:S(2)}) collective-permute-start(bf16[8,2,128,128]{3,2,1,0:T(8,128)(2,1)S(1)} %collective-permute-done.4.rest_13_), channel_id=1, source_target_pairs={{0,16},{16,0},{32,48},{48,32},{64,80},{80,64},{96,112},{112,96},{1... | collective-permute-start | bytes 1572872 | tf_op jit(solution)/shard_map/ppermute | solution.py:204
  72.0 4.1 %collective-permute-start.13 = (bf16[8,2,128,128]{3,2,1,0:T(8,128)(2,1)}, bf16[8,2,128,128]{3,2,1,0:T(8,128)(2,1)}, u32[]{:S(2)}, u32[]{:S(2)}) collective-permute-start(bf16[8,2,128,128]{3,2,1,0:T(8,128)(2,1)} %collective-permute-done.6.rest_16_), channel_id=1, source_target_pairs={{0,16},{16,0},{32,48},{48,32},{64,80},{80,64},{96,112},{112,96},{1... | collective-permute-start | bytes 1572872 | tf_op jit(solution)/shard_map/ppermute | solution.py:204
  73.0 3.9 %copy-start.5 = (bf16[8,2,128,128]{3,2,1,0:T(8,128)(2,1)}, bf16[8,2,128,128]{3,2,1,0:T(8,128)(2,1)S(1)}, u32[]{:S(2)}) copy-start(bf16[8,2,128,128]{3,2,1,0:T(8,128)(2,1)S(1)} %collective-permute-done.9.rest_10_) | copy-start | bytes 1572868
  73.0 3.9 %collective-permute-start.14 = (bf16[8,2,128,128]{3,2,1,0:T(8,128)(2,1)}, bf16[8,2,128,128]{3,2,1,0:T(8,128)(2,1)}, u32[]{:S(2)}, u32[]{:S(2)}) collective-permute-start(bf16[8,2,128,128]{3,2,1,0:T(8,128)(2,1)} %collective-permute-done.1.rest_17_), channel_id=1, source_target_pairs={{0,16},{16,0},{32,48},{48,32},{64,80},{80,64},{96,112},{112,96},{1... | collective-permute-start | bytes 1572872 | tf_op jit(solution)/shard_map/ppermute | solution.py:204

commit v3 on v2

v3 whole, which is shorter than its diff:
```python
import functools

import jax
import jax.numpy as jnp
from jax import lax
from jax.experimental import pallas as pl
from jax.experimental.pallas import tpu as pltpu
from jax.sharding import PartitionSpec as P

DH = 128
QT = 256
BK = 128
LOG2E = 1.4426950408889634
VMEM_BYTES = 52 * 2**20


def scaled_query(query_rows):
    scaled = query_rows.astype(jnp.float32) * (LOG2E * DH**-0.5)
    high = scaled.astype(jnp.bfloat16)
    low = (scaled - high.astype(jnp.float32)).astype(jnp.bfloat16)
    return jnp.concatenate([high, low], axis=1)


def scores_of(query_pair, keys_twice):
    return lax.dot_general(
        query_pair, keys_twice, (((1,), (1,)), ((), ())), preferred_element_type=jnp.float32
    )


def pack_kernel(k_ref, v_ref, out_ref):
    for head in range(out_ref.shape[0]):
        columns = slice(head * DH, (head + 1) * DH)
        out_ref[head, :, :DH] = k_ref[0, :, columns]
        out_ref[head, :, DH:] = v_ref[0, :, columns]


def own_kernel(heads, q_ref, near_ref, other_ref, acc_ref, stat_ref, keys, values):
    blocks = near_ref.shape[0]
    for n in range(2 * blocks):
        source = near_ref if n < blocks else other_ref
        rows = slice(n * BK, (n + 1) * BK)
        block = source[n % blocks, :, :DH]
        keys[rows, :DH] = block
        keys[rows, DH:] = block
        values[rows, :DH] = source[n % blocks, :, DH:]
    values[:, DH:] = jnp.ones((2 * blocks * BK, DH), jnp.bfloat16)

    def tile(t, carry):
        at = pl.ds(pl.multiple_of(t * QT, QT), QT)
        for head in range(heads):
            columns = slice(head * DH, (head + 1) * DH)
            scores = scores_of(scaled_query(q_ref[at, columns]), keys[...])
            top = jnp.max(scores, axis=1, keepdims=True)
            weights = jnp.exp2(scores - top).astype(jnp.bfloat16)
            sums = jnp.dot(weights, values[...], preferred_element_type=jnp.float32)
            total = sums[:, DH:]
            acc_ref[at, columns] = sums[:, :DH] / total
            stat_ref[at, head : head + 1] = (top + jnp.log2(total))[:, :1]
        return carry

    lax.fori_loop(0, q_ref.shape[0] // QT, tile, 0)


def far_kernel(heads, tiles, slots, chunks, ids_ref, place_ref, q_ref, *rest):
    own = [(rest[2 * n], rest[2 * n + 1]) for n in range(chunks)]
    pieces, (out_ref, far, ready) = rest[2 * chunks : -3], rest[-3:]
    piece_blocks = pieces[0].shape[0]
    bits = piece_blocks.bit_length() - 1
    plane, core, part = place_ref[0], place_ref[1], place_ref[2]

    def fetch(source, block, t, j):
        to = pl.ds(pl.multiple_of(j * BK, BK), BK)
        pltpu.make_async_copy(
            source.at[block], far.at[t, to, pl.ds(DH, 2 * DH)], ready.at[t]
        ).start()

    def fetch_from(low, high, at, block, t, j):
        if high - low == 1:
            fetch(pieces[low], block, t, j)
            return
        middle = (low + high) // 2
        lax.cond(
            at < middle,
            lambda: fetch_from(low, middle, at, block, t, j),
            lambda: fetch_from(middle, high, at, block, t, j),
        )

    for t in range(tiles):

        def slot(j, carry):
            listed = ids_ref[t * slots + j]
            number = jnp.maximum(listed, 0)
            span, half = number >> (bits + 1), (number >> bits) & 1
            back = plane - (span >> 1)
            at = back * 4 + ((span & 1) ^ core) * 2 + (half ^ part)
            at = jnp.where(listed >= 0, at, 0)
            block = (number & (piece_blocks - 1)) ^ (half * (piece_blocks // 2))
            block = jnp.where(listed >= 0, block, 0)
            fetch_from(0, len(pieces), at, block, t, j)
            return carry

        lax.fori_loop(0, slots, slot, 0)

    for t in range(tiles):
        acc_ref, stat_ref = own[t * chunks // tiles]
        landed = far.at[t, :, pl.ds(DH, 2 * DH)]
        pltpu.make_async_copy(landed, landed, ready.at[t]).wait()
        far[t, :, :DH] = far[t, :, DH : 2 * DH]
        far[t, :, 3 * DH :] = jnp.ones((slots * BK, DH), jnp.bfloat16)
        for j in range(slots):

            @pl.when(ids_ref[t * slots + j] < 0)
            def _():
                far[t, j * BK : (j + 1) * BK, 2 * DH :] = jnp.zeros((BK, 2 * DH), jnp.bfloat16)

        at = slice(t * QT, (t + 1) * QT)
        first = (t % (tiles // chunks)) * QT
        own_at = slice(first, first + QT)
        columns = [slice(head * DH, (head + 1) * DH) for head in range(heads)]
        keys, values = far[t, :, : 2 * DH], far[t, :, 2 * DH :]
        scores = [scores_of(scaled_query(q_ref[at, column]), keys) for column in columns]
        own_size = [stat_ref[own_at, head : head + 1] for head in range(heads)]
        tops = [
            jnp.maximum(jnp.max(score, axis=1, keepdims=True), size)
            for score, size in zip(scores, own_size)
        ]
        weights = [jnp.exp2(score - top).astype(jnp.bfloat16) for score, top in zip(scores, tops)]
        sums = [jnp.dot(w, values, preferred_element_type=jnp.float32) for w in weights]
        for head, column in enumerate(columns):
            share = jnp.exp2(own_size[head] - tops[head])
            total = share + sums[head][:, DH:]
            result = (acc_ref[own_at, column] * share + sums[head][:, :DH]) / total
            out_ref[at, column] = result.astype(jnp.bfloat16)


def pack(key_states, value_states):
    rows, heads = key_states.shape[1], key_states.shape[2] // DH
    whole = pl.BlockSpec(memory_space=pltpu.VMEM)
    return pl.pallas_call(
        pack_kernel,
        out_shape=jax.ShapeDtypeStruct((heads, rows, 2 * DH), key_states.dtype),
        in_specs=[whole] * 2,
        out_specs=whole,
        name="pack",
    )(key_states, value_states)


def own_attention(q, near, other, chunk, chunks):
    tokens, width = q.shape[0] // chunks, q.shape[1]
    heads = width // DH
    keys = 2 * near.shape[0] * BK
    whole = pl.BlockSpec(memory_space=pltpu.VMEM)
    scores = tokens * heads * keys
    return pl.pallas_call(
        functools.partial(own_kernel, heads),
        grid=(1,),
        out_shape=(
            jax.ShapeDtypeStruct((tokens, width), jnp.float32),
            jax.ShapeDtypeStruct((tokens, heads), jnp.float32),
        ),
        in_specs=[pl.BlockSpec((tokens, width), lambda _: (chunk, 0)), whole, whole],
        out_specs=(whole, whole),
        scratch_shapes=[pltpu.VMEM((keys, 2 * DH), jnp.bfloat16)] * 2,
        cost_estimate=pl.CostEstimate(
            flops=8 * scores * DH, bytes_accessed=8 * tokens * width, transcendentals=scores
        ),
        compiler_params=pltpu.CompilerParams(vmem_limit_bytes=VMEM_BYTES),
        name="own_attention",
    )(q, near, other)


def far_attention(ids, place, q, own, pieces, tiles, slots):
    tokens, width = q.shape
    heads = width // DH
    whole = pl.BlockSpec(memory_space=pltpu.VMEM)
    scalars = pl.BlockSpec(memory_space=pltpu.SMEM)
    anywhere = pl.BlockSpec(memory_space=pl.ANY)
    scores = tokens * heads * slots * BK
    return pl.pallas_call(
        functools.partial(far_kernel, heads, tiles, slots, len(own)),
        out_shape=jax.ShapeDtypeStruct((tokens, width), jnp.bfloat16),
        in_specs=[scalars] * 2 + [whole] * (1 + 2 * len(own)) + [anywhere] * len(pieces),
        out_specs=whole,
        scratch_shapes=[
            pltpu.VMEM((tiles, slots * BK, 4 * DH), jnp.bfloat16),
            pltpu.SemaphoreType.DMA((tiles,)),
        ],
        cost_estimate=pl.CostEstimate(
            flops=8 * scores * DH, bytes_accessed=8 * tokens * width, transcendentals=scores
        ),
        compiler_params=pltpu.CompilerParams(vmem_limit_bytes=VMEM_BYTES),
        name="far_attention",
    )(ids, place, q, *[x for pair in own for x in pair], *pieces)


def on_device(queries, key_states, value_states, block_lists):
    tok_rows = queries.shape[1]
    model_width = queries.shape[2]
    kv_heads = key_states.shape[2] // DH
    spans = lax.axis_size("span")
    width = model_width // kv_heads
    place = lax.axis_index("seq")
    part = place // kv_heads
    turned = kv_heads // 2
    group = (place % kv_heads) ^ (part * turned)
    span = lax.axis_index("span")
    tile_count, slots = block_lists.shape[2], block_lists.shape[3]
    tiles = tile_count // 2
    rings = [[c * kv_heads + (j ^ (c * turned)) for j in range(kv_heads)] for c in range(2)]

    def turn(x):
        return lax.ppermute(x, "seq", [pair for a, b in zip(*rings) for pair in ((a, b), (b, a))])

    def shift(x, by):
        return lax.ppermute(x, "span", [(i, (i + by) % spans) for i in range(spans)])

    def swap(x):
        return lax.ppermute(x, "span", [(i, i ^ 1) for i in range(spans)])

    sent = pack(key_states, value_states)
    near = lax.all_to_all(sent, "seq", 0, 0, tiled=True, axis_index_groups=rings)
    q_send = jnp.transpose(queries[0].reshape(tok_rows, kv_heads, width), (1, 0, 2))
    q = lax.all_to_all(q_send, "seq", 0, 0, tiled=True, axis_index_groups=rings)
    q = q.reshape(kv_heads * tok_rows, width)

    other = turn(near)

    up_near = shift(near, 2)
    down_near = shift(near, -2)
    up_other = shift(other, 2)
    down_other = shift(other, -2)
    two_near = shift(up_near, 2)
    swap_near, swap_other = swap(near), swap(other)
    early = (q, up_near, down_near, swap_near, swap_other)
    q, up_near, down_near, swap_near, swap_other = lax.optimization_barrier(early)
    swap_up, swap_down = swap(up_near), swap(down_near)
    own = [own_attention(q, near, other, 0, 2)]
    between = (own[0], q, down_other, swap_up, swap_down)
    own[0], q, down_other, swap_up, swap_down = lax.optimization_barrier(between)
    two_other = shift(down_other, -2)
    own.append(own_attention(q, near, other, 1, 2))
    late = (own[1], two_near, two_other, up_other, down_other)
    own[1], two_near, two_other, up_other, down_other = lax.optimization_barrier(late)
    pieces = [near, other, swap_near, swap_other]
    pieces += [up_near, up_other, swap_up, swap(up_other)]
    pieces += [two_near, two_other, swap(two_near), swap(two_other)]
    pieces += [down_near, down_other, swap_down, swap(down_other)]
    ids = lax.dynamic_slice(block_lists, (0, group, part * tiles, 0), (1, 1, tiles, slots))[0, 0]
    ids = jnp.where(part == 0, ids, jnp.roll(ids, tiles // 2, axis=0))
    where = jnp.stack([span // 2, span % 2, part]).astype(jnp.int32)
    out = far_attention(ids.reshape(tiles * slots), where, q, own, pieces, tiles, slots)

    out = out.reshape(kv_heads, tok_rows, width)
    back = lax.all_to_all(out, "seq", 0, 0, tiled=True, axis_index_groups=rings)
    return jnp.transpose(back, (1, 0, 2)).reshape(1, tok_rows, model_width)


def solution(mesh):
    in_specs = (
        P("span", "seq", None),
        P("span", "seq", None),
        P("span", "seq", None),
        P("span", None, None, None),
    )
    out_specs = P("span", "seq", None)
    return jax.shard_map(
        on_device, mesh=mesh, in_specs=in_specs, out_specs=out_specs, check_vma=False
    )
```

time: 124 us -> 117 us (0.944)
  local copies, waits for them, and re-layouts: 8.33 us -> 5.09 us
  waiting for transfers between devices: 23.7 us -> 21 us
  Pallas kernels: 41.6 us -> 39.3 us
  starting transfers between devices: 23.9 us -> 25.3 us
    pallas_call x1, Pallas kernels: 19.2 us -> 14.8 us  [far_attention(): pl.pallas_call(functools.partial(far_kernel, heads, tiles, slots, len(own...]
    unnamed x15 -> x17, local copies, waits for them, and re-layouts: 3.85 us -> 0.99 us
    pallas_call x0 -> x1, Pallas kernels: none -> 2.05 us  [pack(): pl.pallas_call(pack_kernel, out_shape=jax.ShapeDtypeStruct((heads, rows,...]
  transfers between devices with their start and end apart: 17 -> 17, of which waited for: 10 -> 9; matrix products, arithmetic and copies ran while one was open for 2% -> 2% of each run, Pallas kernels for 18% -> 19%
where the time goes in v3:
time: 117 us; the launch traced here: 116 us
  Pallas kernels  39.3 us (34%)
  blocking collectives  25.5 us (22%)
  starting transfers between devices  25.3 us (22%)
  waiting for transfers between devices  21 us (18%)
  local copies, waits for them, and re-layouts  5.09 us (4%)
    all_to_all x1, blocking collectives, on_device(): back = lax.all_to_all(out, 'seq', 0, 0, tiled=True, axis_index_groups=rings)  25.5 us
    pallas_call x2, Pallas kernels, own_attention(): pl.pallas_call(functools.partial(own_kernel, heads), grid=(1,), out_shape...  22.4 us
    pallas_call x1, Pallas kernels, far_attention(): pl.pallas_call(functools.partial(far_kernel, heads, tiles, slots, len(own...  14.8 us
    ppermute x6, starting transfers between devices, shift(): lax.ppermute(x, 'span', [(i, (i + by) % spans) for i in range(spans)])  12.5 us
    ppermute x1, waiting for transfers between devices, turn(): lax.ppermute(x, 'seq', [pair for a, b in zip(*rings) for pair in ((a, b),...  8.2 us
    all_to_all x1, waiting for transfers between devices, on_device(): lax.all_to_all(sent, 'seq', 0, 0, tiled=True, axis_index_groups=rings)  7.8 us
    all_to_all x1, starting transfers between devices, on_device(): lax.all_to_all(sent, 'seq', 0, 0, tiled=True, axis_index_groups=rings)  5.48 us
    all_to_all x1, starting transfers between devices, on_device(): q = lax.all_to_all(q_send, 'seq', 0, 0, tiled=True, axis_index_groups=rings)  3.58 us
  transfers between devices with their start and end apart: 17, of which 9 were waited for; matrix products, arithmetic and copies ran while one was open for 2% of the time, Pallas kernels for 19%

profile of v3, /device:TPU:0, one launch (start us, length us, event | category | flops | bytes accessed | tf_op | source)
XLA Modules:
  0.0 116.4 jit_solution(14708039670156387081)
XLA Ops:
  0.0 0.0 copy-start
  0.0 0.0 copy-start.1
  0.0 2.0 %pack.1 = bf16[8,128,256]{2,1,0:T(8,128)(2,1)} custom-call(bf16[1,128,1024]{2,1,0:T(8,128)(2,1)} %k_ref.1, bf16[1,128,1024]{2,1,0:T(8,128)(2,1)} %v_ref.1), custom_call_target="tpu_custom_call" | custom-call | tf_op jit(solution)/shard_map/pack/pallas_call | solution.py:139
  2.1 5.5 %all-to-all-start.1 = ((bf16[8,128,256]{2,1,0:T(8,128)(2,1)}), bf16[8,128,256]{2,1,0:T(8,128)(2,1)S(1)}, u32[]{:S(2)}, u32[]{:S(2)}) async-start(bf16[8,128,256]{2,1,0:T(8,128)(2,1)} %pack.1), calls=%async_computation.1 | async-start | bytes 1048576 | tf_op jit(solution)/shard_map/all_to_all | solution.py:221
  7.5 0.0 copy-done.1
  7.5 0.3 copy.7
  7.9 1.4 %copy.9 = bf16[128,8,768]{2,0,1:T(8,128)(2,1)} copy(bf16[128,8,768]{2,1,0:T(8,128)(2,1)S(1)} %bitcast.17) | data formatting | bytes 3145728 | tf_op jit(solution)/shard_map/reshape;squeeze | solution.py:222
  9.3 7.8 %all-to-all-done.1.near_ref.rest_4_ = bf16[8,128,256]{2,1,0:T(8,128)(2,1)S(1)} async-done(((bf16[8,128,256]{2,1,0:T(8,128)(2,1)}), bf16[8,128,256]{2,1,0:T(8,128)(2,1)S(1)}, u32[]{:S(2)}, u32[]{:S(2)}) %all-to-all-start.1) | async-done | bytes 524320 | tf_op jit(solution)/shard_map/all_to_all | solution.py:221
  17.1 3.6 %all-to-all-start = ((bf16[8,128,768]{2,1,0:T(8,128)(2,1)}), bf16[8,128,768]{2,1,0:T(8,128)(2,1)S(1)}, u32[]{:S(2)}, u32[]{:S(2)}) async-start(bf16[8,128,768]{2,1,0:T(8,128)(2,1)} %bitcast.15), calls=%async_computation | async-start | bytes 3145728 | tf_op jit(solution)/shard_map/all_to_all | solution.py:223
  20.7 2.2 %collective-permute-start.3 = (bf16[8,128,256]{2,1,0:T(8,128)(2,1)S(1)}, bf16[8,128,256]{2,1,0:T(8,128)(2,1)S(1)}, u32[]{:S(2)}, u32[]{:S(2)}) collective-permute-start(bf16[8,128,256]{2,1,0:T(8,128)(2,1)S(1)} %all-to-all-done.1.near_ref.rest_4_), channel_id=1, source_target_pairs={{0,12},{12,0},{1,13},{13,1},{2,14},{14,2},{3,15},{15,3},{4,8},{8,4... | collective-permute-start | bytes 1572872 | tf_op jit(solution)/shard_map/ppermute | solution.py:212
  22.9 0.0 collective-permute-start.2
  22.9 1.9 %collective-permute-start = (bf16[8,128,256]{2,1,0:T(8,128)(2,1)S(1)}, bf16[8,128,256]{2,1,0:T(8,128)(2,1)}, u32[]{:S(2)}, u32[]{:S(2)}) collective-permute-start(bf16[8,128,256]{2,1,0:T(8,128)(2,1)S(1)} %all-to-all-done.1.near_ref.rest_4_), channel_id=1, source_target_pairs={{0,32},{16,48},{32,64},{48,80},{64,96},{80,112},{96,0},{112,16},{1... | collective-permute-start | bytes 1572872 | tf_op jit(solution)/shard_map/ppermute | solution.py:215
  24.8 2.1 %collective-permute-start.1 = (bf16[8,128,256]{2,1,0:T(8,128)(2,1)S(1)}, bf16[8,128,256]{2,1,0:T(8,128)(2,1)}, u32[]{:S(2)}, u32[]{:S(2)}) collective-permute-start(bf16[8,128,256]{2,1,0:T(8,128)(2,1)S(1)} %all-to-all-done.1.near_ref.rest_4_), channel_id=1, source_target_pairs={{0,96},{16,112},{32,0},{48,16},{64,32},{80,48},{96,64},{112,80},{1... | collective-permute-start | bytes 1572872 | tf_op jit(solution)/shard_map/ppermute | solution.py:215
  26.9 8.2 %collective-permute-done.3.other_ref.rest_5_ = bf16[8,128,256]{2,1,0:T(8,128)(2,1)S(1)} collective-permute-done((bf16[8,128,256]{2,1,0:T(8,128)(2,1)S(1)}, bf16[8,128,256]{2,1,0:T(8,128)(2,1)S(1)}, u32[]{:S(2)}, u32[]{:S(2)}) %collective-permute-start.3) | collective-permute-done | bytes 524320 | tf_op jit(solution)/shard_map/ppermute | solution.py:212
  35.1 0.0 collective-permute-start.4
  35.1 0.0 copy-done
  35.1 2.0 %collective-permute-start.10 = (bf16[8,128,256]{2,1,0:T(8,128)(2,1)S(1)}, bf16[8,128,256]{2,1,0:T(8,128)(2,1)}, u32[]{:S(2)}, u32[]{:S(2)}) collective-permute-start(bf16[8,128,256]{2,1,0:T(8,128)(2,1)S(1)} %collective-permute-done.3.other_ref.rest_5_), channel_id=1, source_target_pairs={{0,32},{16,48},{32,64},{48,80},{64,96},{80,112},{96,0},{112,16},{1... | collective-permute-start | bytes 1572872 | tf_op jit(solution)/shard_map/ppermute | solution.py:215
  37.1 0.0 collective-permute-done.2.rest_6_
  37.1 0.0 copy-start.3
  37.1 2.2 %collective-permute-start.5 = (bf16[8,128,256]{2,1,0:T(8,128)(2,1)S(1)}, bf16[8,128,256]{2,1,0:T(8,128)(2,1)}, u32[]{:S(2)}, u32[]{:S(2)}) collective-permute-start(bf16[8,128,256]{2,1,0:T(8,128)(2,1)S(1)} %collective-permute-done.3.other_ref.rest_5_), channel_id=1, source_target_pairs={{0,96},{16,112},{32,0},{48,16},{64,32},{80,48},{96,64},{112,80},{1... | collective-permute-start | bytes 1572872 | tf_op jit(solution)/shard_map/ppermute | solution.py:215
  39.4 0.3 collective-permute-done.rest_8_
  39.6 0.0 collective-permute-start.8
  39.6 0.0 collective-permute-done.1.rest_16_
  39.6 1.3 %all-to-all-done = bf16[8,128,768]{2,1,0:T(8,128)(2,1)S(1)} async-done(((bf16[8,128,768]{2,1,0:T(8,128)(2,1)}), bf16[8,128,768]{2,1,0:T(8,128)(2,1)S(1)}, u32[]{:S(2)}, u32[]{:S(2)}) %all-to-all-start) | async-done | bytes 1572896 | tf_op jit(solution)/shard_map/all_to_all | solution.py:223
  41.0 0.0 copy-start.2
  41.0 0.0 collective-permute-done.4.rest_7_
  41.0 0.0 collective-permute-start.6
  41.0 0.0 copy-done.3
  41.0 0.5 collective-permute-start.7
  41.5 0.6 copy-done.2
  42.1 11.2 %own_attention.2 = (f32[512,768]{1,0:T(8,128)}, f32[512,6]{1,0:T(8,128)S(1)}) custom-call(bf16[1024,768]{1,0:T(8,128)(2,1)} %bitcast.19, bf16[8,128,256]{2,1,0:T(8,128)(2,1)S(1)} %all-to-all-done.1.near_ref.rest_4_, bf16[8,128,256]{2,1,0:T(8,128)(2,1)S(1)} %collective-permute-done.3.other_ref.rest_5_), custom_call_target="tpu_custom_call" | custom-call | flops 6442450944 | bytes 3145728 | tf_op jit(solution)/shard_map/own_attention/pallas_call | solution.py:154
  53.3 0.0 collective-permute-done.5.rest_17_
  53.3 0.0 collective-permute-done.6.rest_10_
  53.3 0.0 copy-start.4
  53.3 0.0 collective-permute-done.7.rest_18_
  53.4 0.0 copy-start.5
  53.4 4.3 %collective-permute-start.9 = (bf16[8,128,256]{2,1,0:T(8,128)(2,1)}, bf16[8,128,256]{2,1,0:T(8,128)(2,1)S(1)}, u32[]{:S(2)}, u32[]{:S(2)}) collective-permute-start(bf16[8,128,256]{2,1,0:T(8,128)(2,1)} %collective-permute-done.5.rest_17_), channel_id=1, source_target_pairs={{0,96},{16,112},{32,0},{48,16},{64,32},{80,48},{96,64},{112,80},{1... | collective-permute-start | bytes 1572872 | tf_op jit(solution)/shard_map/ppermute | solution.py:215
  57.7 11.2 %own_attention.3 = (f32[512,768]{1,0:T(8,128)}, f32[512,6]{1,0:T(8,128)S(1)}) custom-call(bf16[1024,768]{1,0:T(8,128)(2,1)} %bitcast.20, bf16[8,128,256]{2,1,0:T(8,128)(2,1)S(1)} %all-to-all-done.1.near_ref.rest_4_, bf16[8,128,256]{2,1,0:T(8,128)(2,1)S(1)} %collective-permute-done.3.other_ref.rest_5_), custom_call_target="tpu_custom_call" | custom-call | flops 6442450944 | bytes 3145728 | tf_op jit(solution)/shard_map/own_attention/pallas_call | solution.py:154
  68.9 0.0 copy-done.4
  68.9 0.0 copy-done.5
  68.9 0.0 collective-permute-done.10.rest_9_
  68.9 0.0 collective-permute-done.8.rest_12_
  68.9 0.2 collective-permute-done.9.rest_13_
  69.1 0.0 copy-start.6
  69.1 0.0 collective-permute-start.11
  69.1 0.5 collective-permute-start.12
  69.6 0.0 collective-permute-start.13
  69.6 0.5 collective-permute-start.14
  70.1 0.1 squeeze.3
  70.2 0.1 concatenate.7
  70.3 0.1 pad_add_fusion.1.place_ref
  70.4 1.6 %collective-permute-done.11.rest_11_ = bf16[8,128,256]{2,1,0:T(8,128)(2,1)S(1)} collective-permute-done((bf16[8,128,256]{2,1,0:T(8,128)(2,1)}, bf16[8,128,256]{2,1,0:T(8,128)(2,1)S(1)}, u32[]{:S(2)}, u32[]{:S(2)}) %collective-permute-start.11) | collective-permute-done | bytes 524320 | tf_op jit(solution)/shard_map/ppermute | solution.py:218
  71.9 0.0 copy-start.7
  71.9 0.5 collective-permute-done.12.rest_14_
  72.5 0.9 collective-permute-done.13.rest_15_
  73.3 0.2 collective-permute-done.14.rest_19_
  73.6 0.0 copy-done.6
  73.6 0.0 copy-done.7
  73.6 14.8 %far_attention.1 = bf16[1024,768]{1,0:T(8,128)(2,1)} custom-call(s32[32]{0:T(128)S(1)} %broadcast_select_fusion.ids_ref, s32[3]{0:T(128)S(1)} %pad_add_fusion.1.place_ref, bf16[1024,768]{1,0:T(8,128)(2,1)} %bitcast.21, f32[512,768]{1,0:T(8,128)} %get-tuple-element.32.rest_0_, f32[512,6]{1,0:T(8,128)S(1)} %get-tuple-element.33.rest_1_, ...), custom_call_target="tpu_custom_call" | custom-call | flops 6442450944 | bytes 6291456 | tf_op jit(solution)/shard_map/far_attention/pallas_call | solution.py:179
  88.4 25.5 %all_to_all.15 = bf16[8,128,768]{2,1,0:T(8,128)(2,1)S(1)} all-to-all(bf16[8,128,768]{2,1,0:T(8,128)(2,1)} %bitcast.22), channel_id=1, replica_groups={{0,1,2,3,4,5,6,7},{12,13,14,15,8,9,10,11},{16,17,18,19,20,21,22,23},{28..., dimensions={0} | all-to-all | bytes 3145728 | tf_op jit(solution)/shard_map/all_to_all | solution.py:254
  113.9 0.9 copy.6
  114.8 1.6 %reshape.16 = bf16[1,128,6144]{2,1,0:T(8,128)(2,1)} reshape(bf16[128,8,768]{2,1,0:T(8,128)(2,1)S(1)} %copy.6) | data formatting | bytes 3145728 | tf_op jit(solution)/shard_map/reshape | solution.py:255
  (4 shorter events, 0.0 us)
Async XLA Ops:
  0.0 35.1 %copy-start = (s32[1,8,8,8]{3,2,1,0:T(8,128)S(1)}, s32[1,8,8,8]{3,2,1,0:T(8,128)}, u32[]{:S(2)}) copy-start(s32[1,8,8,8]{3,2,1,0:T(8,128)} %param.7) | copy-start | bytes 6148
  0.0 7.5 %copy-start.1 = (bf16[1,128,6144]{2,1,0:T(8,128)(2,1)S(1)}, bf16[1,128,6144]{2,1,0:T(8,128)(2,1)}, u32[]{:S(2)}) copy-start(bf16[1,128,6144]{2,1,0:T(8,128)(2,1)} %param.4) | copy-start | bytes 4718596
  2.1 15.1 %all-to-all-start.1 = ((bf16[8,128,256]{2,1,0:T(8,128)(2,1)}), bf16[8,128,256]{2,1,0:T(8,128)(2,1)S(1)}, u32[]{:S(2)}, u32[]{:S(2)}) async-start(bf16[8,128,256]{2,1,0:T(8,128)(2,1)} %pack.1), calls=%async_computation.1 | async-start | bytes 1048576 | tf_op jit(solution)/shard_map/all_to_all | solution.py:221
  17.1 23.8 %all-to-all-start = ((bf16[8,128,768]{2,1,0:T(8,128)(2,1)}), bf16[8,128,768]{2,1,0:T(8,128)(2,1)S(1)}, u32[]{:S(2)}, u32[]{:S(2)}) async-start(bf16[8,128,768]{2,1,0:T(8,128)(2,1)} %bitcast.15), calls=%async_computation | async-start | bytes 3145728 | tf_op jit(solution)/shard_map/all_to_all | solution.py:223
  20.7 14.4 %collective-permute-start.3 = (bf16[8,128,256]{2,1,0:T(8,128)(2,1)S(1)}, bf16[8,128,256]{2,1,0:T(8,128)(2,1)S(1)}, u32[]{:S(2)}, u32[]{:S(2)}) collective-permute-start(bf16[8,128,256]{2,1,0:T(8,128)(2,1)S(1)} %all-to-all-done.1.near_ref.rest_4_), channel_id=1, source_target_pairs={{0,12},{12,0},{1,13},{13,1},{2,14},{14,2},{3,15},{15,3},{4,8},{8,4... | collective-permute-start | bytes 1572872 | tf_op jit(solution)/shard_map/ppermute | solution.py:212
  22.9 14.3 %collective-permute-start.2 = (bf16[8,128,256]{2,1,0:T(8,128)(2,1)S(1)}, bf16[8,128,256]{2,1,0:T(8,128)(2,1)S(1)}, u32[]{:S(2)}, u32[]{:S(2)}) collective-permute-start(bf16[8,128,256]{2,1,0:T(8,128)(2,1)S(1)} %all-to-all-done.1.near_ref.rest_4_), channel_id=1, source_target_pairs={{0,16},{16,0},{32,48},{48,32},{64,80},{80,64},{96,112},{112,96},{1... | collective-permute-start | bytes 1572872 | tf_op jit(solution)/shard_map/ppermute | solution.py:218
  22.9 16.7 %collective-permute-start = (bf16[8,128,256]{2,1,0:T(8,128)(2,1)S(1)}, bf16[8,128,256]{2,1,0:T(8,128)(2,1)}, u32[]{:S(2)}, u32[]{:S(2)}) collective-permute-start(bf16[8,128,256]{2,1,0:T(8,128)(2,1)S(1)} %all-to-all-done.1.near_ref.rest_4_), channel_id=1, source_target_pairs={{0,32},{16,48},{32,64},{48,80},{64,96},{80,112},{96,0},{112,16},{1... | collective-permute-start | bytes 1572872 | tf_op jit(solution)/shard_map/ppermute | solution.py:215
  24.8 14.8 %collective-permute-start.1 = (bf16[8,128,256]{2,1,0:T(8,128)(2,1)S(1)}, bf16[8,128,256]{2,1,0:T(8,128)(2,1)}, u32[]{:S(2)}, u32[]{:S(2)}) collective-permute-start(bf16[8,128,256]{2,1,0:T(8,128)(2,1)S(1)} %all-to-all-done.1.near_ref.rest_4_), channel_id=1, source_target_pairs={{0,96},{16,112},{32,0},{48,16},{64,32},{80,48},{96,64},{112,80},{1... | collective-permute-start | bytes 1572872 | tf_op jit(solution)/shard_map/ppermute | solution.py:215
  35.1 5.8 %collective-permute-start.4 = (bf16[8,128,256]{2,1,0:T(8,128)(2,1)S(1)}, bf16[8,128,256]{2,1,0:T(8,128)(2,1)}, u32[]{:S(2)}, u32[]{:S(2)}) collective-permute-start(bf16[8,128,256]{2,1,0:T(8,128)(2,1)S(1)} %collective-permute-done.3.other_ref.rest_5_), channel_id=1, source_target_pairs={{0,16},{16,0},{32,48},{48,32},{64,80},{80,64},{96,112},{112,96},{1... | collective-permute-start | bytes 1572872 | tf_op jit(solution)/shard_map/ppermute | solution.py:218
  35.1 33.7 %collective-permute-start.10 = (bf16[8,128,256]{2,1,0:T(8,128)(2,1)S(1)}, bf16[8,128,256]{2,1,0:T(8,128)(2,1)}, u32[]{:S(2)}, u32[]{:S(2)}) collective-permute-start(bf16[8,128,256]{2,1,0:T(8,128)(2,1)S(1)} %collective-permute-done.3.other_ref.rest_5_), channel_id=1, source_target_pairs={{0,32},{16,48},{32,64},{48,80},{64,96},{80,112},{96,0},{112,16},{1... | collective-permute-start | bytes 1572872 | tf_op jit(solution)/shard_map/ppermute | solution.py:215
  37.1 3.8 %copy-start.3 = (bf16[8,128,256]{2,1,0:T(8,128)(2,1)}, bf16[8,128,256]{2,1,0:T(8,128)(2,1)S(1)}, u32[]{:S(2)}) copy-start(bf16[8,128,256]{2,1,0:T(8,128)(2,1)S(1)} %collective-permute-done.2.rest_6_) | copy-start | bytes 1572868
  37.1 16.2 %collective-permute-start.5 = (bf16[8,128,256]{2,1,0:T(8,128)(2,1)S(1)}, bf16[8,128,256]{2,1,0:T(8,128)(2,1)}, u32[]{:S(2)}, u32[]{:S(2)}) collective-permute-start(bf16[8,128,256]{2,1,0:T(8,128)(2,1)S(1)} %collective-permute-done.3.other_ref.rest_5_), channel_id=1, source_target_pairs={{0,96},{16,112},{32,0},{48,16},{64,32},{80,48},{96,64},{112,80},{1... | collective-permute-start | bytes 1572872 | tf_op jit(solution)/shard_map/ppermute | solution.py:215
  39.6 29.2 %collective-permute-start.8 = (bf16[8,128,256]{2,1,0:T(8,128)(2,1)}, bf16[8,128,256]{2,1,0:T(8,128)(2,1)}, u32[]{:S(2)}, u32[]{:S(2)}) collective-permute-start(bf16[8,128,256]{2,1,0:T(8,128)(2,1)} %collective-permute-done.rest_8_), channel_id=1, source_target_pairs={{0,32},{16,48},{32,64},{48,80},{64,96},{80,112},{96,0},{112,16},{1... | collective-permute-start | bytes 1572872 | tf_op jit(solution)/shard_map/ppermute | solution.py:215
  41.0 1.1 copy-start.2
  41.0 12.4 %collective-permute-start.6 = (bf16[8,128,256]{2,1,0:T(8,128)(2,1)}, bf16[8,128,256]{2,1,0:T(8,128)(2,1)S(1)}, u32[]{:S(2)}, u32[]{:S(2)}) collective-permute-start(bf16[8,128,256]{2,1,0:T(8,128)(2,1)} %collective-permute-done.rest_8_), channel_id=1, source_target_pairs={{0,16},{16,0},{32,48},{48,32},{64,80},{80,64},{96,112},{112,96},{1... | collective-permute-start | bytes 1572872 | tf_op jit(solution)/shard_map/ppermute | solution.py:218
  41.0 12.4 %collective-permute-start.7 = (bf16[8,128,256]{2,1,0:T(8,128)(2,1)}, bf16[8,128,256]{2,1,0:T(8,128)(2,1)S(1)}, u32[]{:S(2)}, u32[]{:S(2)}) collective-permute-start(bf16[8,128,256]{2,1,0:T(8,128)(2,1)} %collective-permute-done.1.rest_16_), channel_id=1, source_target_pairs={{0,16},{16,0},{32,48},{48,32},{64,80},{80,64},{96,112},{112,96},{1... | collective-permute-start | bytes 1572872 | tf_op jit(solution)/shard_map/ppermute | solution.py:218
  53.3 15.5 %copy-start.4 = (bf16[8,128,256]{2,1,0:T(8,128)(2,1)}, bf16[8,128,256]{2,1,0:T(8,128)(2,1)S(1)}, u32[]{:S(2)}) copy-start(bf16[8,128,256]{2,1,0:T(8,128)(2,1)S(1)} %collective-permute-done.6.rest_10_) | copy-start | bytes 1572868
  53.4 15.5 %copy-start.5 = (bf16[8,128,256]{2,1,0:T(8,128)(2,1)}, bf16[8,128,256]{2,1,0:T(8,128)(2,1)S(1)}, u32[]{:S(2)}) copy-start(bf16[8,128,256]{2,1,0:T(8,128)(2,1)S(1)} %collective-permute-done.7.rest_18_) | copy-start | bytes 1572868
  53.4 15.7 %collective-permute-start.9 = (bf16[8,128,256]{2,1,0:T(8,128)(2,1)}, bf16[8,128,256]{2,1,0:T(8,128)(2,1)S(1)}, u32[]{:S(2)}, u32[]{:S(2)}) collective-permute-start(bf16[8,128,256]{2,1,0:T(8,128)(2,1)} %collective-permute-done.5.rest_17_), channel_id=1, source_target_pairs={{0,96},{16,112},{32,0},{48,16},{64,32},{80,48},{96,64},{112,80},{1... | collective-permute-start | bytes 1572872 | tf_op jit(solution)/shard_map/ppermute | solution.py:215
  69.1 4.5 %copy-start.6 = (bf16[8,128,256]{2,1,0:T(8,128)(2,1)}, bf16[8,128,256]{2,1,0:T(8,128)(2,1)S(1)}, u32[]{:S(2)}) copy-start(bf16[8,128,256]{2,1,0:T(8,128)(2,1)S(1)} %collective-permute-done.9.rest_13_) | copy-start | bytes 1572868
  69.1 2.8 %collective-permute-start.11 = (bf16[8,128,256]{2,1,0:T(8,128)(2,1)}, bf16[8,128,256]{2,1,0:T(8,128)(2,1)S(1)}, u32[]{:S(2)}, u32[]{:S(2)}) collective-permute-start(bf16[8,128,256]{2,1,0:T(8,128)(2,1)} %collective-permute-done.10.rest_9_), channel_id=1, source_target_pairs={{0,16},{16,0},{32,48},{48,32},{64,80},{80,64},{96,112},{112,96},{1... | collective-permute-start | bytes 1572872 | tf_op jit(solution)/shard_map/ppermute | solution.py:218
  69.1 3.4 %collective-permute-start.12 = (bf16[8,128,256]{2,1,0:T(8,128)(2,1)}, bf16[8,128,256]{2,1,0:T(8,128)(2,1)}, u32[]{:S(2)}, u32[]{:S(2)}) collective-permute-start(bf16[8,128,256]{2,1,0:T(8,128)(2,1)} %collective-permute-done.8.rest_12_), channel_id=1, source_target_pairs={{0,16},{16,0},{32,48},{48,32},{64,80},{80,64},{96,112},{112,96},{1... | collective-permute-start | bytes 1572872 | tf_op jit(solution)/shard_map/ppermute | solution.py:218
  69.6 3.7 %collective-permute-start.13 = (bf16[8,128,256]{2,1,0:T(8,128)(2,1)S(1)}, bf16[8,128,256]{2,1,0:T(8,128)(2,1)}, u32[]{:S(2)}, u32[]{:S(2)}) collective-permute-start(bf16[8,128,256]{2,1,0:T(8,128)(2,1)S(1)} %collective-permute-done.9.rest_13_), channel_id=1, source_target_pairs={{0,16},{16,0},{32,48},{48,32},{64,80},{80,64},{96,112},{112,96},{1... | collective-permute-start | bytes 1572872 | tf_op jit(solution)/shard_map/ppermute | solution.py:218
  69.6 4.0 %collective-permute-start.14 = (bf16[8,128,256]{2,1,0:T(8,128)(2,1)}, bf16[8,128,256]{2,1,0:T(8,128)(2,1)}, u32[]{:S(2)}, u32[]{:S(2)}) collective-permute-start(bf16[8,128,256]{2,1,0:T(8,128)(2,1)} %collective-permute-done.5.rest_17_), channel_id=1, source_target_pairs={{0,16},{16,0},{32,48},{48,32},{64,80},{80,64},{96,112},{112,96},{1... | collective-permute-start | bytes 1572872 | tf_op jit(solution)/shard_map/ppermute | solution.py:218
  71.9 1.7 %copy-start.7 = (bf16[8,128,256]{2,1,0:T(8,128)(2,1)}, bf16[8,128,256]{2,1,0:T(8,128)(2,1)S(1)}, u32[]{:S(2)}) copy-start(bf16[8,128,256]{2,1,0:T(8,128)(2,1)S(1)} %collective-permute-done.11.rest_11_) | copy-start | bytes 1572868

commit v4 on v3

v4 whole, which is shorter than its diff:
```python
import functools

import jax
import jax.numpy as jnp
from jax import lax
from jax.experimental import pallas as pl
from jax.experimental.pallas import tpu as pltpu
from jax.sharding import PartitionSpec as P

DH = 128
QT = 256
BK = 128
LOG2E = 1.4426950408889634
OWN_VMEM = 16 * 2**20
OWN_SLOTS = 64
FAR_VMEM = 16 * 2**20


def scaled_query(query_rows):
    scaled = query_rows.astype(jnp.float32) * (LOG2E * DH**-0.5)
    high = scaled.astype(jnp.bfloat16)
    low = (scaled - high.astype(jnp.float32)).astype(jnp.bfloat16)
    return jnp.concatenate([high, low], axis=1)


def scores_of(query_pair, keys_twice):
    return lax.dot_general(
        query_pair, keys_twice, (((1,), (1,)), ((), ())), preferred_element_type=jnp.float32
    )


def pack_kernel(k_ref, v_ref, out_ref):
    for head in range(out_ref.shape[0]):
        columns = slice(head * DH, (head + 1) * DH)
        out_ref[head, :, :DH] = k_ref[0, :, columns]
        out_ref[head, :, DH:] = v_ref[0, :, columns]


def own_kernel(heads, steps, place_ref, q_ref, kv_ref, *rest):
    own_ref, keys, values, held, sent = rest[-5:]
    wide = heads * DH
    blocks = kv_ref.shape[0]
    for n in range(blocks):
        rows = slice(n * BK, (n + 1) * BK)
        block = kv_ref[n, :, :DH]
        keys[rows, :DH] = block
        keys[rows, DH:] = block
        values[rows, :DH] = kv_ref[n, :, DH:]
    values[:, DH:] = jnp.ones((blocks * BK, DH), jnp.bfloat16)

    def tile(n, step):
        tile_at = pl.ds(pl.multiple_of(((place_ref[3] >> 1) ^ step) * QT, QT), QT)
        for head in range(heads):
            columns = slice(head * DH, (head + 1) * DH)
            scores = scores_of(scaled_query(q_ref[tile_at, columns]), keys[...])
            top = jnp.max(scores, axis=1, keepdims=True)
            weights = jnp.exp2(scores - top).astype(jnp.bfloat16)
            sums = jnp.dot(weights, values[...], preferred_element_type=jnp.float32)
            total = sums[:, DH:]
            held[n, :, columns] = sums[:, :DH] / total
            held[n, :, wide + head : wide + head + 1] = (top + jnp.log2(total))[:, :1]
        pltpu.make_async_copy(held.at[n], own_ref.at[n], sent.at[n]).start()

    for n, step in enumerate(steps):
        tile(n, step)
    for n in range(len(steps)):
        pltpu.make_async_copy(held.at[n], own_ref.at[n], sent.at[n]).wait()


def far_kernel(heads, steps, slots, ids_ref, place_ref, q_ref, *rest):
    outs = len(steps) * 2
    own_ref, rest = rest[0], rest[1:]
    pieces, out_refs, (far, held, ready, here) = rest[: -4 - outs], rest[-4 - outs : -4], rest[-4:]
    wide = heads * DH
    for n, step in enumerate(steps):
        pltpu.make_async_copy(own_ref.at[step], held.at[n], here.at[n]).start()
    half_blocks = pieces[0].shape[0] // 2
    bits = half_blocks.bit_length() - 1
    plane, core, part, place = [place_ref[n] for n in range(4)]
    tiles = [(place >> 1) ^ step for step in steps]

    def fetch(source, block, n, j):
        to = pl.ds(pl.multiple_of(j * BK, BK), BK)
        pltpu.make_async_copy(
            source.at[block], far.at[n, to, pl.ds(DH, 2 * DH)], ready.at[n]
        ).start()

    def fetch_from(low, high, at, block, n, j):
        if high - low == 1:
            fetch(pieces[low], block, n, j)
            return
        middle = (low + high) // 2
        lax.cond(
            at < middle,
            lambda: fetch_from(low, middle, at, block, n, j),
            lambda: fetch_from(middle, high, at, block, n, j),
        )

    for n, tile in enumerate(tiles):

        def slot(j, carry):
            listed = ids_ref[tile * slots + j]
            number = jnp.maximum(listed, 0)
            span, half = number >> (bits + 1), (number >> bits) & 1
            back = plane - (span >> 1)
            sibling, other = (span & 1) ^ core, half ^ part
            block = (number & (half_blocks - 1)) ^ (half * (half_blocks // 2))
            apart = back == 2
            at = back * 2 + sibling + jnp.where(apart, sibling + other, 0) + 2 * (back >> 1) * (back & 1)
            block = jnp.where(apart, block, block + other * half_blocks)
            at, block = jnp.where(listed >= 0, at, 0), jnp.where(listed >= 0, block, 0)
            fetch_from(0, len(pieces), at, block, n, j)
            return carry

        lax.fori_loop(0, slots, slot, 0)

    for n, tile in enumerate(tiles):
        landed = far.at[n, :, pl.ds(DH, 2 * DH)]
        pltpu.make_async_copy(landed, landed, ready.at[n]).wait()
        far[n, :, :DH] = far[n, :, DH : 2 * DH]
        far[n, :, 3 * DH :] = jnp.ones((slots * BK, DH), jnp.bfloat16)
        for j in range(slots):

            @pl.when(ids_ref[tile * slots + j] < 0)
            def _():
                far[n, j * BK : (j + 1) * BK, 2 * DH :] = jnp.zeros((BK, 2 * DH), jnp.bfloat16)

        at = pl.ds(pl.multiple_of(tile * QT, QT), QT)
        pltpu.make_async_copy(own_ref.at[0], held.at[n], here.at[n]).wait()
        columns = [slice(head * DH, (head + 1) * DH) for head in range(heads)]
        keys, values = far[n, :, : 2 * DH], far[n, :, 2 * DH :]
        scores = [scores_of(scaled_query(q_ref[at, column]), keys) for column in columns]
        own_size = [held[n, :, wide + head : wide + head + 1] for head in range(heads)]
        tops = [
            jnp.maximum(jnp.max(score, axis=1, keepdims=True), size)
            for score, size in zip(scores, own_size)
        ]
        weights = [jnp.exp2(score - top).astype(jnp.bfloat16) for score, top in zip(scores, tops)]
        sums = [jnp.dot(w, values, preferred_element_type=jnp.float32) for w in weights]
        for head, column in enumerate(columns):
            share = jnp.exp2(own_size[head] - tops[head])
            total = share + sums[head][:, DH:]
            result = (held[n, :, column] * share + sums[head][:, :DH]) / total
            upper, lower = result[: QT // 2], result[QT // 2 :]
            odd = (place & 1) == 1
            out_refs[2 * n][:, column] = jnp.where(odd, lower, upper).astype(jnp.bfloat16)
            out_refs[2 * n + 1][:, column] = jnp.where(odd, upper, lower).astype(jnp.bfloat16)


def unpack_kernel(place_ref, *refs):
    width = refs[0].shape[1]
    for step, ref in enumerate(refs[:-1]):
        at = pl.multiple_of((place_ref[3] ^ step) * width, width)
        refs[-1][0, :, pl.ds(at, width)] = ref[...]


def pack(key_states, value_states):
    rows, heads = key_states.shape[1], key_states.shape[2] // DH
    whole = pl.BlockSpec(memory_space=pltpu.VMEM)
    return pl.pallas_call(
        pack_kernel,
        out_shape=jax.ShapeDtypeStruct((heads, rows, 2 * DH), key_states.dtype),
        in_specs=[whole] * 2,
        out_specs=whole,
        name="pack",
    )(key_states, value_states)


def unpack(place, parts):
    rows, width = parts[0].shape
    whole = pl.BlockSpec(memory_space=pltpu.VMEM)
    return pl.pallas_call(
        unpack_kernel,
        out_shape=jax.ShapeDtypeStruct((1, rows, width * len(parts)), parts[0].dtype),
        in_specs=[pl.BlockSpec(memory_space=pltpu.SMEM)] + [whole] * len(parts),
        out_specs=whole,
        name="unpack",
    )(place, *parts)


def own_attention(place, q, kv, steps, after):
    tiles = len(steps)
    tokens, width = tiles * QT, q.shape[1]
    heads = width // DH
    keys = kv.shape[0] * BK
    whole = pl.BlockSpec(memory_space=pltpu.VMEM)
    scores = tokens * heads * keys
    return pl.pallas_call(
        functools.partial(own_kernel, heads, steps),
        out_shape=jax.ShapeDtypeStruct((OWN_SLOTS, QT, width + DH), jnp.float32),
        in_specs=[pl.BlockSpec(memory_space=pltpu.SMEM)]
        + [whole] * 2
        + [pl.BlockSpec(memory_space=pl.ANY)] * len(after),
        out_specs=pl.BlockSpec(memory_space=pl.ANY),
        scratch_shapes=[pltpu.VMEM((keys, 2 * DH), jnp.bfloat16)] * 2
        + [pltpu.VMEM((tiles, QT, width + DH), jnp.float32), pltpu.SemaphoreType.DMA((tiles,))],
        cost_estimate=pl.CostEstimate(
            flops=8 * scores * DH, bytes_accessed=8 * tokens * width, transcendentals=scores
        ),
        compiler_params=pltpu.CompilerParams(vmem_limit_bytes=OWN_VMEM),
        name="own_attention",
    )(place, q, kv, *after)


def far_attention(ids, place, q, own, pieces, steps, slots):
    width = q.shape[1]
    heads = width // DH
    whole = pl.BlockSpec(memory_space=pltpu.VMEM)
    scalars = pl.BlockSpec(memory_space=pltpu.SMEM)
    anywhere = pl.BlockSpec(memory_space=pl.ANY)
    scores = len(steps) * QT * heads * slots * BK
    return pl.pallas_call(
        functools.partial(far_kernel, heads, steps, slots),
        out_shape=[jax.ShapeDtypeStruct((QT // 2, width), jnp.bfloat16)] * (2 * len(steps)),
        in_specs=[scalars] * 2
        + [whole]
        + [anywhere] * (1 + len(pieces)),
        out_specs=[whole] * (2 * len(steps)),
        scratch_shapes=[
            pltpu.VMEM((len(steps), slots * BK, 4 * DH), jnp.bfloat16),
            pltpu.VMEM((len(steps), QT, width + DH), jnp.float32),
            pltpu.SemaphoreType.DMA((len(steps),)),
            pltpu.SemaphoreType.DMA((len(steps),)),
        ],
        cost_estimate=pl.CostEstimate(
            flops=8 * scores * DH, bytes_accessed=8 * q.size, transcendentals=scores
        ),
        compiler_params=pltpu.CompilerParams(vmem_limit_bytes=FAR_VMEM),
        name="far_attention",
    )(ids, place, q, own, *pieces)


def on_device(queries, key_states, value_states, block_lists):
    tok_rows = queries.shape[1]
    model_width = queries.shape[2]
    kv_heads = key_states.shape[2] // DH
    spans = lax.axis_size("span")
    width = model_width // kv_heads
    place = lax.axis_index("seq")
    part = place // kv_heads
    turned = kv_heads // 2
    group = (place % kv_heads) ^ (part * turned)
    span = lax.axis_index("span")
    tile_count, slots = block_lists.shape[2], block_lists.shape[3]
    tiles = tile_count // 2
    rings = [[c * kv_heads + (j ^ (c * turned)) for j in range(kv_heads)] for c in range(2)]

    def turn(x):
        return lax.ppermute(x, "seq", [pair for a, b in zip(*rings) for pair in ((a, b), (b, a))])

    def trade(x, step):
        pairs = [(ring[j], ring[j ^ step]) for ring in rings for j in range(kv_heads)]
        return lax.ppermute(x, "seq", pairs)

    def shift(x, by):
        return lax.ppermute(x, "span", [(i, (i + by) % spans) for i in range(spans)])

    def swap(x):
        return lax.ppermute(x, "span", [(i, i ^ 1) for i in range(spans)])

    where = jnp.stack([span // 2, span % 2, part, group]).astype(jnp.int32)
    sent = pack(key_states, value_states)
    near = lax.all_to_all(sent, "seq", 0, 0, tiled=True, axis_index_groups=rings)
    q_send = jnp.transpose(queries[0].reshape(tok_rows, kv_heads, width), (1, 0, 2))
    q = lax.all_to_all(q_send, "seq", 0, 0, tiled=True, axis_index_groups=rings)
    q = q.reshape(kv_heads * tok_rows, width)

    other = turn(near)
    two_near = shift(near, 4)
    kv = jnp.concatenate([near, other], axis=0)
    up, down = shift(kv, 2), shift(kv, -2)
    two_other = turn(two_near)
    swap_kv, swap_two = swap(kv), swap(two_near)
    own = own_attention(where, q, kv, range(tiles), [])
    own, up, down, two_other = lax.optimization_barrier((own, up, down, two_other))
    pieces = [kv, swap_kv, up, swap(up), two_near, two_other, swap_two, swap(two_other)]
    pieces += [down, swap(down)]
    ids = lax.dynamic_slice(block_lists, (0, group, part * tiles, 0), (1, 1, tiles, slots))[0, 0]
    ids = jnp.where(part == 0, ids, jnp.roll(ids, tiles // 2, axis=0))
    ids = ids.reshape(tiles * slots)
    parts = [None] * kv_heads
    for steps in ((2, 1), (3, 0)):
        results = far_attention(ids, where, q, own, pieces, steps, slots)
        for n, step in enumerate(steps):
            parts[2 * step] = results[2 * n]
            parts[2 * step + 1] = results[2 * n + 1]
        for step in [s for t in steps for s in (2 * t, 2 * t + 1) if s]:
            parts[step] = trade(parts[step], step)
    return unpack(where, parts)


def solution(mesh):
    in_specs = (
        P("span", "seq", None),
        P("span", "seq", None),
        P("span", "seq", None),
        P("span", None, None, None),
    )
    out_specs = P("span", "seq", None)
    return jax.shard_map(
        on_device, mesh=mesh, in_specs=in_specs, out_specs=out_specs, check_vma=False
    )
```

time: 117 us -> 108 us (0.923)
  blocking collectives: 25.5 us -> 0 us
  waiting for transfers between devices: 21 us -> 31.3 us
  starting transfers between devices: 25.3 us -> 34 us
  Pallas kernels: 39.3 us -> 34.7 us
  local copies, waits for them, and re-layouts: 5.09 us -> 6.84 us
    all_to_all x1 -> x0, blocking collectives: 25.5 us -> none  [on_device(): back = lax.all_to_all(out, 'seq', 0, 0, tiled=True, axis_index_groups=rings)]
    ppermute x0 -> x7, starting transfers between devices: none -> 11.5 us  [trade(): return lax.ppermute(x, 'seq', pairs)]
    ppermute x0 -> x7, waiting for transfers between devices: none -> 9.63 us  [trade(): return lax.ppermute(x, 'seq', pairs)]
    pallas_call x3 -> x4, Pallas kernels: 37.3 us -> 32.7 us  [the longest x1 16.8 us: own_attention(): pl.pallas_call(functools.partial(own_kernel, heads, steps), out_shape=jax...]
    ppermute x6 -> x3, starting transfers between devices: 12.5 us -> 8.07 us  [shift(): lax.ppermute(x, 'span', [(i, (i + by) % spans) for i in range(spans)])]
    unnamed x17 -> x24, local copies, waits for them, and re-layouts: 0.99 us -> 4.15 us
    ppermute x6 -> x3, waiting for transfers between devices: 0.48 us -> 2.83 us  [shift(): lax.ppermute(x, 'span', [(i, (i + by) % spans) for i in range(spans)])]
    ppermute x1 -> x2, starting transfers between devices: 2.18 us -> 4.27 us  [turn(): lax.ppermute(x, 'seq', [pair for a, b in zip(*rings) for pair in ((a, b),...]
  transfers between devices with their start and end apart: 17 -> 19, of which waited for: 9 -> 8; matrix products, arithmetic and copies ran while one was open for 2% -> 5% of each run, Pallas kernels for 19% -> 22%
where the time goes in v4:
time: 108 us; the launch traced here: 107 us
  Pallas kernels  34.7 us (32%)
  starting transfers between devices  34 us (31%)
  waiting for transfers between devices  31.3 us (29%)
  local copies, waits for them, and re-layouts  6.84 us (6%)
    pallas_call x1, Pallas kernels, own_attention(): pl.pallas_call(functools.partial(own_kernel, heads, steps), out_shape=jax...  16.8 us
    pallas_call x2, Pallas kernels, far_attention(): pl.pallas_call(functools.partial(far_kernel, heads, steps, slots), out_sh...  13.2 us
    ppermute x7, starting transfers between devices, trade(): return lax.ppermute(x, 'seq', pairs)  11.5 us
    ppermute x7, waiting for transfers between devices, trade(): return lax.ppermute(x, 'seq', pairs)  9.63 us
    ppermute x3, starting transfers between devices, shift(): lax.ppermute(x, 'span', [(i, (i + by) % spans) for i in range(spans)])  8.07 us
    ppermute x2, waiting for transfers between devices, turn(): lax.ppermute(x, 'seq', [pair for a, b in zip(*rings) for pair in ((a, b),...  7.53 us
    all_to_all x1, waiting for transfers between devices, on_device(): lax.all_to_all(sent, 'seq', 0, 0, tiled=True, axis_index_groups=rings)  6.51 us
    all_to_all x1, starting transfers between devices, on_device(): lax.all_to_all(sent, 'seq', 0, 0, tiled=True, axis_index_groups=rings)  5.48 us
  transfers between devices with their start and end apart: 19, of which 8 were waited for; matrix products, arithmetic and copies ran while one was open for 5% of the time, Pallas kernels for 22%

profile of v4, /device:TPU:0, one launch (start us, length us, event | category | flops | bytes accessed | tf_op | source)
XLA Modules:
  0.0 107.0 jit_solution(16296683628896333391)
XLA Ops:
  0.0 0.0 copy-start
  0.0 1.9 %pack.1 = bf16[8,128,256]{2,1,0:T(8,128)(2,1)} custom-call(bf16[1,128,1024]{2,1,0:T(8,128)(2,1)} %k_ref.1, bf16[1,128,1024]{2,1,0:T(8,128)(2,1)} %v_ref.1), custom_call_target="tpu_custom_call" | custom-call | tf_op jit(solution)/shard_map/pack/pallas_call | solution.py:160
  1.9 5.5 %all-to-all-start.1 = ((bf16[8,128,256]{2,1,0:T(8,128)(2,1)}), bf16[8,128,256]{2,1,0:T(8,128)(2,1)}, u32[]{:S(2)}, u32[]{:S(2)}) async-start(bf16[8,128,256]{2,1,0:T(8,128)(2,1)} %pack.1), calls=%async_computation.1 | async-start | bytes 1048576 | tf_op jit(solution)/shard_map/all_to_all | solution.py:263
  7.4 1.7 %copy.6 = bf16[16,8,8,768]{3,2,1,0:T(8,128)(2,1)S(1)} copy(bf16[16,8,8,768]{3,1,2,0:T(8,128)(2,1)} %bitcast.19) | data formatting | bytes 3145728
  9.2 1.4 %copy.8 = bf16[128,8,768]{2,0,1:T(8,128)(2,1)} copy(bf16[128,8,768]{2,1,0:T(8,128)(2,1)S(1)} %bitcast.18) | data formatting | bytes 3145728 | tf_op jit(solution)/shard_map/reshape;squeeze | solution.py:264
  10.6 6.5 %all-to-all-done.1 = bf16[8,128,256]{2,1,0:T(8,128)(2,1)} async-done(((bf16[8,128,256]{2,1,0:T(8,128)(2,1)}), bf16[8,128,256]{2,1,0:T(8,128)(2,1)}, u32[]{:S(2)}, u32[]{:S(2)}) %all-to-all-start.1) | async-done | bytes 524320 | tf_op jit(solution)/shard_map/all_to_all | solution.py:263
  17.1 3.6 %all-to-all-start = ((bf16[8,128,768]{2,1,0:T(8,128)(2,1)}), bf16[8,128,768]{2,1,0:T(8,128)(2,1)S(1)}, u32[]{:S(2)}, u32[]{:S(2)}) async-start(bf16[8,128,768]{2,1,0:T(8,128)(2,1)} %bitcast.14), calls=%async_computation | async-start | bytes 3145728 | tf_op jit(solution)/shard_map/all_to_all | solution.py:265
  20.7 2.2 %collective-permute-start = (bf16[8,128,256]{2,1,0:T(8,128)(2,1)}, bf16[8,128,256]{2,1,0:T(8,128)(2,1)}, u32[]{:S(2)}, u32[]{:S(2)}) collective-permute-start(bf16[8,128,256]{2,1,0:T(8,128)(2,1)} %all-to-all-done.1), channel_id=1, source_target_pairs={{0,12},{12,0},{1,13},{13,1},{2,14},{14,2},{3,15},{15,3},{4,8},{8,4... | collective-permute-start | bytes 1572872 | tf_op jit(solution)/shard_map/ppermute | solution.py:249
  22.9 3.9 %collective-permute-start.3 = (bf16[8,128,256]{2,1,0:T(8,128)(2,1)}, bf16[8,128,256]{2,1,0:T(8,128)(2,1)S(1)}, u32[]{:S(2)}, u32[]{:S(2)}) collective-permute-start(bf16[8,128,256]{2,1,0:T(8,128)(2,1)} %all-to-all-done.1), channel_id=1, source_target_pairs={{0,64},{16,80},{32,96},{48,112},{64,0},{80,16},{96,32},{112,48},{1... | collective-permute-start | bytes 1572872 | tf_op jit(solution)/shard_map/ppermute | solution.py:256
  26.7 0.1 pad_add_fusion.1.place_ref
  26.8 1.1 %constant_dynamic-update-slice_fusion.1 = bf16[16,128,256]{2,1,0:T(8,128)(2,1)S(1)} fusion(bf16[8,128,256]{2,1,0:T(8,128)(2,1)} %all-to-all-done.1), kind=kLoop, calls=%fused_computation.2 | loop fusion | bytes 1048576
  27.9 7.5 %collective-permute-done = bf16[8,128,256]{2,1,0:T(8,128)(2,1)} collective-permute-done((bf16[8,128,256]{2,1,0:T(8,128)(2,1)}, bf16[8,128,256]{2,1,0:T(8,128)(2,1)}, u32[]{:S(2)}, u32[]{:S(2)}) %collective-permute-start) | collective-permute-done | bytes 524320 | tf_op jit(solution)/shard_map/ppermute | solution.py:249
  35.4 1.1 %constant_dynamic-update-slice_fusion.kv_ref.rest_1_ = bf16[16,128,256]{2,1,0:T(8,128)(2,1)S(1)} fusion(bf16[16,128,256]{2,1,0:T(8,128)(2,1)S(1)} %constant_dynamic-update-slice_fusion.1, bf16[8,128,256]{2,1,0:T(8,128)(2,1)} %collective-permute-done), kind=kLoop, calls=%fused_computation.1 | loop fusion | bytes 1048576 | tf_op jit(solution)/shard_map/concatenate | solution.py:270
  36.5 2.0 %collective-permute-start.1 = (bf16[16,128,256]{2,1,0:T(8,128)(2,1)S(1)}, bf16[16,128,256]{2,1,0:T(8,128)(2,1)}, u32[]{:S(2)}, u32[]{:S(2)}) collective-permute-start(bf16[16,128,256]{2,1,0:T(8,128)(2,1)S(1)} %constant_dynamic-update-slice_fusion.kv_ref.rest_1_), channel_id=1, source_target_pairs={{0,32},{16,48},{32,64},{48,80},{64,96},{80,112},{96,0},{112,16},{1... | collective-permute-start | bytes 3145736 | tf_op jit(solution)/shard_map/ppermute | solution.py:256
  38.5 2.2 %collective-permute-start.2 = (bf16[16,128,256]{2,1,0:T(8,128)(2,1)S(1)}, bf16[16,128,256]{2,1,0:T(8,128)(2,1)}, u32[]{:S(2)}, u32[]{:S(2)}) collective-permute-start(bf16[16,128,256]{2,1,0:T(8,128)(2,1)S(1)} %constant_dynamic-update-slice_fusion.kv_ref.rest_1_), channel_id=1, source_target_pairs={{0,96},{16,112},{32,0},{48,16},{64,32},{80,48},{96,64},{112,80},{1... | collective-permute-start | bytes 3145736 | tf_op jit(solution)/shard_map/ppermute | solution.py:256
  40.7 0.0 collective-permute-start.5
  40.7 0.0 collective-permute-done.3.rest_5_
  40.7 2.1 %collective-permute-start.4 = (bf16[8,128,256]{2,1,0:T(8,128)(2,1)S(1)}, bf16[8,128,256]{2,1,0:T(8,128)(2,1)}, u32[]{:S(2)}, u32[]{:S(2)}) collective-permute-start(bf16[8,128,256]{2,1,0:T(8,128)(2,1)S(1)} %collective-permute-done.3.rest_5_), channel_id=1, source_target_pairs={{0,12},{12,0},{1,13},{13,1},{2,14},{14,2},{3,15},{15,3},{4,8},{8,4... | collective-permute-start | bytes 1572872 | tf_op jit(solution)/shard_map/ppermute | solution.py:249
  42.8 0.0 all-to-all-done
  42.8 16.8 %own_attention.1.rest_0_ = f32[64,256,896]{2,1,0:T(8,128)} custom-call(s32[4]{0:T(128)S(1)} %pad_add_fusion.1.place_ref, bf16[1024,768]{1,0:T(8,128)(2,1)S(1)} %bitcast.15, bf16[16,128,256]{2,1,0:T(8,128)(2,1)S(1)} %constant_dynamic-update-slice_fusion.kv_ref.rest_1_), custom_call_target="tpu_custom_call" | custom-call | flops 12884901888 | bytes 6291456 | tf_op jit(solution)/shard_map/own_attention/pallas_call | solution.py:188
  59.6 0.0 collective-permute-done.4.rest_6_
  59.6 2.8 %collective-permute-done.1.rest_3_ = bf16[16,128,256]{2,1,0:T(8,128)(2,1)} collective-permute-done((bf16[16,128,256]{2,1,0:T(8,128)(2,1)S(1)}, bf16[16,128,256]{2,1,0:T(8,128)(2,1)}, u32[]{:S(2)}, u32[]{:S(2)}) %collective-permute-start.1) | collective-permute-done | bytes 1048608 | tf_op jit(solution)/shard_map/ppermute | solution.py:256
  62.4 0.0 collective-permute-done.2.rest_9_
  62.4 0.0 collective-permute-start.6
  62.4 0.5 collective-permute-start.9
  62.9 0.0 copy-done
  63.0 0.1 squeeze.3
  63.0 0.0 collective-permute-start.7
  63.1 0.5 collective-permute-start.8
  63.6 0.1 concatenate.10
  63.7 3.1 %collective-permute-done.7.rest_7_ = bf16[8,128,256]{2,1,0:T(8,128)(2,1)} collective-permute-done((bf16[8,128,256]{2,1,0:T(8,128)(2,1)S(1)}, bf16[8,128,256]{2,1,0:T(8,128)(2,1)}, u32[]{:S(2)}, u32[]{:S(2)}) %collective-permute-start.7) | collective-permute-done | bytes 524320 | tf_op jit(solution)/shard_map/ppermute | solution.py:259
  66.7 0.0 collective-permute-done.5.rest_2_
  66.7 1.7 %collective-permute-done.8.rest_8_ = bf16[8,128,256]{2,1,0:T(8,128)(2,1)} collective-permute-done((bf16[8,128,256]{2,1,0:T(8,128)(2,1)}, bf16[8,128,256]{2,1,0:T(8,128)(2,1)}, u32[]{:S(2)}, u32[]{:S(2)}) %collective-permute-start.8) | collective-permute-done | bytes 524320 | tf_op jit(solution)/shard_map/ppermute | solution.py:259
  68.4 0.0 collective-permute-done.6.rest_4_
  68.4 0.0 collective-permute-done.9.rest_10_
  68.4 6.6 %far_attention.3 = (bf16[128,768]{1,0:T(8,128)(2,1)S(1)}, bf16[128,768]{1,0:T(8,128)(2,1)S(1)}, bf16[128,768]{1,0:T(8,128)(2,1)S(1)}, bf16[128,768]{1,0:T(8,128)(2,1)S(1)}) custom-call(s32[32]{0:T(128)S(1)} %broadcast_select_fusion.ids_ref, s32[4]{0:T(128)S(1)} %pad_add_fusion.1.place_ref, bf16[1024,768]{1,0:T(8,128)(2,1)S(1)} %bitcast.16, ...), custom_call_target="tpu_custom_call" | custom-call | flops 3221225472 | bytes 6291456 | tf_op jit(solution)/shard_map/far_attention/pallas_call | solution.py:212
  75.0 3.2 %collective-permute-start.11 = (bf16[128,768]{1,0:T(8,128)(2,1)S(1)}, bf16[128,768]{1,0:T(8,128)(2,1)S(1)}, u32[]{:S(2)}, u32[]{:S(2)}) collective-permute-start(bf16[128,768]{1,0:T(8,128)(2,1)S(1)} %get-tuple-element.23), channel_id=1, source_target_pairs={{0,2},{1,3},{2,0},{3,1},{4,6},{5,7},{6,4},{7,5},{12,14},{13,15},{1... | collective-permute-start | bytes 589832 | tf_op jit(solution)/shard_map/ppermute | solution.py:253
  78.2 1.2 %collective-permute-start.12 = (bf16[128,768]{1,0:T(8,128)(2,1)S(1)}, bf16[128,768]{1,0:T(8,128)(2,1)S(1)}, u32[]{:S(2)}, u32[]{:S(2)}) collective-permute-start(bf16[128,768]{1,0:T(8,128)(2,1)S(1)} %get-tuple-element.24), channel_id=1, source_target_pairs={{0,3},{1,2},{2,1},{3,0},{4,7},{5,6},{6,5},{7,4},{12,15},{13,14},{1... | collective-permute-start | bytes 589832 | tf_op jit(solution)/shard_map/ppermute | solution.py:253
  79.4 0.2 collective-permute-start.13
  79.6 0.6 collective-permute-start.14
  80.2 0.0 copy-done.3
  80.3 6.7 %far_attention.2 = (bf16[128,768]{1,0:T(8,128)(2,1)S(1)}, bf16[128,768]{1,0:T(8,128)(2,1)S(1)}, bf16[128,768]{1,0:T(8,128)(2,1)S(1)}, bf16[128,768]{1,0:T(8,128)(2,1)S(1)}) custom-call(s32[32]{0:T(128)S(1)} %broadcast_select_fusion.ids_ref, s32[4]{0:T(128)S(1)} %pad_add_fusion.1.place_ref, bf16[1024,768]{1,0:T(8,128)(2,1)S(1)} %bitcast.17, ...), custom_call_target="tpu_custom_call" | custom-call | flops 3221225472 | bytes 6291456 | tf_op jit(solution)/shard_map/far_attention/pallas_call | solution.py:212
  86.9 0.0 copy-start.2
  87.0 0.7 copy-done.2
  87.6 2.6 %collective-permute-start.10 = (bf16[128,768]{1,0:T(8,128)(2,1)S(1)}, bf16[128,768]{1,0:T(8,128)(2,1)S(1)}, u32[]{:S(2)}, u32[]{:S(2)}) collective-permute-start(bf16[128,768]{1,0:T(8,128)(2,1)S(1)} %get-tuple-element.22), channel_id=1, source_target_pairs={{0,1},{1,0},{2,3},{3,2},{4,5},{5,4},{6,7},{7,6},{12,13},{13,12},{1... | collective-permute-start | bytes 589832 | tf_op jit(solution)/shard_map/ppermute | solution.py:253
  90.3 0.0 collective-permute-done.11.refs_2_
  90.3 1.5 %collective-permute-start.15 = (bf16[128,768]{1,0:T(8,128)(2,1)S(1)}, bf16[128,768]{1,0:T(8,128)(2,1)S(1)}, u32[]{:S(2)}, u32[]{:S(2)}) collective-permute-start(bf16[128,768]{1,0:T(8,128)(2,1)S(1)} %get-tuple-element.27), channel_id=1, source_target_pairs={{0,6},{1,7},{2,4},{3,5},{4,2},{5,3},{6,0},{7,1},{12,10},{13,11},{1... | collective-permute-start | bytes 589832 | tf_op jit(solution)/shard_map/ppermute | solution.py:253
  91.8 0.0 collective-permute-done.12.refs_3_
  91.8 2.1 %collective-permute-start.16 = (bf16[128,768]{1,0:T(8,128)(2,1)S(1)}, bf16[128,768]{1,0:T(8,128)(2,1)S(1)}, u32[]{:S(2)}, u32[]{:S(2)}) collective-permute-start(bf16[128,768]{1,0:T(8,128)(2,1)S(1)} %get-tuple-element.28), channel_id=1, source_target_pairs={{0,7},{1,6},{2,5},{3,4},{4,3},{5,2},{6,1},{7,0},{12,11},{13,10},{1... | collective-permute-start | bytes 589832 | tf_op jit(solution)/shard_map/ppermute | solution.py:253
  93.9 0.0 collective-permute-done.13.refs_4_
  93.9 0.0 collective-permute-done.14.refs_5_
  94.0 0.0 copy-start.7
  94.0 5.4 %collective-permute-done.10.refs_1_ = bf16[128,768]{1,0:T(8,128)(2,1)S(1)} collective-permute-done((bf16[128,768]{1,0:T(8,128)(2,1)S(1)}, bf16[128,768]{1,0:T(8,128)(2,1)S(1)}, u32[]{:S(2)}, u32[]{:S(2)}) %collective-permute-start.10) | collective-permute-done | bytes 196640 | tf_op jit(solution)/shard_map/ppermute | solution.py:253
  99.4 1.7 %collective-permute-done.15.refs_6_ = bf16[128,768]{1,0:T(8,128)(2,1)S(1)} collective-permute-done((bf16[128,768]{1,0:T(8,128)(2,1)S(1)}, bf16[128,768]{1,0:T(8,128)(2,1)S(1)}, u32[]{:S(2)}, u32[]{:S(2)}) %collective-permute-start.15) | collective-permute-done | bytes 196640 | tf_op jit(solution)/shard_map/ppermute | solution.py:253
  101.0 2.6 %collective-permute-done.16.refs_7_ = bf16[128,768]{1,0:T(8,128)(2,1)S(1)} collective-permute-done((bf16[128,768]{1,0:T(8,128)(2,1)S(1)}, bf16[128,768]{1,0:T(8,128)(2,1)S(1)}, u32[]{:S(2)}, u32[]{:S(2)}) %collective-permute-start.16) | collective-permute-done | bytes 196640 | tf_op jit(solution)/shard_map/ppermute | solution.py:253
  103.6 0.0 copy-done.5
  103.6 0.0 copy-done.6
  103.6 0.0 copy-done.7
  103.6 0.0 copy-start.10
  103.6 0.0 copy-start.1
  103.6 0.0 copy-done.4
  103.6 0.0 copy-done.8
  103.6 0.6 copy-done.10
  104.3 2.7 %unpack.1 = bf16[1,128,6144]{2,1,0:T(8,128)(2,1)} custom-call(s32[4]{0:T(128)} %copy-done.3, bf16[128,768]{1,0:T(8,128)(2,1)} %copy-done.2, bf16[128,768]{1,0:T(8,128)(2,1)} %copy-done.8, bf16[128,768]{1,0:T(8,128)(2,1)} %copy-done.4, bf16[128,768]{1,0:T(8,128)(2,1)} %copy-done.5, bf16[128,768]{1,0:T(8,128)(2,1)} %copy-done.6, bf16[128,768]{1,0:T(8,128)(2,1)} %copy-done.7, ...), custom_call_target="tpu_custom_call" | custom-call | tf_op jit(solution)/shard_map/unpack/pallas_call | solution.py:172
  (12 shorter events, 0.0 us)
Async XLA Ops:
  0.0 62.9 %copy-start = (s32[1,8,8,8]{3,2,1,0:T(8,128)S(1)}, s32[1,8,8,8]{3,2,1,0:T(8,128)}, u32[]{:S(2)}) copy-start(s32[1,8,8,8]{3,2,1,0:T(8,128)} %param.7) | copy-start | bytes 6148
  1.9 15.2 %all-to-all-start.1 = ((bf16[8,128,256]{2,1,0:T(8,128)(2,1)}), bf16[8,128,256]{2,1,0:T(8,128)(2,1)}, u32[]{:S(2)}, u32[]{:S(2)}) async-start(bf16[8,128,256]{2,1,0:T(8,128)(2,1)} %pack.1), calls=%async_computation.1 | async-start | bytes 1048576 | tf_op jit(solution)/shard_map/all_to_all | solution.py:263
  17.1 25.7 %all-to-all-start = ((bf16[8,128,768]{2,1,0:T(8,128)(2,1)}), bf16[8,128,768]{2,1,0:T(8,128)(2,1)S(1)}, u32[]{:S(2)}, u32[]{:S(2)}) async-start(bf16[8,128,768]{2,1,0:T(8,128)(2,1)} %bitcast.14), calls=%async_computation | async-start | bytes 3145728 | tf_op jit(solution)/shard_map/all_to_all | solution.py:265
  20.7 14.7 %collective-permute-start = (bf16[8,128,256]{2,1,0:T(8,128)(2,1)}, bf16[8,128,256]{2,1,0:T(8,128)(2,1)}, u32[]{:S(2)}, u32[]{:S(2)}) collective-permute-start(bf16[8,128,256]{2,1,0:T(8,128)(2,1)} %all-to-all-done.1), channel_id=1, source_target_pairs={{0,12},{12,0},{1,13},{13,1},{2,14},{14,2},{3,15},{15,3},{4,8},{8,4... | collective-permute-start | bytes 1572872 | tf_op jit(solution)/shard_map/ppermute | solution.py:249
  22.9 17.8 %collective-permute-start.3 = (bf16[8,128,256]{2,1,0:T(8,128)(2,1)}, bf16[8,128,256]{2,1,0:T(8,128)(2,1)S(1)}, u32[]{:S(2)}, u32[]{:S(2)}) collective-permute-start(bf16[8,128,256]{2,1,0:T(8,128)(2,1)} %all-to-all-done.1), channel_id=1, source_target_pairs={{0,64},{16,80},{32,96},{48,112},{64,0},{80,16},{96,32},{112,48},{1... | collective-permute-start | bytes 1572872 | tf_op jit(solution)/shard_map/ppermute | solution.py:256
  26.8 53.4 %copy-start.3 = (s32[4]{0:T(128)}, s32[4]{0:T(128)S(1)}, u32[]{:S(2)}) copy-start(s32[4]{0:T(128)S(1)} %pad_add_fusion.1.place_ref) | copy-start | bytes 52
  36.5 25.9 %collective-permute-start.1 = (bf16[16,128,256]{2,1,0:T(8,128)(2,1)S(1)}, bf16[16,128,256]{2,1,0:T(8,128)(2,1)}, u32[]{:S(2)}, u32[]{:S(2)}) collective-permute-start(bf16[16,128,256]{2,1,0:T(8,128)(2,1)S(1)} %constant_dynamic-update-slice_fusion.kv_ref.rest_1_), channel_id=1, source_target_pairs={{0,32},{16,48},{32,64},{48,80},{64,96},{80,112},{96,0},{112,16},{1... | collective-permute-start | bytes 3145736 | tf_op jit(solution)/shard_map/ppermute | solution.py:256
  38.5 23.9 %collective-permute-start.2 = (bf16[16,128,256]{2,1,0:T(8,128)(2,1)S(1)}, bf16[16,128,256]{2,1,0:T(8,128)(2,1)}, u32[]{:S(2)}, u32[]{:S(2)}) collective-permute-start(bf16[16,128,256]{2,1,0:T(8,128)(2,1)S(1)} %constant_dynamic-update-slice_fusion.kv_ref.rest_1_), channel_id=1, source_target_pairs={{0,96},{16,112},{32,0},{48,16},{64,32},{80,48},{96,64},{112,80},{1... | collective-permute-start | bytes 3145736 | tf_op jit(solution)/shard_map/ppermute | solution.py:256
  40.7 26.0 %collective-permute-start.5 = (bf16[16,128,256]{2,1,0:T(8,128)(2,1)S(1)}, bf16[16,128,256]{2,1,0:T(8,128)(2,1)}, u32[]{:S(2)}, u32[]{:S(2)}) collective-permute-start(bf16[16,128,256]{2,1,0:T(8,128)(2,1)S(1)} %constant_dynamic-update-slice_fusion.kv_ref.rest_1_), channel_id=1, source_target_pairs={{0,16},{16,0},{32,48},{48,32},{64,80},{80,64},{96,112},{112,96},{1... | collective-permute-start | bytes 3145736 | tf_op jit(solution)/shard_map/ppermute | solution.py:259
  40.7 18.9 %collective-permute-start.4 = (bf16[8,128,256]{2,1,0:T(8,128)(2,1)S(1)}, bf16[8,128,256]{2,1,0:T(8,128)(2,1)}, u32[]{:S(2)}, u32[]{:S(2)}) collective-permute-start(bf16[8,128,256]{2,1,0:T(8,128)(2,1)S(1)} %collective-permute-done.3.rest_5_), channel_id=1, source_target_pairs={{0,12},{12,0},{1,13},{13,1},{2,14},{14,2},{3,15},{15,3},{4,8},{8,4... | collective-permute-start | bytes 1572872 | tf_op jit(solution)/shard_map/ppermute | solution.py:249
  62.4 6.0 %collective-permute-start.6 = (bf16[16,128,256]{2,1,0:T(8,128)(2,1)}, bf16[16,128,256]{2,1,0:T(8,128)(2,1)}, u32[]{:S(2)}, u32[]{:S(2)}) collective-permute-start(bf16[16,128,256]{2,1,0:T(8,128)(2,1)} %collective-permute-done.1.rest_3_), channel_id=1, source_target_pairs={{0,16},{16,0},{32,48},{48,32},{64,80},{80,64},{96,112},{112,96},{1... | collective-permute-start | bytes 3145736 | tf_op jit(solution)/shard_map/ppermute | solution.py:259
  62.4 6.0 %collective-permute-start.9 = (bf16[16,128,256]{2,1,0:T(8,128)(2,1)}, bf16[16,128,256]{2,1,0:T(8,128)(2,1)}, u32[]{:S(2)}, u32[]{:S(2)}) collective-permute-start(bf16[16,128,256]{2,1,0:T(8,128)(2,1)} %collective-permute-done.2.rest_9_), channel_id=1, source_target_pairs={{0,16},{16,0},{32,48},{48,32},{64,80},{80,64},{96,112},{112,96},{1... | collective-permute-start | bytes 3145736 | tf_op jit(solution)/shard_map/ppermute | solution.py:259
  63.0 3.7 %collective-permute-start.7 = (bf16[8,128,256]{2,1,0:T(8,128)(2,1)S(1)}, bf16[8,128,256]{2,1,0:T(8,128)(2,1)}, u32[]{:S(2)}, u32[]{:S(2)}) collective-permute-start(bf16[8,128,256]{2,1,0:T(8,128)(2,1)S(1)} %collective-permute-done.3.rest_5_), channel_id=1, source_target_pairs={{0,16},{16,0},{32,48},{48,32},{64,80},{80,64},{96,112},{112,96},{1... | collective-permute-start | bytes 1572872 | tf_op jit(solution)/shard_map/ppermute | solution.py:259
  63.1 5.4 %collective-permute-start.8 = (bf16[8,128,256]{2,1,0:T(8,128)(2,1)}, bf16[8,128,256]{2,1,0:T(8,128)(2,1)}, u32[]{:S(2)}, u32[]{:S(2)}) collective-permute-start(bf16[8,128,256]{2,1,0:T(8,128)(2,1)} %collective-permute-done.4.rest_6_), channel_id=1, source_target_pairs={{0,16},{16,0},{32,48},{48,32},{64,80},{80,64},{96,112},{112,96},{1... | collective-permute-start | bytes 1572872 | tf_op jit(solution)/shard_map/ppermute | solution.py:259
  75.0 15.3 %collective-permute-start.11 = (bf16[128,768]{1,0:T(8,128)(2,1)S(1)}, bf16[128,768]{1,0:T(8,128)(2,1)S(1)}, u32[]{:S(2)}, u32[]{:S(2)}) collective-permute-start(bf16[128,768]{1,0:T(8,128)(2,1)S(1)} %get-tuple-element.23), channel_id=1, source_target_pairs={{0,2},{1,3},{2,0},{3,1},{4,6},{5,7},{6,4},{7,5},{12,14},{13,15},{1... | collective-permute-start | bytes 589832 | tf_op jit(solution)/shard_map/ppermute | solution.py:253
  78.2 13.6 %collective-permute-start.12 = (bf16[128,768]{1,0:T(8,128)(2,1)S(1)}, bf16[128,768]{1,0:T(8,128)(2,1)S(1)}, u32[]{:S(2)}, u32[]{:S(2)}) collective-permute-start(bf16[128,768]{1,0:T(8,128)(2,1)S(1)} %get-tuple-element.24), channel_id=1, source_target_pairs={{0,3},{1,2},{2,1},{3,0},{4,7},{5,6},{6,5},{7,4},{12,15},{13,14},{1... | collective-permute-start | bytes 589832 | tf_op jit(solution)/shard_map/ppermute | solution.py:253
  79.4 14.5 %collective-permute-start.13 = (bf16[128,768]{1,0:T(8,128)(2,1)S(1)}, bf16[128,768]{1,0:T(8,128)(2,1)S(1)}, u32[]{:S(2)}, u32[]{:S(2)}) collective-permute-start(bf16[128,768]{1,0:T(8,128)(2,1)S(1)} %get-tuple-element.25), channel_id=1, source_target_pairs={{0,4},{1,5},{2,6},{3,7},{4,0},{5,1},{6,2},{7,3},{12,8},{13,9},{14,... | collective-permute-start | bytes 589832 | tf_op jit(solution)/shard_map/ppermute | solution.py:253
  79.6 14.3 %collective-permute-start.14 = (bf16[128,768]{1,0:T(8,128)(2,1)S(1)}, bf16[128,768]{1,0:T(8,128)(2,1)S(1)}, u32[]{:S(2)}, u32[]{:S(2)}) collective-permute-start(bf16[128,768]{1,0:T(8,128)(2,1)S(1)} %get-tuple-element.26), channel_id=1, source_target_pairs={{0,5},{1,4},{2,7},{3,6},{4,1},{5,0},{6,3},{7,2},{12,9},{13,8},{14,... | collective-permute-start | bytes 589832 | tf_op jit(solution)/shard_map/ppermute | solution.py:253
  86.9 0.7 copy-start.2
  87.6 11.7 %collective-permute-start.10 = (bf16[128,768]{1,0:T(8,128)(2,1)S(1)}, bf16[128,768]{1,0:T(8,128)(2,1)S(1)}, u32[]{:S(2)}, u32[]{:S(2)}) collective-permute-start(bf16[128,768]{1,0:T(8,128)(2,1)S(1)} %get-tuple-element.22), channel_id=1, source_target_pairs={{0,1},{1,0},{2,3},{3,2},{4,5},{5,4},{6,7},{7,6},{12,13},{13,12},{1... | collective-permute-start | bytes 589832 | tf_op jit(solution)/shard_map/ppermute | solution.py:253
  90.3 13.3 %copy-start.4 = (bf16[128,768]{1,0:T(8,128)(2,1)}, bf16[128,768]{1,0:T(8,128)(2,1)S(1)}, u32[]{:S(2)}) copy-start(bf16[128,768]{1,0:T(8,128)(2,1)S(1)} %collective-permute-done.11.refs_2_) | copy-start | bytes 589828
  90.3 10.7 %collective-permute-start.15 = (bf16[128,768]{1,0:T(8,128)(2,1)S(1)}, bf16[128,768]{1,0:T(8,128)(2,1)S(1)}, u32[]{:S(2)}, u32[]{:S(2)}) collective-permute-start(bf16[128,768]{1,0:T(8,128)(2,1)S(1)} %get-tuple-element.27), channel_id=1, source_target_pairs={{0,6},{1,7},{2,4},{3,5},{4,2},{5,3},{6,0},{7,1},{12,10},{13,11},{1... | collective-permute-start | bytes 589832 | tf_op jit(solution)/shard_map/ppermute | solution.py:253
  91.8 11.8 %copy-start.5 = (bf16[128,768]{1,0:T(8,128)(2,1)}, bf16[128,768]{1,0:T(8,128)(2,1)S(1)}, u32[]{:S(2)}) copy-start(bf16[128,768]{1,0:T(8,128)(2,1)S(1)} %collective-permute-done.12.refs_3_) | copy-start | bytes 589828
  91.8 11.8 %collective-permute-start.16 = (bf16[128,768]{1,0:T(8,128)(2,1)S(1)}, bf16[128,768]{1,0:T(8,128)(2,1)S(1)}, u32[]{:S(2)}, u32[]{:S(2)}) collective-permute-start(bf16[128,768]{1,0:T(8,128)(2,1)S(1)} %get-tuple-element.28), channel_id=1, source_target_pairs={{0,7},{1,6},{2,5},{3,4},{4,3},{5,2},{6,1},{7,0},{12,11},{13,10},{1... | collective-permute-start | bytes 589832 | tf_op jit(solution)/shard_map/ppermute | solution.py:253
  93.9 9.6 %copy-start.6 = (bf16[128,768]{1,0:T(8,128)(2,1)}, bf16[128,768]{1,0:T(8,128)(2,1)S(1)}, u32[]{:S(2)}) copy-start(bf16[128,768]{1,0:T(8,128)(2,1)S(1)} %collective-permute-done.13.refs_4_) | copy-start | bytes 589828
  94.0 9.6 %copy-start.7 = (bf16[128,768]{1,0:T(8,128)(2,1)}, bf16[128,768]{1,0:T(8,128)(2,1)S(1)}, u32[]{:S(2)}) copy-start(bf16[128,768]{1,0:T(8,128)(2,1)S(1)} %collective-permute-done.14.refs_5_) | copy-start | bytes 589828
  99.4 4.3 %copy-start.8 = (bf16[128,768]{1,0:T(8,128)(2,1)}, bf16[128,768]{1,0:T(8,128)(2,1)S(1)}, u32[]{:S(2)}) copy-start(bf16[128,768]{1,0:T(8,128)(2,1)S(1)} %collective-permute-done.10.refs_1_) | copy-start | bytes 589828
  101.0 2.6 %copy-start.9 = (bf16[128,768]{1,0:T(8,128)(2,1)}, bf16[128,768]{1,0:T(8,128)(2,1)S(1)}, u32[]{:S(2)}) copy-start(bf16[128,768]{1,0:T(8,128)(2,1)S(1)} %collective-permute-done.15.refs_6_) | copy-start | bytes 589828
  103.6 0.7 copy-start.10
  103.6 3.4 %copy-start.1 = (s32[1,8,8,8]{3,2,1,0:T(8,128)S(1)}, s32[1,8,8,8]{3,2,1,0:T(8,128)}, u32[]{:S(2)}) copy-start(s32[1,8,8,8]{3,2,1,0:T(8,128)} %param.7) | copy-start | bytes 6148

commit v5 on v4

--- a/solution.py
+++ b/solution.py
@@ -13,7 +13,7 @@
 LOG2E = 1.4426950408889634
 OWN_VMEM = 16 * 2**20
 OWN_SLOTS = 64
-FAR_VMEM = 16 * 2**20
+FAR_VMEM = 22 * 2**20
 
 
 def scaled_query(query_rows):
@@ -279,7 +279,7 @@
     ids = jnp.where(part == 0, ids, jnp.roll(ids, tiles // 2, axis=0))
     ids = ids.reshape(tiles * slots)
     parts = [None] * kv_heads
-    for steps in ((2, 1), (3, 0)):
+    for steps in ((2, 3, 1), (0,)):
         results = far_attention(ids, where, q, own, pieces, steps, slots)
         for n, step in enumerate(steps):
             parts[2 * step] = results[2 * n]

time: 108 us -> 107 us (level)
  transfers between devices with their start and end apart: 19 -> 19, of which waited for: 8 -> 7; matrix products, arithmetic and copies ran while one was open for 5% -> 5% of each run, Pallas kernels for 22% -> 20%
where the time goes in v5:
time: 107 us; the launch traced here: 106 us
  Pallas kernels  34.8 us (33%)
  starting transfers between devices  33.9 us (32%)
  waiting for transfers between devices  30.6 us (29%)
  local copies, waits for them, and re-layouts  6.9 us (6%)
    pallas_call x1, Pallas kernels, own_attention(): pl.pallas_call(functools.partial(own_kernel, heads, steps), out_shape=jax...  16.8 us
    pallas_call x2, Pallas kernels, far_attention(): pl.pallas_call(functools.partial(far_kernel, heads, steps, slots), out_sh...  13.4 us
    ppermute x7, starting transfers between devices, trade(): return lax.ppermute(x, 'seq', pairs)  11.5 us
    ppermute x7, waiting for transfers between devices, trade(): return lax.ppermute(x, 'seq', pairs)  8.94 us
    ppermute x3, starting transfers between devices, shift(): lax.ppermute(x, 'span', [(i, (i + by) % spans) for i in range(spans)])  8.07 us
    ppermute x2, waiting for transfers between devices, turn(): lax.ppermute(x, 'seq', [pair for a, b in zip(*rings) for pair in ((a, b),...  7.53 us
    all_to_all x1, waiting for transfers between devices, on_device(): lax.all_to_all(sent, 'seq', 0, 0, tiled=True, axis_index_groups=rings)  6.51 us
    all_to_all x1, starting transfers between devices, on_device(): lax.all_to_all(sent, 'seq', 0, 0, tiled=True, axis_index_groups=rings)  5.48 us
  transfers between devices with their start and end apart: 19, of which 7 were waited for; matrix products, arithmetic and copies ran while one was open for 5% of the time, Pallas kernels for 20%

profile of v5, /device:TPU:0, one launch (start us, length us, event | category | flops | bytes accessed | tf_op | source)
XLA Modules:
  0.0 106.5 jit_solution(15436109479533504140)
XLA Ops:
  0.0 0.0 copy-start
  0.0 1.9 %pack.1 = bf16[8,128,256]{2,1,0:T(8,128)(2,1)} custom-call(bf16[1,128,1024]{2,1,0:T(8,128)(2,1)} %k_ref.1, bf16[1,128,1024]{2,1,0:T(8,128)(2,1)} %v_ref.1), custom_call_target="tpu_custom_call" | custom-call | tf_op jit(solution)/shard_map/pack/pallas_call | solution.py:160
  1.9 5.5 %all-to-all-start.1 = ((bf16[8,128,256]{2,1,0:T(8,128)(2,1)}), bf16[8,128,256]{2,1,0:T(8,128)(2,1)}, u32[]{:S(2)}, u32[]{:S(2)}) async-start(bf16[8,128,256]{2,1,0:T(8,128)(2,1)} %pack.1), calls=%async_computation.1 | async-start | bytes 1048576 | tf_op jit(solution)/shard_map/all_to_all | solution.py:263
  7.4 1.7 %copy.6 = bf16[16,8,8,768]{3,2,1,0:T(8,128)(2,1)S(1)} copy(bf16[16,8,8,768]{3,1,2,0:T(8,128)(2,1)} %bitcast.19) | data formatting | bytes 3145728
  9.2 1.4 %copy.8 = bf16[128,8,768]{2,0,1:T(8,128)(2,1)} copy(bf16[128,8,768]{2,1,0:T(8,128)(2,1)S(1)} %bitcast.18) | data formatting | bytes 3145728 | tf_op jit(solution)/shard_map/reshape;squeeze | solution.py:264
  10.6 6.5 %all-to-all-done.1 = bf16[8,128,256]{2,1,0:T(8,128)(2,1)} async-done(((bf16[8,128,256]{2,1,0:T(8,128)(2,1)}), bf16[8,128,256]{2,1,0:T(8,128)(2,1)}, u32[]{:S(2)}, u32[]{:S(2)}) %all-to-all-start.1) | async-done | bytes 524320 | tf_op jit(solution)/shard_map/all_to_all | solution.py:263
  17.1 3.6 %all-to-all-start = ((bf16[8,128,768]{2,1,0:T(8,128)(2,1)}), bf16[8,128,768]{2,1,0:T(8,128)(2,1)S(1)}, u32[]{:S(2)}, u32[]{:S(2)}) async-start(bf16[8,128,768]{2,1,0:T(8,128)(2,1)} %bitcast.14), calls=%async_computation | async-start | bytes 3145728 | tf_op jit(solution)/shard_map/all_to_all | solution.py:265
  20.7 2.2 %collective-permute-start = (bf16[8,128,256]{2,1,0:T(8,128)(2,1)}, bf16[8,128,256]{2,1,0:T(8,128)(2,1)}, u32[]{:S(2)}, u32[]{:S(2)}) collective-permute-start(bf16[8,128,256]{2,1,0:T(8,128)(2,1)} %all-to-all-done.1), channel_id=1, source_target_pairs={{0,12},{12,0},{1,13},{13,1},{2,14},{14,2},{3,15},{15,3},{4,8},{8,4... | collective-permute-start | bytes 1572872 | tf_op jit(solution)/shard_map/ppermute | solution.py:249
  22.9 3.9 %collective-permute-start.3 = (bf16[8,128,256]{2,1,0:T(8,128)(2,1)}, bf16[8,128,256]{2,1,0:T(8,128)(2,1)S(1)}, u32[]{:S(2)}, u32[]{:S(2)}) collective-permute-start(bf16[8,128,256]{2,1,0:T(8,128)(2,1)} %all-to-all-done.1), channel_id=1, source_target_pairs={{0,64},{16,80},{32,96},{48,112},{64,0},{80,16},{96,32},{112,48},{1... | collective-permute-start | bytes 1572872 | tf_op jit(solution)/shard_map/ppermute | solution.py:256
  26.7 0.1 pad_add_fusion.1.place_ref
  26.8 1.1 %constant_dynamic-update-slice_fusion.1 = bf16[16,128,256]{2,1,0:T(8,128)(2,1)S(1)} fusion(bf16[8,128,256]{2,1,0:T(8,128)(2,1)} %all-to-all-done.1), kind=kLoop, calls=%fused_computation.2 | loop fusion | bytes 1048576
  27.9 7.5 %collective-permute-done = bf16[8,128,256]{2,1,0:T(8,128)(2,1)} collective-permute-done((bf16[8,128,256]{2,1,0:T(8,128)(2,1)}, bf16[8,128,256]{2,1,0:T(8,128)(2,1)}, u32[]{:S(2)}, u32[]{:S(2)}) %collective-permute-start) | collective-permute-done | bytes 524320 | tf_op jit(solution)/shard_map/ppermute | solution.py:249
  35.4 1.1 %constant_dynamic-update-slice_fusion.kv_ref.rest_1_ = bf16[16,128,256]{2,1,0:T(8,128)(2,1)S(1)} fusion(bf16[16,128,256]{2,1,0:T(8,128)(2,1)S(1)} %constant_dynamic-update-slice_fusion.1, bf16[8,128,256]{2,1,0:T(8,128)(2,1)} %collective-permute-done), kind=kLoop, calls=%fused_computation.1 | loop fusion | bytes 1048576 | tf_op jit(solution)/shard_map/concatenate | solution.py:270
  36.5 2.0 %collective-permute-start.1 = (bf16[16,128,256]{2,1,0:T(8,128)(2,1)S(1)}, bf16[16,128,256]{2,1,0:T(8,128)(2,1)}, u32[]{:S(2)}, u32[]{:S(2)}) collective-permute-start(bf16[16,128,256]{2,1,0:T(8,128)(2,1)S(1)} %constant_dynamic-update-slice_fusion.kv_ref.rest_1_), channel_id=1, source_target_pairs={{0,32},{16,48},{32,64},{48,80},{64,96},{80,112},{96,0},{112,16},{1... | collective-permute-start | bytes 3145736 | tf_op jit(solution)/shard_map/ppermute | solution.py:256
  38.5 2.2 %collective-permute-start.2 = (bf16[16,128,256]{2,1,0:T(8,128)(2,1)S(1)}, bf16[16,128,256]{2,1,0:T(8,128)(2,1)}, u32[]{:S(2)}, u32[]{:S(2)}) collective-permute-start(bf16[16,128,256]{2,1,0:T(8,128)(2,1)S(1)} %constant_dynamic-update-slice_fusion.kv_ref.rest_1_), channel_id=1, source_target_pairs={{0,96},{16,112},{32,0},{48,16},{64,32},{80,48},{96,64},{112,80},{1... | collective-permute-start | bytes 3145736 | tf_op jit(solution)/shard_map/ppermute | solution.py:256
  40.7 0.0 collective-permute-start.5
  40.7 0.0 collective-permute-done.3.rest_5_
  40.7 2.1 %collective-permute-start.4 = (bf16[8,128,256]{2,1,0:T(8,128)(2,1)S(1)}, bf16[8,128,256]{2,1,0:T(8,128)(2,1)}, u32[]{:S(2)}, u32[]{:S(2)}) collective-permute-start(bf16[8,128,256]{2,1,0:T(8,128)(2,1)S(1)} %collective-permute-done.3.rest_5_), channel_id=1, source_target_pairs={{0,12},{12,0},{1,13},{13,1},{2,14},{14,2},{3,15},{15,3},{4,8},{8,4... | collective-permute-start | bytes 1572872 | tf_op jit(solution)/shard_map/ppermute | solution.py:249
  42.8 0.0 all-to-all-done
  42.8 16.8 %own_attention.1.rest_0_ = f32[64,256,896]{2,1,0:T(8,128)} custom-call(s32[4]{0:T(128)S(1)} %pad_add_fusion.1.place_ref, bf16[1024,768]{1,0:T(8,128)(2,1)S(1)} %bitcast.15, bf16[16,128,256]{2,1,0:T(8,128)(2,1)S(1)} %constant_dynamic-update-slice_fusion.kv_ref.rest_1_), custom_call_target="tpu_custom_call" | custom-call | flops 12884901888 | bytes 6291456 | tf_op jit(solution)/shard_map/own_attention/pallas_call | solution.py:188
  59.6 0.0 collective-permute-done.4.rest_6_
  59.6 2.8 %collective-permute-done.1.rest_3_ = bf16[16,128,256]{2,1,0:T(8,128)(2,1)} collective-permute-done((bf16[16,128,256]{2,1,0:T(8,128)(2,1)S(1)}, bf16[16,128,256]{2,1,0:T(8,128)(2,1)}, u32[]{:S(2)}, u32[]{:S(2)}) %collective-permute-start.1) | collective-permute-done | bytes 1048608 | tf_op jit(solution)/shard_map/ppermute | solution.py:256
  62.4 0.0 collective-permute-done.2.rest_9_
  62.4 0.0 collective-permute-start.6
  62.4 0.5 collective-permute-start.9
  62.9 0.0 copy-done
  63.0 0.1 squeeze.3
  63.0 0.0 collective-permute-start.7
  63.1 0.5 collective-permute-start.8
  63.6 0.1 concatenate.10
  63.7 3.1 %collective-permute-done.7.rest_7_ = bf16[8,128,256]{2,1,0:T(8,128)(2,1)} collective-permute-done((bf16[8,128,256]{2,1,0:T(8,128)(2,1)S(1)}, bf16[8,128,256]{2,1,0:T(8,128)(2,1)}, u32[]{:S(2)}, u32[]{:S(2)}) %collective-permute-start.7) | collective-permute-done | bytes 524320 | tf_op jit(solution)/shard_map/ppermute | solution.py:259
  66.7 0.0 collective-permute-done.5.rest_2_
  66.7 1.7 %collective-permute-done.8.rest_8_ = bf16[8,128,256]{2,1,0:T(8,128)(2,1)} collective-permute-done((bf16[8,128,256]{2,1,0:T(8,128)(2,1)}, bf16[8,128,256]{2,1,0:T(8,128)(2,1)}, u32[]{:S(2)}, u32[]{:S(2)}) %collective-permute-start.8) | collective-permute-done | bytes 524320 | tf_op jit(solution)/shard_map/ppermute | solution.py:259
  68.4 0.0 collective-permute-done.6.rest_4_
  68.4 0.0 collective-permute-done.9.rest_10_
  68.4 9.2 %far_attention.3 = (bf16[128,768]{1,0:T(8,128)(2,1)S(1)}, bf16[128,768]{1,0:T(8,128)(2,1)S(1)}, bf16[128,768]{1,0:T(8,128)(2,1)S(1)}, bf16[128,768]{1,0:T(8,128)...) custom-call(s32[32]{0:T(128)S(1)} %broadcast_select_fusion.ids_ref, s32[4]{0:T(128)S(1)} %pad_add_fusion.1.place_ref, ...), custom_call_target="tpu_custom_call" | custom-call | flops 4831838208 | bytes 6291456 | tf_op jit(solution)/shard_map/far_attention/pallas_call | solution.py:212
  77.6 3.2 %collective-permute-start.11 = (bf16[128,768]{1,0:T(8,128)(2,1)S(1)}, bf16[128,768]{1,0:T(8,128)(2,1)S(1)}, u32[]{:S(2)}, u32[]{:S(2)}) collective-permute-start(bf16[128,768]{1,0:T(8,128)(2,1)S(1)} %get-tuple-element.23), channel_id=1, source_target_pairs={{0,2},{1,3},{2,0},{3,1},{4,6},{5,7},{6,4},{7,5},{12,14},{13,15},{1... | collective-permute-start | bytes 589832 | tf_op jit(solution)/shard_map/ppermute | solution.py:253
  80.9 1.2 %collective-permute-start.12 = (bf16[128,768]{1,0:T(8,128)(2,1)S(1)}, bf16[128,768]{1,0:T(8,128)(2,1)S(1)}, u32[]{:S(2)}, u32[]{:S(2)}) collective-permute-start(bf16[128,768]{1,0:T(8,128)(2,1)S(1)} %get-tuple-element.24), channel_id=1, source_target_pairs={{0,3},{1,2},{2,1},{3,0},{4,7},{5,6},{6,5},{7,4},{12,15},{13,14},{1... | collective-permute-start | bytes 589832 | tf_op jit(solution)/shard_map/ppermute | solution.py:253
  82.0 0.2 collective-permute-start.13
  82.3 0.6 collective-permute-start.14
  82.9 3.8 %collective-permute-start.15 = (bf16[128,768]{1,0:T(8,128)(2,1)S(1)}, bf16[128,768]{1,0:T(8,128)(2,1)S(1)}, u32[]{:S(2)}, u32[]{:S(2)}) collective-permute-start(bf16[128,768]{1,0:T(8,128)(2,1)S(1)} %get-tuple-element.27), channel_id=1, source_target_pairs={{0,6},{1,7},{2,4},{3,5},{4,2},{5,3},{6,0},{7,1},{12,10},{13,11},{1... | collective-permute-start | bytes 589832 | tf_op jit(solution)/shard_map/ppermute | solution.py:253
  86.7 0.0 copy-done.3
  86.7 4.2 %far_attention.2 = (bf16[128,768]{1,0:T(8,128)(2,1)S(1)}, bf16[128,768]{1,0:T(8,128)(2,1)S(1)}) custom-call(s32[32]{0:T(128)S(1)} %broadcast_select_fusion.ids_ref, s32[4]{0:T(128)S(1)} %pad_add_fusion.1.place_ref, bf16[1024,768]{1,0:T(8,128)(2,1)S(1)} %bitcast.17, f32[64,256,896]{2,1,0:T(8,128)} %own_attention.1.rest_0_, ...), custom_call_target="tpu_custom_call" | custom-call | flops 1610612736 | bytes 6291456 | tf_op jit(solution)/shard_map/far_attention/pallas_call | solution.py:212
  90.9 0.0 copy-start.2
  90.9 0.7 copy-done.2
  91.6 0.0 collective-permute-done.11.refs_2_
  91.6 2.4 %collective-permute-start.16 = (bf16[128,768]{1,0:T(8,128)(2,1)S(1)}, bf16[128,768]{1,0:T(8,128)(2,1)S(1)}, u32[]{:S(2)}, u32[]{:S(2)}) collective-permute-start(bf16[128,768]{1,0:T(8,128)(2,1)S(1)} %get-tuple-element.28), channel_id=1, source_target_pairs={{0,7},{1,6},{2,5},{3,4},{4,3},{5,2},{6,1},{7,0},{12,11},{13,10},{1... | collective-permute-start | bytes 589832 | tf_op jit(solution)/shard_map/ppermute | solution.py:253
  94.0 0.0 collective-permute-done.12.refs_3_
  94.0 0.0 collective-permute-start.10
  94.0 0.0 collective-permute-done.13.refs_4_
  94.0 0.0 copy-start.6
  94.0 0.0 collective-permute-done.14.refs_5_
  94.1 0.0 copy-start.7
  94.1 5.1 %collective-permute-done.15.refs_6_ = bf16[128,768]{1,0:T(8,128)(2,1)S(1)} collective-permute-done((bf16[128,768]{1,0:T(8,128)(2,1)S(1)}, bf16[128,768]{1,0:T(8,128)(2,1)S(1)}, u32[]{:S(2)}, u32[]{:S(2)}) %collective-permute-start.15) | collective-permute-done | bytes 196640 | tf_op jit(solution)/shard_map/ppermute | solution.py:253
  99.1 3.9 %collective-permute-done.16.refs_7_ = bf16[128,768]{1,0:T(8,128)(2,1)S(1)} collective-permute-done((bf16[128,768]{1,0:T(8,128)(2,1)S(1)}, bf16[128,768]{1,0:T(8,128)(2,1)S(1)}, u32[]{:S(2)}, u32[]{:S(2)}) %collective-permute-start.16) | collective-permute-done | bytes 196640 | tf_op jit(solution)/shard_map/ppermute | solution.py:253
  103.0 0.0 collective-permute-done.10.refs_1_
  103.0 0.0 copy-done.5
  103.0 0.0 copy-done.6
  103.0 0.0 copy-done.7
  103.0 0.0 copy-done.8
  103.0 0.0 copy-start.1
  103.1 0.6 copy-done.9
  103.7 0.1 copy-done.10
  103.8 2.7 %unpack.1 = bf16[1,128,6144]{2,1,0:T(8,128)(2,1)} custom-call(s32[4]{0:T(128)} %copy-done.3, bf16[128,768]{1,0:T(8,128)(2,1)} %copy-done.2, bf16[128,768]{1,0:T(8,128)(2,1)} %copy-done.10, bf16[128,768]{1,0:T(8,128)(2,1)} %copy-done.4, bf16[128,768]{1,0:T(8,128)(2,1)} %copy-done.5, bf16[128,768]{1,0:T(8,128)(2,1)} %copy-done.6, bf16[128,768]{1,0:T(8,128)(2,1)} %copy-done.7, ...), custom_call_target="tpu_custom_call" | custom-call | tf_op jit(solution)/shard_map/unpack/pallas_call | solution.py:172
  (12 shorter events, 0.0 us)
Async XLA Ops:
  0.0 62.9 %copy-start = (s32[1,8,8,8]{3,2,1,0:T(8,128)S(1)}, s32[1,8,8,8]{3,2,1,0:T(8,128)}, u32[]{:S(2)}) copy-start(s32[1,8,8,8]{3,2,1,0:T(8,128)} %param.7) | copy-start | bytes 6148
  1.9 15.2 %all-to-all-start.1 = ((bf16[8,128,256]{2,1,0:T(8,128)(2,1)}), bf16[8,128,256]{2,1,0:T(8,128)(2,1)}, u32[]{:S(2)}, u32[]{:S(2)}) async-start(bf16[8,128,256]{2,1,0:T(8,128)(2,1)} %pack.1), calls=%async_computation.1 | async-start | bytes 1048576 | tf_op jit(solution)/shard_map/all_to_all | solution.py:263
  17.1 25.7 %all-to-all-start = ((bf16[8,128,768]{2,1,0:T(8,128)(2,1)}), bf16[8,128,768]{2,1,0:T(8,128)(2,1)S(1)}, u32[]{:S(2)}, u32[]{:S(2)}) async-start(bf16[8,128,768]{2,1,0:T(8,128)(2,1)} %bitcast.14), calls=%async_computation | async-start | bytes 3145728 | tf_op jit(solution)/shard_map/all_to_all | solution.py:265
  20.7 14.7 %collective-permute-start = (bf16[8,128,256]{2,1,0:T(8,128)(2,1)}, bf16[8,128,256]{2,1,0:T(8,128)(2,1)}, u32[]{:S(2)}, u32[]{:S(2)}) collective-permute-start(bf16[8,128,256]{2,1,0:T(8,128)(2,1)} %all-to-all-done.1), channel_id=1, source_target_pairs={{0,12},{12,0},{1,13},{13,1},{2,14},{14,2},{3,15},{15,3},{4,8},{8,4... | collective-permute-start | bytes 1572872 | tf_op jit(solution)/shard_map/ppermute | solution.py:249
  22.9 17.8 %collective-permute-start.3 = (bf16[8,128,256]{2,1,0:T(8,128)(2,1)}, bf16[8,128,256]{2,1,0:T(8,128)(2,1)S(1)}, u32[]{:S(2)}, u32[]{:S(2)}) collective-permute-start(bf16[8,128,256]{2,1,0:T(8,128)(2,1)} %all-to-all-done.1), channel_id=1, source_target_pairs={{0,64},{16,80},{32,96},{48,112},{64,0},{80,16},{96,32},{112,48},{1... | collective-permute-start | bytes 1572872 | tf_op jit(solution)/shard_map/ppermute | solution.py:256
  26.8 59.9 %copy-start.3 = (s32[4]{0:T(128)}, s32[4]{0:T(128)S(1)}, u32[]{:S(2)}) copy-start(s32[4]{0:T(128)S(1)} %pad_add_fusion.1.place_ref) | copy-start | bytes 52
  36.5 25.9 %collective-permute-start.1 = (bf16[16,128,256]{2,1,0:T(8,128)(2,1)S(1)}, bf16[16,128,256]{2,1,0:T(8,128)(2,1)}, u32[]{:S(2)}, u32[]{:S(2)}) collective-permute-start(bf16[16,128,256]{2,1,0:T(8,128)(2,1)S(1)} %constant_dynamic-update-slice_fusion.kv_ref.rest_1_), channel_id=1, source_target_pairs={{0,32},{16,48},{32,64},{48,80},{64,96},{80,112},{96,0},{112,16},{1... | collective-permute-start | bytes 3145736 | tf_op jit(solution)/shard_map/ppermute | solution.py:256
  38.5 23.9 %collective-permute-start.2 = (bf16[16,128,256]{2,1,0:T(8,128)(2,1)S(1)}, bf16[16,128,256]{2,1,0:T(8,128)(2,1)}, u32[]{:S(2)}, u32[]{:S(2)}) collective-permute-start(bf16[16,128,256]{2,1,0:T(8,128)(2,1)S(1)} %constant_dynamic-update-slice_fusion.kv_ref.rest_1_), channel_id=1, source_target_pairs={{0,96},{16,112},{32,0},{48,16},{64,32},{80,48},{96,64},{112,80},{1... | collective-permute-start | bytes 3145736 | tf_op jit(solution)/shard_map/ppermute | solution.py:256
  40.7 26.0 %collective-permute-start.5 = (bf16[16,128,256]{2,1,0:T(8,128)(2,1)S(1)}, bf16[16,128,256]{2,1,0:T(8,128)(2,1)}, u32[]{:S(2)}, u32[]{:S(2)}) collective-permute-start(bf16[16,128,256]{2,1,0:T(8,128)(2,1)S(1)} %constant_dynamic-update-slice_fusion.kv_ref.rest_1_), channel_id=1, source_target_pairs={{0,16},{16,0},{32,48},{48,32},{64,80},{80,64},{96,112},{112,96},{1... | collective-permute-start | bytes 3145736 | tf_op jit(solution)/shard_map/ppermute | solution.py:259
  40.7 18.9 %collective-permute-start.4 = (bf16[8,128,256]{2,1,0:T(8,128)(2,1)S(1)}, bf16[8,128,256]{2,1,0:T(8,128)(2,1)}, u32[]{:S(2)}, u32[]{:S(2)}) collective-permute-start(bf16[8,128,256]{2,1,0:T(8,128)(2,1)S(1)} %collective-permute-done.3.rest_5_), channel_id=1, source_target_pairs={{0,12},{12,0},{1,13},{13,1},{2,14},{14,2},{3,15},{15,3},{4,8},{8,4... | collective-permute-start | bytes 1572872 | tf_op jit(solution)/shard_map/ppermute | solution.py:249
  62.4 6.0 %collective-permute-start.6 = (bf16[16,128,256]{2,1,0:T(8,128)(2,1)}, bf16[16,128,256]{2,1,0:T(8,128)(2,1)}, u32[]{:S(2)}, u32[]{:S(2)}) collective-permute-start(bf16[16,128,256]{2,1,0:T(8,128)(2,1)} %collective-permute-done.1.rest_3_), channel_id=1, source_target_pairs={{0,16},{16,0},{32,48},{48,32},{64,80},{80,64},{96,112},{112,96},{1... | collective-permute-start | bytes 3145736 | tf_op jit(solution)/shard_map/ppermute | solution.py:259
  62.4 6.0 %collective-permute-start.9 = (bf16[16,128,256]{2,1,0:T(8,128)(2,1)}, bf16[16,128,256]{2,1,0:T(8,128)(2,1)}, u32[]{:S(2)}, u32[]{:S(2)}) collective-permute-start(bf16[16,128,256]{2,1,0:T(8,128)(2,1)} %collective-permute-done.2.rest_9_), channel_id=1, source_target_pairs={{0,16},{16,0},{32,48},{48,32},{64,80},{80,64},{96,112},{112,96},{1... | collective-permute-start | bytes 3145736 | tf_op jit(solution)/shard_map/ppermute | solution.py:259
  63.0 3.7 %collective-permute-start.7 = (bf16[8,128,256]{2,1,0:T(8,128)(2,1)S(1)}, bf16[8,128,256]{2,1,0:T(8,128)(2,1)}, u32[]{:S(2)}, u32[]{:S(2)}) collective-permute-start(bf16[8,128,256]{2,1,0:T(8,128)(2,1)S(1)} %collective-permute-done.3.rest_5_), channel_id=1, source_target_pairs={{0,16},{16,0},{32,48},{48,32},{64,80},{80,64},{96,112},{112,96},{1... | collective-permute-start | bytes 1572872 | tf_op jit(solution)/shard_map/ppermute | solution.py:259
  63.1 5.4 %collective-permute-start.8 = (bf16[8,128,256]{2,1,0:T(8,128)(2,1)}, bf16[8,128,256]{2,1,0:T(8,128)(2,1)}, u32[]{:S(2)}, u32[]{:S(2)}) collective-permute-start(bf16[8,128,256]{2,1,0:T(8,128)(2,1)} %collective-permute-done.4.rest_6_), channel_id=1, source_target_pairs={{0,16},{16,0},{32,48},{48,32},{64,80},{80,64},{96,112},{112,96},{1... | collective-permute-start | bytes 1572872 | tf_op jit(solution)/shard_map/ppermute | solution.py:259
  77.6 14.0 %collective-permute-start.11 = (bf16[128,768]{1,0:T(8,128)(2,1)S(1)}, bf16[128,768]{1,0:T(8,128)(2,1)S(1)}, u32[]{:S(2)}, u32[]{:S(2)}) collective-permute-start(bf16[128,768]{1,0:T(8,128)(2,1)S(1)} %get-tuple-element.23), channel_id=1, source_target_pairs={{0,2},{1,3},{2,0},{3,1},{4,6},{5,7},{6,4},{7,5},{12,14},{13,15},{1... | collective-permute-start | bytes 589832 | tf_op jit(solution)/shard_map/ppermute | solution.py:253
  80.9 13.1 %collective-permute-start.12 = (bf16[128,768]{1,0:T(8,128)(2,1)S(1)}, bf16[128,768]{1,0:T(8,128)(2,1)S(1)}, u32[]{:S(2)}, u32[]{:S(2)}) collective-permute-start(bf16[128,768]{1,0:T(8,128)(2,1)S(1)} %get-tuple-element.24), channel_id=1, source_target_pairs={{0,3},{1,2},{2,1},{3,0},{4,7},{5,6},{6,5},{7,4},{12,15},{13,14},{1... | collective-permute-start | bytes 589832 | tf_op jit(solution)/shard_map/ppermute | solution.py:253
  82.0 12.0 %collective-permute-start.13 = (bf16[128,768]{1,0:T(8,128)(2,1)S(1)}, bf16[128,768]{1,0:T(8,128)(2,1)S(1)}, u32[]{:S(2)}, u32[]{:S(2)}) collective-permute-start(bf16[128,768]{1,0:T(8,128)(2,1)S(1)} %get-tuple-element.25), channel_id=1, source_target_pairs={{0,4},{1,5},{2,6},{3,7},{4,0},{5,1},{6,2},{7,3},{12,8},{13,9},{14,... | collective-permute-start | bytes 589832 | tf_op jit(solution)/shard_map/ppermute | solution.py:253
  82.3 11.8 %collective-permute-start.14 = (bf16[128,768]{1,0:T(8,128)(2,1)S(1)}, bf16[128,768]{1,0:T(8,128)(2,1)S(1)}, u32[]{:S(2)}, u32[]{:S(2)}) collective-permute-start(bf16[128,768]{1,0:T(8,128)(2,1)S(1)} %get-tuple-element.26), channel_id=1, source_target_pairs={{0,5},{1,4},{2,7},{3,6},{4,1},{5,0},{6,3},{7,2},{12,9},{13,8},{14,... | collective-permute-start | bytes 589832 | tf_op jit(solution)/shard_map/ppermute | solution.py:253
  82.9 16.2 %collective-permute-start.15 = (bf16[128,768]{1,0:T(8,128)(2,1)S(1)}, bf16[128,768]{1,0:T(8,128)(2,1)S(1)}, u32[]{:S(2)}, u32[]{:S(2)}) collective-permute-start(bf16[128,768]{1,0:T(8,128)(2,1)S(1)} %get-tuple-element.27), channel_id=1, source_target_pairs={{0,6},{1,7},{2,4},{3,5},{4,2},{5,3},{6,0},{7,1},{12,10},{13,11},{1... | collective-permute-start | bytes 589832 | tf_op jit(solution)/shard_map/ppermute | solution.py:253
  90.9 0.7 copy-start.2
  91.6 11.4 %copy-start.4 = (bf16[128,768]{1,0:T(8,128)(2,1)}, bf16[128,768]{1,0:T(8,128)(2,1)S(1)}, u32[]{:S(2)}) copy-start(bf16[128,768]{1,0:T(8,128)(2,1)S(1)} %collective-permute-done.11.refs_2_) | copy-start | bytes 589828
  91.6 11.4 %collective-permute-start.16 = (bf16[128,768]{1,0:T(8,128)(2,1)S(1)}, bf16[128,768]{1,0:T(8,128)(2,1)S(1)}, u32[]{:S(2)}, u32[]{:S(2)}) collective-permute-start(bf16[128,768]{1,0:T(8,128)(2,1)S(1)} %get-tuple-element.28), channel_id=1, source_target_pairs={{0,7},{1,6},{2,5},{3,4},{4,3},{5,2},{6,1},{7,0},{12,11},{13,10},{1... | collective-permute-start | bytes 589832 | tf_op jit(solution)/shard_map/ppermute | solution.py:253
  94.0 9.0 %copy-start.5 = (bf16[128,768]{1,0:T(8,128)(2,1)}, bf16[128,768]{1,0:T(8,128)(2,1)S(1)}, u32[]{:S(2)}) copy-start(bf16[128,768]{1,0:T(8,128)(2,1)S(1)} %collective-permute-done.12.refs_3_) | copy-start | bytes 589828
  94.0 9.0 %collective-permute-start.10 = (bf16[128,768]{1,0:T(8,128)(2,1)S(1)}, bf16[128,768]{1,0:T(8,128)(2,1)S(1)}, u32[]{:S(2)}, u32[]{:S(2)}) collective-permute-start(bf16[128,768]{1,0:T(8,128)(2,1)S(1)} %get-tuple-element.22), channel_id=1, source_target_pairs={{0,1},{1,0},{2,3},{3,2},{4,5},{5,4},{6,7},{7,6},{12,13},{13,12},{1... | collective-permute-start | bytes 589832 | tf_op jit(solution)/shard_map/ppermute | solution.py:253
  94.0 9.0 %copy-start.6 = (bf16[128,768]{1,0:T(8,128)(2,1)}, bf16[128,768]{1,0:T(8,128)(2,1)S(1)}, u32[]{:S(2)}) copy-start(bf16[128,768]{1,0:T(8,128)(2,1)S(1)} %collective-permute-done.13.refs_4_) | copy-start | bytes 589828
  94.1 9.0 %copy-start.7 = (bf16[128,768]{1,0:T(8,128)(2,1)}, bf16[128,768]{1,0:T(8,128)(2,1)S(1)}, u32[]{:S(2)}) copy-start(bf16[128,768]{1,0:T(8,128)(2,1)S(1)} %collective-permute-done.14.refs_5_) | copy-start | bytes 589828
  99.1 3.9 %copy-start.8 = (bf16[128,768]{1,0:T(8,128)(2,1)}, bf16[128,768]{1,0:T(8,128)(2,1)S(1)}, u32[]{:S(2)}) copy-start(bf16[128,768]{1,0:T(8,128)(2,1)S(1)} %collective-permute-done.15.refs_6_) | copy-start | bytes 589828
  103.0 0.7 copy-start.9
  103.0 0.7 copy-start.10
  103.0 3.4 %copy-start.1 = (s32[1,8,8,8]{3,2,1,0:T(8,128)S(1)}, s32[1,8,8,8]{3,2,1,0:T(8,128)}, u32[]{:S(2)}) copy-start(s32[1,8,8,8]{3,2,1,0:T(8,128)} %param.7) | copy-start | bytes 6148
